TPU v7x, 32 devices: a whole 2x2x4 slice. The times are simulated.
32 devices in a mesh: rep: 2 (over core), fsdp: 16 (over z, y, x).
Axes of the slice: x: 2, y: 2, z: 4, core: 2. Of those that a mesh axis runs over, the one named last changes fastest.
Arguments:
- tokens: bfloat16 [16384, 768], P(('rep', 'fsdp')), may hold values from -6 to 6
- modality: int32 [16384, 3], P(('rep', 'fsdp')), may hold values from 0 to 1, as said below
- lengths: int32 [64], P(('rep', 'fsdp')), may hold values from 64 to 256, as said below
- ln1_gain: bfloat16 [768], P('fsdp'), may hold values from 0.5 to 1.5
- ln1_bias: bfloat16 [768], P('fsdp'), may hold values from -3 to 3
- w_qkv: bfloat16 [768, 2304], P('fsdp'), may hold values from -0.21875 to 0.21875
- w_out: bfloat16 [768, 768], P('fsdp'), may hold values from -0.875 to 0.875
- out_bias: bfloat16 [768], P('fsdp'), may hold values from -3 to 3
- ln2_gain: bfloat16 [768], P('fsdp'), may hold values from 0.5 to 1.5
- ln2_bias: bfloat16 [768], P('fsdp'), may hold values from -3 to 3
- w_in: bfloat16 [3, 768, 3072], P(None, 'fsdp'), may hold values from -0.21875 to 0.21875
- in_bias: bfloat16 [3, 3072], P(None, 'fsdp'), may hold values from -3 to 3
- w_back: bfloat16 [3, 3072, 768], P(None, 'fsdp'), may hold values from -0.109375 to 0.109375
- back_bias: bfloat16 [3, 768], P(None, 'fsdp'), may hold values from -3 to 3
- cotangent: bfloat16 [16384, 768], P(('rep', 'fsdp')), may hold values from -6 to 6
Outputs:
- output: bfloat16 [16384, 768], P(('rep', 'fsdp'))
- grad_tokens: bfloat16 [16384, 768], P(('rep', 'fsdp'))
- grad_ln1_gain: float32 [768], P('fsdp')
- grad_ln1_bias: float32 [768], P('fsdp')
- grad_w_qkv: float32 [768, 2304], P('fsdp')
- grad_w_out: float32 [768, 768], P('fsdp')
- grad_out_bias: float32 [768], P('fsdp')
- grad_ln2_gain: float32 [768], P('fsdp')
- grad_ln2_bias: float32 [768], P('fsdp')
- grad_w_in: float32 [3, 768, 3072], P(None, 'fsdp')
- grad_in_bias: float32 [3, 3072], P(None, 'fsdp')
- grad_w_back: float32 [3, 3072, 768], P(None, 'fsdp')
- grad_back_bias: float32 [3, 768], P(None, 'fsdp')
Inputs may be any that keep to these rules, and one draw needn't show every extreme that they name: `modality`: each row has exactly one 1; columns are vision, language and joining. `lengths`: the largest is 256 in every draw.
All inputs are finite; a program needn't handle non-finite values.
Results may differ from a plain program's by a relative error of at most 0.02.
Values may be sent and summed in bfloat16 or wider, within the bound.
No kernel may reach another device: no remote copies, remote signals or barrier semaphores. Data moves between devices by JAX's collectives and lax.ppermute only.
A program may use at most 256 MiB of HBM per device.

v0:
```python
import math

import jax
import jax.numpy as jnp
from jax import lax
from jax.sharding import PartitionSpec as P

HEADS = 12
HEAD_DIM = 64
SEQ = 256


inv_root_two = 1.0 / math.sqrt(2.0)
inv_root_tau = 1.0 / math.sqrt(2.0 * math.pi)


def norm_parts(values, norm_gain, norm_bias):
    average = jnp.mean(values, axis=-1, keepdims=True)
    centred = values - average
    spread = jnp.mean(centred * centred, axis=-1, keepdims=True)
    inverse = lax.rsqrt(spread + 1e-05)
    scaled = centred * inverse
    return (scaled * norm_gain + norm_bias, scaled, inverse)


def norm_backward(upstream, scaled, inverse, norm_gain):
    weighted = upstream * norm_gain
    first_mean = jnp.mean(weighted, axis=-1, keepdims=True)
    second_mean = jnp.mean(weighted * scaled, axis=-1, keepdims=True)
    return inverse * (weighted - first_mean - scaled * second_mean)


def attention_scores(query_part, key_part, valid, scale):
    scores = (
        jnp.einsum("sqhd,skhd->shqk", query_part, key_part, preferred_element_type=jnp.float32)
        * scale
    )
    return jnp.where(valid[:, None, None, :], scores, -1e30)


def gelu_slope(pre):
    return (
        0.5 * (1.0 + lax.erf(pre * inv_root_two)) + pre * jnp.exp(-0.5 * pre * pre) * inv_root_tau
    )


def body(
    tokens,
    modality,
    lengths,
    ln1_gain,
    ln1_bias,
    w_qkv,
    w_out,
    out_bias,
    ln2_gain,
    ln2_bias,
    w_in,
    in_bias,
    w_back,
    back_bias,
    cotangent,
):
    row_count, width = tokens.shape
    seq_count = row_count // SEQ
    scale = HEAD_DIM ** (-0.5)
    attn_full = (
        lax.all_gather(w_qkv, "fsdp", axis=0, tiled=True),
        lax.all_gather(w_out, "fsdp", axis=0, tiled=True),
        lax.all_gather(ln1_gain, "fsdp", axis=0, tiled=True),
        lax.all_gather(ln1_bias, "fsdp", axis=0, tiled=True),
        lax.all_gather(out_bias, "fsdp", axis=0, tiled=True),
    )
    ffn_full = (
        lax.all_gather(w_in, "fsdp", axis=1, tiled=True),
        lax.all_gather(w_back, "fsdp", axis=1, tiled=True),
        lax.all_gather(in_bias, "fsdp", axis=1, tiled=True),
        lax.all_gather(back_bias, "fsdp", axis=1, tiled=True),
        lax.all_gather(ln2_gain, "fsdp", axis=0, tiled=True),
        lax.all_gather(ln2_bias, "fsdp", axis=0, tiled=True),
    )
    qkv_full, out_full, gain_one, bias_one, outb_full = attn_full
    in_full, back_full, inb_full, backb_full, gain_two, bias_two = ffn_full
    resid_in = tokens.astype(jnp.float32)
    normed_one, scaled_one, inverse_one = norm_parts(
        resid_in, gain_one.astype(jnp.float32), bias_one.astype(jnp.float32)
    )
    normed_one = normed_one.astype(jnp.bfloat16)
    packed = jnp.dot(normed_one, qkv_full, preferred_element_type=jnp.float32).astype(jnp.bfloat16)
    packed_five = packed.reshape(seq_count, SEQ, 3, HEADS, HEAD_DIM)
    query_part = packed_five[:, :, 0]
    key_part = packed_five[:, :, 1]
    value_part = packed_five[:, :, 2]
    positions = lax.broadcasted_iota(jnp.int32, (seq_count, SEQ), 1)
    valid = positions < lengths[:, None]
    scores = attention_scores(query_part, key_part, valid, scale)
    top_score = jnp.max(scores, axis=-1, keepdims=True)
    totals = jnp.sum(jnp.exp(scores - top_score), axis=-1, keepdims=True)
    log_total = top_score + jnp.log(totals)
    probs_low = jnp.exp(scores - log_total).astype(jnp.bfloat16)
    mixed = jnp.einsum("shqk,skhd->sqhd", probs_low, value_part, preferred_element_type=jnp.float32)
    mixed = mixed.reshape(row_count, width).astype(jnp.bfloat16)
    middle = (
        resid_in
        + jnp.dot(mixed, out_full, preferred_element_type=jnp.float32)
        + outb_full.astype(jnp.float32)
    )
    normed_two, scaled_two, inverse_two = norm_parts(
        middle, gain_two.astype(jnp.float32), bias_two.astype(jnp.float32)
    )
    normed_two = normed_two.astype(jnp.bfloat16)
    mask_cols = jnp.transpose(modality.astype(jnp.float32))[:, :, None]
    inb_float = inb_full.astype(jnp.float32)
    backb_float = backb_full.astype(jnp.float32)
    pre = (
        jnp.einsum("td,edf->etf", normed_two, in_full, preferred_element_type=jnp.float32)
        + inb_float[:, None, :]
    )
    act = jax.nn.gelu(pre, approximate=False).astype(jnp.bfloat16)
    expert_out = (
        jnp.einsum("etf,efd->etd", act, back_full, preferred_element_type=jnp.float32)
        + backb_float[:, None, :]
    )
    final = middle + jnp.sum(mask_cols * expert_out, axis=0)
    output = final.astype(jnp.bfloat16)
    attn_again = (
        lax.all_gather(w_qkv, "fsdp", axis=0, tiled=True),
        lax.all_gather(w_out, "fsdp", axis=0, tiled=True),
        lax.all_gather(ln1_gain, "fsdp", axis=0, tiled=True),
        lax.all_gather(ln1_bias, "fsdp", axis=0, tiled=True),
        lax.all_gather(out_bias, "fsdp", axis=0, tiled=True),
    )
    ffn_again = (
        lax.all_gather(w_in, "fsdp", axis=1, tiled=True),
        lax.all_gather(w_back, "fsdp", axis=1, tiled=True),
        lax.all_gather(in_bias, "fsdp", axis=1, tiled=True),
        lax.all_gather(back_bias, "fsdp", axis=1, tiled=True),
        lax.all_gather(ln2_gain, "fsdp", axis=0, tiled=True),
        lax.all_gather(ln2_bias, "fsdp", axis=0, tiled=True),
    )
    qkv_back, out_back, gain_one_back = (attn_again[0], attn_again[1], attn_again[2])
    in_back, back_back, gain_two_back = (ffn_again[0], ffn_again[1], ffn_again[4])
    cot_float = cotangent.astype(jnp.float32)
    part_grad = (mask_cols * cot_float[None]).astype(jnp.bfloat16)
    grad_back_bias = jnp.sum(part_grad.astype(jnp.float32), axis=1)
    grad_w_back = jnp.einsum("etf,etd->efd", act, part_grad, preferred_element_type=jnp.float32)
    act_grad = jnp.einsum("etd,efd->etf", part_grad, back_back, preferred_element_type=jnp.float32)
    pre_grad = (act_grad * gelu_slope(pre)).astype(jnp.bfloat16)
    grad_in_bias = jnp.sum(pre_grad.astype(jnp.float32), axis=1)
    grad_w_in = jnp.einsum("td,etf->edf", normed_two, pre_grad, preferred_element_type=jnp.float32)
    norm2_grad = jnp.einsum("etf,edf->td", pre_grad, in_back, preferred_element_type=jnp.float32)
    grad_ln2_gain = jnp.sum(norm2_grad * scaled_two, axis=0)
    grad_ln2_bias = jnp.sum(norm2_grad, axis=0)
    mid_grad = cot_float + norm_backward(
        norm2_grad, scaled_two, inverse_two, gain_two_back.astype(jnp.float32)
    )
    ffn_shares = (
        lax.psum_scatter(
            grad_w_in.astype(jnp.bfloat16), "fsdp", scatter_dimension=1, tiled=True
        ).astype(jnp.float32),
        lax.psum_scatter(
            grad_w_back.astype(jnp.bfloat16), "fsdp", scatter_dimension=1, tiled=True
        ).astype(jnp.float32),
        lax.psum_scatter(
            grad_in_bias.astype(jnp.bfloat16), "fsdp", scatter_dimension=1, tiled=True
        ).astype(jnp.float32),
        lax.psum_scatter(
            grad_back_bias.astype(jnp.bfloat16), "fsdp", scatter_dimension=1, tiled=True
        ).astype(jnp.float32),
        lax.psum_scatter(
            grad_ln2_gain.astype(jnp.bfloat16), "fsdp", scatter_dimension=0, tiled=True
        ).astype(jnp.float32),
        lax.psum_scatter(
            grad_ln2_bias.astype(jnp.bfloat16), "fsdp", scatter_dimension=0, tiled=True
        ).astype(jnp.float32),
    )
    branch_grad = mid_grad.astype(jnp.bfloat16)
    grad_out_bias = jnp.sum(branch_grad.astype(jnp.float32), axis=0)
    grad_w_out = jnp.einsum("td,te->de", mixed, branch_grad, preferred_element_type=jnp.float32)
    mixed_grad = jnp.einsum(
        "te,de->td", branch_grad, out_back, preferred_element_type=jnp.float32
    ).astype(jnp.bfloat16)
    mixed_grad = mixed_grad.reshape(seq_count, SEQ, HEADS, HEAD_DIM)
    value_grad = jnp.einsum(
        "shqk,sqhd->skhd", probs_low, mixed_grad, preferred_element_type=jnp.float32
    )
    prob_grad = jnp.einsum(
        "sqhd,skhd->shqk", mixed_grad, value_part, preferred_element_type=jnp.float32
    )
    probs_again = jnp.exp(attention_scores(query_part, key_part, valid, scale) - log_total)
    score_grad = probs_again * (
        prob_grad - jnp.sum(probs_again * prob_grad, axis=-1, keepdims=True)
    )
    score_grad = score_grad.astype(jnp.bfloat16)
    query_grad = (
        jnp.einsum("shqk,skhd->sqhd", score_grad, key_part, preferred_element_type=jnp.float32)
        * scale
    )
    key_grad = (
        jnp.einsum("shqk,sqhd->skhd", score_grad, query_part, preferred_element_type=jnp.float32)
        * scale
    )
    packed_grad = (
        jnp.stack([query_grad, key_grad, value_grad], axis=2)
        .reshape(row_count, 3 * width)
        .astype(jnp.bfloat16)
    )
    grad_w_qkv = jnp.einsum(
        "td,tc->dc", normed_one, packed_grad, preferred_element_type=jnp.float32
    )
    norm1_grad = jnp.einsum("tc,dc->td", packed_grad, qkv_back, preferred_element_type=jnp.float32)
    grad_ln1_gain = jnp.sum(norm1_grad * scaled_one, axis=0)
    grad_ln1_bias = jnp.sum(norm1_grad, axis=0)
    grad_tokens = (
        mid_grad
        + norm_backward(norm1_grad, scaled_one, inverse_one, gain_one_back.astype(jnp.float32))
    ).astype(jnp.bfloat16)
    attn_shares = (
        lax.psum_scatter(grad_w_qkv, "fsdp", scatter_dimension=0, tiled=True),
        lax.psum_scatter(grad_w_out, "fsdp", scatter_dimension=0, tiled=True),
        lax.psum_scatter(grad_ln1_gain, "fsdp", scatter_dimension=0, tiled=True),
        lax.psum_scatter(grad_ln1_bias, "fsdp", scatter_dimension=0, tiled=True),
        lax.psum_scatter(grad_out_bias, "fsdp", scatter_dimension=0, tiled=True),
    )
    summed = (
        lax.psum(attn_shares[2].astype(jnp.bfloat16), "rep").astype(jnp.float32),
        lax.psum(attn_shares[3].astype(jnp.bfloat16), "rep").astype(jnp.float32),
        lax.psum(attn_shares[0].astype(jnp.bfloat16), "rep").astype(jnp.float32),
        lax.psum(attn_shares[1].astype(jnp.bfloat16), "rep").astype(jnp.float32),
        lax.psum(attn_shares[4].astype(jnp.bfloat16), "rep").astype(jnp.float32),
        lax.psum(ffn_shares[4].astype(jnp.bfloat16), "rep").astype(jnp.float32),
        lax.psum(ffn_shares[5].astype(jnp.bfloat16), "rep").astype(jnp.float32),
        lax.psum(ffn_shares[0].astype(jnp.bfloat16), "rep").astype(jnp.float32),
        lax.psum(ffn_shares[2].astype(jnp.bfloat16), "rep").astype(jnp.float32),
        lax.psum(ffn_shares[1].astype(jnp.bfloat16), "rep").astype(jnp.float32),
        lax.psum(ffn_shares[3].astype(jnp.bfloat16), "rep").astype(jnp.float32),
    )
    return (
        output,
        grad_tokens,
        summed[0],
        summed[1],
        summed[2],
        summed[3],
        summed[4],
        summed[5],
        summed[6],
        summed[7],
        summed[8],
        summed[9],
        summed[10],
    )


def solution(mesh):
    placed = (
        P(("rep", "fsdp"), None),
        P(("rep", "fsdp"), None),
        P(("rep", "fsdp")),
        P("fsdp"),
        P("fsdp"),
        P("fsdp", None),
        P("fsdp", None),
        P("fsdp"),
        P("fsdp"),
        P("fsdp"),
        P(None, "fsdp", None),
        P(None, "fsdp"),
        P(None, "fsdp", None),
        P(None, "fsdp"),
        P(("rep", "fsdp"), None),
    )
    return jax.shard_map(
        body,
        mesh=mesh,
        in_specs=placed,
        out_specs=(
            P(("rep", "fsdp"), None),
            P(("rep", "fsdp"), None),
            P("fsdp"),
            P("fsdp"),
            P("fsdp", None),
            P("fsdp", None),
            P("fsdp"),
            P("fsdp"),
            P("fsdp"),
            P(None, "fsdp", None),
            P(None, "fsdp"),
            P(None, "fsdp", None),
            P(None, "fsdp"),
        ),
        check_vma=False,
    )
```

profile of v0, /device:TPU:0, one launch (start us, length us, event | category | flops | bytes accessed | tf_op | source)
XLA Modules:
  0.0 1845.7 jit_solution(4292938209261262663)
XLA Ops:
  16.2 79.2 %all-reduce.13 = (bf16[768]{0:T(1024)(128)(2,1)S(1)}, bf16[768]{0:T(1024)(128)(2,1)S(1)}, bf16[768]{0:T(1024)(128)(2,1)S(1)}, bf16[768]{0:T(1024)(128)(2,1)S(1)}, bf16[768]{0:T(1024)(128)(2,1)S(1)}) all-reduce(bf16[768]{0:T(1024)(128)(2,1)S(1)} %dynamic-update-slice.1, ...), channel_id=1, replica_groups=mesh['rep'=2,'fsdp'=16] {'fsdp'}, use_global_device_ids=true, to_apply=%add.1 | all-reduce | flops 3840 | bytes 15360
  95.5 36.1 %all-gather = bf16[16,192,3]{1,2,0:T(4,128)(2,1)S(1)} all-gather(bf16[1,192,3]{1,2,0:T(4,128)(2,1)} %bitcast.171), channel_id=1, replica_groups=mesh['rep'=2,'fsdp'=16] {'fsdp'}, dimensions={0}, use_global_device_ids=true | all-gather | bytes 19584 | tf_op jit(solution)/shard_map/all_gather | solution.py:77
  131.7 2.4 convert_element_type.181
  134.1 37.7 %all-gather.1 = bf16[16,48,3]{1,2,0:T(4,128)(2,1)S(1)} all-gather(bf16[1,48,3]{1,2,0:T(4,128)(2,1)S(1)} %bitcast.172), channel_id=1, replica_groups=mesh['rep'=2,'fsdp'=16] {'fsdp'}, dimensions={0}, use_global_device_ids=true | all-gather | bytes 4896 | tf_op jit(solution)/shard_map/all_gather | solution.py:78
  173.2 4.2 convolution_convert_fusion.1
  177.4 2.5 copy.77
  179.9 5.1 reshape.110
  184.9 1.7 fusion.72
  187.5 1.5 fusion.23
  190.5 1.5 fusion.50
  193.1 2.5 fusion.74
  197.0 114.7 %all-gather.11.cloned.1.call-done = bf16[3,768,3072]{2,1,0:T(8,128)(2,1)} async-done(((bf16[3,48,3072]{2,1,0:T(8,128)(2,1)}), bf16[3,768,3072]{2,1,0:T(8,128)(2,1)}) %all-gather.11.cloned.1.call-update) | async-done | bytes 14155792 | tf_op jit(solution)/shard_map/all_gather | solution.py:75
  311.7 54.2 %fusion.2 = (bf16[3,512,3072]{2,1,0:T(8,128)(2,1)}, f32[512,3,3072]{2,0,1:T(8,128)}) fusion(f32[3,3072]{1,0:T(4,128)S(1)} %bitcast.167, bf16[3,768,3072]{2,1,0:T(8,128)(2,1)} %all-gather.11.cloned.1.call-done, f32[512,768]{1,0:T(8,128)} %copy-done.11, f32[768]{0:T(1024)S(1)} %convert_element_type.175, f32[768]{0:T(1024)S(1)} %convert_element_type.174, ...), kind=kOutput, calls=%fused_computation.4 | convolution fusion | flops 7561150464 | bytes 44087296 | tf_op jit(solution)/shard_map/td,edf->etf/dot_general | solution.py:116
  365.9 113.5 %all-gather.13.cloned.1.call-done = bf16[3,3072,768]{2,1,0:T(8,128)(2,1)} async-done(((bf16[3,192,768]{2,1,0:T(8,128)(2,1)}), bf16[3,3072,768]{2,1,0:T(8,128)(2,1)}) %all-gather.13.cloned.1.call-update) | async-done | bytes 14155792 | tf_op jit(solution)/shard_map/all_gather | solution.py:76
  479.3 20.0 %fusion.75 = (bf16[3,3072]{1,0:T(4,128)(2,1)S(1)}, bf16[3,512,3072]{2,1,0:T(8,128)(2,1)}) fusion(f32[512,3,3072]{2,0,1:T(8,128)} %get-tuple-element.108, f32[3,3072]{1,0:T(4,128)S(1)} %bitcast.168, bf16[3,3072,768]{2,1,0:T(8,128)(2,1)} %all-gather.13.cloned.1.call-done, f32[512,768]{1,0:T(8,128)S(1)} %copy-done.9, f32[3,512]{1,0:T(4,128)S(1)} %convert_bitcast_fusion.1), kind=kOutput, calls=%fused_computation.130 | convolution fusion | flops 7306730496 | bytes 44101632 | tf_op jit(solution)/shard_map/etd,efd->etf/dot_general | solution.py:147
  499.3 14.6 fusion.46
  514.0 14.4 multiply_reduce_fusion.1
  528.4 1.6 convert_reduce_fusion.1
  531.1 2.2 fusion.59
  533.4 14.7 convert_bitcast_fusion
  548.1 30.9 %copy.93 = bf16[3,768,3072]{2,0,1:T(4,128)(2,1)} copy(bf16[3,768,3072]{1,2,0:T(8,128)(2,1)} %convert_bitcast_fusion) | data formatting | bytes 28311552 | tf_op jit(solution)/shard_map/convert_element_type | solution.py:159
  579.4 3.6 convolution_convert_fusion.3
  583.0 1.4 copy.85
  585.5 5.8 multiply_reduce_fusion
  591.3 1.9 multiply_convert_fusion
  595.0 1.5 fusion.51
  596.9 2.5 copy.91
  601.3 5.3 fusion.69
  608.0 17.1 convolution_convert_fusion
  628.5 31.5 %reduce-scatter.12.cloned.1.call-done = f32[48,768]{1,0:T(8,128)} async-done(((f32[768,768]{1,0:T(8,128)}), f32[48,768]{1,0:T(8,128)}) %reduce-scatter.12.cloned.1.call-update) | async-done | bytes 147472 | tf_op jit(solution)/shard_map/reduce_scatter | solution.py:220
  660.0 1.6 convert_element_type.195
  661.5 508.8 %all-reduce.19.cloned.1.call-done = bf16[3,768,3072]{2,0,1:T(4,128)(2,1)} async-done(((bf16[3,768,3072]{2,0,1:T(4,128)(2,1)}), bf16[3,768,3072]{2,0,1:T(4,128)(2,1)}) %all-reduce.19.cloned.1.call-update) | async-done | bytes 14155792
  1170.3 2.8 constant_dynamic-slice_fusion
  1173.1 153.0 %reduce-scatter.10.cloned.1.call-done = f32[48,2304]{1,0:T(8,128)} async-done(((f32[768,2304]{1,0:T(8,128)}), f32[48,2304]{1,0:T(8,128)}) %reduce-scatter.10.cloned.1.call-update) | async-done | bytes 442384 | tf_op jit(solution)/shard_map/reduce_scatter | solution.py:219
  1326.1 1.7 convert_element_type.193
  1327.8 224.1 %reduce-scatter.14.cloned.1.call-done = bf16[3,192,768]{2,1,0:T(8,128)(2,1)} async-done(((bf16[3,3072,768]{2,1,0:T(8,128)(2,1)}), bf16[3,192,768]{2,1,0:T(8,128)(2,1)}) %reduce-scatter.14.cloned.1.call-update) | async-done | bytes 884752 | tf_op jit(solution)/shard_map/reduce_scatter | solution.py:161
  1551.9 127.1 %reduce-scatter.18.cloned.1.call-done = bf16[48,3]{1,0:T(8,128)(2,1)} async-done(((bf16[768,3]{1,0:T(8,128)(2,1)}), bf16[48,3]{1,0:T(8,128)(2,1)}) %reduce-scatter.18.cloned.1.call-update) | async-done | bytes 304
  1679.8 6.4 fusion.43
  1686.2 75.1 %all-reduce.11 = (bf16[768]{0:T(1024)(128)(2,1)S(1)}, bf16[768]{0:T(1024)(128)(2,1)S(1)}, bf16[768]{0:T(1024)(128)(2,1)S(1)}) all-reduce(f32[768]{0:T(1024)S(1)} %get-tuple-element.67, f32[768]{0:T(1024)S(1)} %get-tuple-element.72, f32[768]{0:T(1024)S(1)} %get-tuple-element.94), channel_id=2, replica_groups=mesh['rep'=2,'fsdp'=16] {'fsdp'}, use_global_device_ids=true, to_apply=%region_13.14.clone | all-reduce | flops 2304 | bytes 13824
  1761.4 36.6 %all-reduce.12 = (bf16[768]{0:T(1024)(128)(2,1)S(1)}, bf16[768]{0:T(1024)(128)(2,1)S(1)}) all-reduce(bf16[768]{0:T(1024)(128)(2,1)S(1)} %get-tuple-element.65, bf16[768]{0:T(1024)(128)(2,1)S(1)} %get-tuple-element.71), channel_id=7, replica_groups=mesh['rep'=2,'fsdp'=16] {'fsdp'}, use_global_device_ids=true, to_apply=%region_26.27.clone | all-reduce | flops 1536 | bytes 6144
  1798.2 2.9 fusion.42
  1801.1 4.8 reduce-scatter.16.cloned.1.call-done
  1806.8 2.5 all-reduce.14
  1813.0 17.1 all-reduce.21.cloned.1.call-done
  1830.1 1.7 convert_element_type.194
  1831.8 1.6 convert_element_type.196
  1833.4 2.9 copy.95
  1836.2 2.5 convert_element_type.209
  (157 shorter events, 30.9 us)
Async XLA Ops:
  7.2 126.9 %copy-start.33 = (bf16[3,48]{1,0:T(4,128)(2,1)S(1)}, bf16[3,48]{1,0:T(4,128)(2,1)}, u32[]{:S(2)}) copy-start(bf16[3,48]{1,0:T(4,128)(2,1)} %param.28) | copy-start | bytes 868
  7.2 165.3 %copy-start.7 = (bf16[512,768]{1,0:T(8,128)(2,1)S(1)}, bf16[512,768]{1,0:T(8,128)(2,1)}, u32[]{:S(2)}) copy-start(bf16[512,768]{1,0:T(8,128)(2,1)} %param.15) | copy-start | bytes 2359300
  7.2 165.8 %copy-start.34 = (s32[2]{0:T(128)S(1)}, s32[2]{0:T(128)}, u32[]{:S(2)}) copy-start(s32[2]{0:T(128)} %param.17) | copy-start | bytes 28
  7.2 165.9 %copy-start.30 = (s32[512,3]{0,1:T(4,128)S(1)}, s32[512,3]{0,1:T(4,128)}, u32[]{:S(2)}) copy-start(s32[512,3]{0,1:T(4,128)} %param.16) | copy-start | bytes 18436
  7.2 165.9 %all-gather.7.cloned.1.call-start = ((), (), s32[]{:S(2)}) async-start(), calls=%async_computation.5 | async-start | bytes 3760128 | tf_op jit(solution)/shard_map/all_gather | solution.py:68
  8.0 185.1 %all-gather.9.cloned.1.call-start = ((), (), s32[]{:S(2)}) async-start(), calls=%async_computation.6 | async-start | bytes 1253376 | tf_op jit(solution)/shard_map/all_gather | solution.py:69
  8.7 303.0 %all-gather.11.cloned.1.call-start = ((), (), s32[]{:S(2)}) async-start(), calls=%async_computation.7 | async-start | bytes 15040512 | tf_op jit(solution)/shard_map/all_gather | solution.py:75
  9.4 469.9 %all-gather.13.cloned.1.call-start = ((), (), s32[]{:S(2)}) async-start(), calls=%async_computation.8 | async-start | bytes 15040512 | tf_op jit(solution)/shard_map/all_gather | solution.py:76
  10.0 649.9 %reduce-scatter.12.cloned.1.call-start = ((), (), s32[]{:S(2)}) async-start(), calls=%async_computation.10 | async-start | bytes 2506752 | tf_op jit(solution)/shard_map/reduce_scatter | solution.py:220
  95.5 81.8 %copy-start.31 = (f32[768]{0:T(1024)}, f32[768]{0:T(1024)S(1)}, u32[]{:S(2)}) copy-start(f32[768]{0:T(1024)S(1)} %convert_element_type.165) | copy-start | bytes 9220
  95.5 81.8 %copy-start.25 = (f32[768]{0:T(1024)}, f32[768]{0:T(1024)S(1)}, u32[]{:S(2)}) copy-start(f32[768]{0:T(1024)S(1)} %convert_element_type.164) | copy-start | bytes 9220
  172.7 4.7 copy-start.23
  173.1 17.4 copy-start.21
  173.1 4.2 copy-start.28
  186.6 0.9 copy-start.3
  186.6 2.4 copy-start.5
  186.6 3.9 copy-start.15
  189.0 3.0 copy-start
  190.5 2.4 copy-start.19
  193.0 118.6 %copy-start.13 = (bf16[96,8,2,256]{3,1,2,0:T(8,128)(2,1)}, bf16[96,8,2,256]{3,1,2,0:T(8,128)(2,1)S(1)}, u32[]{:S(2)}) copy-start(bf16[96,8,2,256]{3,1,2,0:T(8,128)(2,1)S(1)} %copy.109) | copy-start | bytes 2359300
  195.5 1.1 copy-start.11
  311.7 167.6 %copy-start.9 = (f32[512,768]{1,0:T(8,128)S(1)}, f32[512,768]{1,0:T(8,128)}, u32[]{:S(2)}) copy-start(f32[512,768]{1,0:T(8,128)} %convert_element_type.181) | copy-start | bytes 4718596
  479.3 20.0 %copy-start.12 = (f32[512,768]{1,0:T(8,128)S(1)}, f32[512,768]{1,0:T(8,128)}, u32[]{:S(2)}) copy-start(f32[512,768]{1,0:T(8,128)} %copy-done.11) | copy-start | bytes 4718596
  499.3 14.6 copy-start.27
  513.9 14.4 copy-start.17
  528.4 2.8 copy-start.14
  530.0 1.1 copy-start.1
  533.3 636.9 %all-reduce.19.cloned.1.call-start = ((), (), s32[]{:S(2)}) async-start(), calls=%async_computation.14 | async-start | bytes 37748736
  579.1 6.4 copy-start.20
  579.1 6.4 copy-start.22
  579.1 747.0 %reduce-scatter.10.cloned.1.call-start = ((), (), s32[]{:S(2)}) async-start(), calls=%async_computation.9 | async-start | bytes 7520256 | tf_op jit(solution)/shard_map/reduce_scatter | solution.py:219
  579.4 11.9 slice-start
  585.5 5.8 slice-start.1
  591.3 1.9 copy-start.6
  593.3 1.1 copy-start.4
  593.3 1.8 copy-start.16
  596.9 4.4 copy-start.8
  596.9 4.4 copy-start.24
  596.9 4.4 copy-start.26
  596.9 4.4 copy-start.29
  596.9 4.4 copy-start.32
  599.9 1.4 copy-start.18
  606.6 1.4 copy-start.10
  606.6 945.2 %reduce-scatter.14.cloned.1.call-start = ((), (), s32[]{:S(2)}) async-start(), calls=%async_computation.11 | async-start | bytes 15040512 | tf_op jit(solution)/shard_map/reduce_scatter | solution.py:161
  625.2 1053.8 %reduce-scatter.18.cloned.1.call-start = ((), (), s32[]{:S(2)}) async-start(), calls=%async_computation.13 | async-start | bytes 208896
  626.5 1179.4 %reduce-scatter.16.cloned.1.call-start = ((), (), s32[]{:S(2)}) async-start(), calls=%async_computation.12 | async-start | bytes 835584
  628.4 1201.6 %all-reduce.21.cloned.1.call-start = ((), (), s32[]{:S(2)}) async-start(), calls=%async_computation.15 | async-start | bytes 4718592 | tf_op jit(solution)/shard_map/psum | solution.py:233
  1679.8 118.4 %copy-start.2 = (f32[512,768]{1,0:T(8,128)S(1)}, f32[512,768]{1,0:T(8,128)}, u32[]{:S(2)}) copy-start(f32[512,768]{1,0:T(8,128)} %copy-done.1) | copy-start | bytes 4718596
Sparse Core Ops, SparseCore 0:
  10.9 74.6 all-gather.6
  88.3 54.7 all-gather.8
  145.8 165.7 all-gather.10
  314.2 165.0 all-gather.12
  533.4 126.4 reduce-scatter.11
  667.4 502.8 all-reduce.18
  1175.6 150.4 reduce-scatter.9
  1331.9 219.9 reduce-scatter.13
  1557.8 121.1 reduce-scatter.17
  1684.2 121.6 reduce-scatter.15
  1809.2 20.8 all-reduce.20
where the time goes:
time: 1860 us; the launch traced here: 1850 us
  waiting for transfers between devices  1300 us (70%)
  blocking collectives  267 us (14%)
  matrix products  171 us (9%)
  local copies, waits for them, and re-layouts  68.7 us (4%)
  other arithmetic  24.6 us (1%)
    unnamed x14, waiting for transfers between devices  643 us
    reduce_scatter x1, waiting for transfers between devices, body(): lax.psum_scatter(grad_w_back.astype(jnp.bfloat16), 'fsdp', scatter_dimens...  224 us
    unnamed x3, blocking collectives  191 us
    reduce_scatter x1, waiting for transfers between devices, body(): lax.psum_scatter(grad_w_qkv, 'fsdp', scatter_dimension=0, tiled=True)  153 us
    all_gather x1, waiting for transfers between devices, body(): lax.all_gather(w_in, 'fsdp', axis=1, tiled=True)  115 us
    all_gather x1, waiting for transfers between devices, body(): lax.all_gather(w_back, 'fsdp', axis=1, tiled=True)  113 us
    dot_general x1, matrix products, body(): jnp.einsum('td,edf->etf', normed_two, in_full, preferred_element_type=jnp...  54.2 us
    all_gather x1, blocking collectives, body(): lax.all_gather(back_bias, 'fsdp', axis=1, tiled=True)  37.7 us
  transfers between devices with their start and end apart: 11, of which 9 were waited for; matrix products, arithmetic and copies ran while one was open for 11% of the time, Pallas kernels for 0%

commit v1 on v0

v1 whole, which is shorter than its diff:
```python
import functools
import math

import jax
import jax.numpy as jnp
from jax import lax
from jax.experimental import pallas as pl
from jax.experimental.pallas import tpu as pltpu
from jax.sharding import Mesh
from jax.sharding import PartitionSpec as P

HEADS = 12
HEAD_DIM = 64
SEQ = 256
D = 768
EXPERTS = 3
UNIT = 16
TILE = 256
UNITS = TILE // UNIT

INV_ROOT_TWO = 1.0 / math.sqrt(2.0)
INV_ROOT_TAU = 1.0 / math.sqrt(2.0 * math.pi)
F32 = jnp.float32
BF16 = jnp.bfloat16

VMEM = pl.BlockSpec(memory_space=pltpu.VMEM)
SMEM = pl.BlockSpec(memory_space=pltpu.SMEM)
ANY = pl.BlockSpec(memory_space=pl.ANY)


def dot(a, b):
    return lax.dot_general(a, b, (((1,), (0,)), ((), ())), preferred_element_type=F32)


def dot_nt(a, b):
    return lax.dot_general(a, b, (((1,), (1,)), ((), ())), preferred_element_type=F32)


def dot_tn(a, b):
    return lax.dot_general(a, b, (((0,), (0,)), ((), ())), preferred_element_type=F32)


def norm_stats(values):
    average = jnp.mean(values, axis=-1, keepdims=True)
    centred = values - average
    inverse = lax.rsqrt(jnp.mean(centred * centred, axis=-1, keepdims=True) + 1e-05)
    return centred * inverse, inverse


def norm_backward(weighted, scaled, inverse):
    first = jnp.mean(weighted, axis=-1, keepdims=True)
    second = jnp.mean(weighted * scaled, axis=-1, keepdims=True)
    return inverse * (weighted - first - scaled * second)


def two_heads(block):
    low = lax.broadcasted_iota(jnp.int32, block.shape, 1) < HEAD_DIM
    nothing = jnp.zeros_like(block)
    return jnp.concatenate([jnp.where(low, block, nothing), jnp.where(low, nothing, block)], axis=0)


def merge_heads(block):
    low = lax.broadcasted_iota(jnp.int32, (SEQ, 2 * HEAD_DIM), 1) < HEAD_DIM
    return jnp.where(low, block[:SEQ], block[SEQ:])


PAIRS = HEADS // 2


def attn_fwd_kernel(share, where_ref, len_ref, tok_ref, vec_ref, perm_ref, *rest):
    pieces = rest[:8]
    mid_ref, xs_ref, q_ref, k_ref, v_ref, mixed_ref, probs_ref, w_ref = rest[8:16]
    sems = rest[16]
    core, y, x = where_ref[0], where_ref[1], where_ref[2]
    depth = pieces[0].shape[0]
    copies = []
    for matrix in range(2):
        for n, piece in enumerate(pieces):
            far, y_of, x_of = n // 4, (n // 2) % 2, n % 2
            slot = 2 * jnp.where(far == 1, 1 - core, core) + matrix
            place = 2 * jnp.where(y_of == 1, 1 - y, y) + jnp.where(x_of == 1, 1 - x, x)
            for z in range(depth):
                row = pl.multiple_of((4 * z + place) * share, share)
                first = matrix * (share + 8)
                copies.append(pltpu.make_async_copy(
                    piece.at[z, pl.ds(first, share)], w_ref.at[slot, pl.ds(row, share)],
                    sems.at[matrix, n, z]))
    for copy in copies:
        copy.start()
    values = tok_ref[...].astype(F32)
    scaled, _ = norm_stats(values)
    normed = (scaled * vec_ref[0:1, :] + vec_ref[1:2, :]).astype(BF16)
    for copy in copies:
        copy.wait()
    q_ref[...] = dot(normed, w_ref[0]).astype(BF16)
    k_ref[...] = dot(normed, w_ref[1]).astype(BF16)
    v_ref[...] = dot(normed, w_ref[2]).astype(BF16)
    seqs = tok_ref.shape[0] // SEQ
    for seq in range(seqs):
        length = len_ref[seq]
        rows = slice(seq * SEQ, (seq + 1) * SEQ)

        def step(pair, carry):
            cols = pl.ds(pl.multiple_of(pair * 128, 128), 128)
            both = two_heads(q_ref[rows, cols])
            scores = dot_nt(both, k_ref[rows, cols]) * (HEAD_DIM ** -0.5)
            valid = lax.broadcasted_iota(jnp.int32, scores.shape, 1) < length
            scores = jnp.where(valid, scores, -1e30)
            top = jnp.max(scores, axis=-1, keepdims=True)
            grown = jnp.exp(scores - top)
            total = jnp.sum(grown, axis=-1, keepdims=True)
            probs = (grown * (1.0 / total)).astype(BF16)
            probs_ref[seq * PAIRS + pair] = probs
            mixed_ref[rows, cols] = merge_heads(dot(probs, v_ref[rows, cols])).astype(BF16)
            return carry

        lax.fori_loop(0, PAIRS, step, 0)
    middle = values + dot(mixed_ref[...], w_ref[3]) + vec_ref[2:3, :]
    mid_ref[...] = middle
    scaled_two, _ = norm_stats(middle)
    normed_two = (scaled_two * vec_ref[3:4, :] + vec_ref[4:5, :]).astype(BF16)
    xs_ref[...] = dot(perm_ref[...], normed_two).astype(BF16)


def attn_fwd(where, lengths, tokens, vec, perm, pieces, share):
    rows = tokens.shape[0]
    seqs = rows // SEQ
    low = jax.ShapeDtypeStruct((rows, D), BF16)
    return pl.pallas_call(
        functools.partial(attn_fwd_kernel, share),
        out_shape=(
            jax.ShapeDtypeStruct((rows, D), F32),
            jax.ShapeDtypeStruct((perm.shape[0], D), BF16),
            low, low, low, low,
            jax.ShapeDtypeStruct((seqs * PAIRS, 2 * SEQ, SEQ), BF16),
            jax.ShapeDtypeStruct((4, D, D), BF16),
        ),
        in_specs=[SMEM] * 2 + [VMEM] * 3 + [ANY] * 8,
        out_specs=(VMEM,) * 8,
        scratch_shapes=[pltpu.SemaphoreType.DMA((2, 8, pieces[0].shape[0]))],
        compiler_params=pltpu.CompilerParams(vmem_limit_bytes=48 * 1024 * 1024),
        cost_estimate=pl.CostEstimate(flops=2 * rows * D * D * 5, bytes_accessed=14 * 1024 * 1024, transcendentals=0),
        name="attn_fwd",
    )(where, lengths, tokens, vec, perm, *pieces)


def ffn_kernel(first, tab_ref, tot_ref, where_ref, *rest):
    xs, cs, ws, b_ref = rest[0:4], rest[4:8], rest[8:10], rest[10]
    rest = rest[11:] if first else rest[15:]
    outs, (mine_ref, other_ref, gb_ref) = rest[:4], rest[4:7]
    xv, cv, wi, wb, gwi, gwb, xt, ct, ot, dt, in_sems, w_sems, out_sems = rest[7:]
    y = where_ref[1]
    depth, height = ws[0].shape[0], ws[0].shape[1] // 2
    size = xs[0].shape[0]
    weights, tokens = [], []
    for n, piece in enumerate(ws):
        y_of = y if n == 0 else 1 - y
        for z in range(depth):
            row = pl.multiple_of((2 * z + y_of) * height, height)
            for part, target in enumerate((wi, wb)):
                weights.append(pltpu.make_async_copy(
                    piece.at[z, pl.ds(part * height, height)], target.at[pl.ds(row, height)],
                    w_sems.at[n, z, part]))
    for n in range(4):
        tokens.append(pltpu.make_async_copy(xs[n], xv.at[pl.ds(n * size, size)], in_sems.at[0, n]))
        tokens.append(pltpu.make_async_copy(cs[n], cv.at[pl.ds(n * size, size)], in_sems.at[1, n]))
    for copy in tokens + weights:
        copy.start()
    gwi[...] = jnp.zeros_like(gwi)
    gwb[...] = jnp.zeros_like(gwb)
    gb_ref[...] = jnp.zeros_like(gb_ref)
    for copy in tokens + weights:
        copy.wait()
    total = tot_ref[0]
    border = 2 * size // UNIT

    def move(t, u, act):
        unit = t * UNITS + u
        held = slice(u * UNIT, (u + 1) * UNIT)
        for n, source in enumerate((ot, dt)):
            @pl.when(unit < total)
            def _():
                dst = tab_ref[unit]

                @pl.when(dst < border)
                def _():
                    act(pltpu.make_async_copy(
                        source.at[held], outs[2 * n].at[pl.ds(pl.multiple_of(dst * UNIT, UNIT), UNIT)],
                        out_sems.at[n, u]))

                @pl.when(dst >= border)
                def _():
                    act(pltpu.make_async_copy(
                        source.at[held], outs[2 * n + 1].at[pl.ds(pl.multiple_of((dst - border) * UNIT, UNIT), UNIT)],
                        out_sems.at[n, u]))

    def tile(t, carry):
        for u in range(UNITS):
            src = pl.multiple_of(tab_ref[t * UNITS + u] * UNIT, UNIT)
            xt[u * UNIT:(u + 1) * UNIT, :] = xv[pl.ds(src, UNIT), :]
            ct[u * UNIT:(u + 1) * UNIT, :] = cv[pl.ds(src, UNIT), :]
        left = (total - t * UNITS) * UNIT
        row = lax.broadcasted_iota(jnp.int32, (TILE, D), 0)
        part = jnp.where(row < left, ct[...], jnp.zeros_like(ct))
        pre = dot(xt[...], wi[...]) + b_ref[...]
        share = 0.5 * (1.0 + lax.erf(pre * INV_ROOT_TWO))
        act = (pre * share).astype(BF16)
        slope = share + pre * jnp.exp(-0.5 * pre * pre) * INV_ROOT_TAU

        @pl.when(t > 0)
        def _():
            for u in range(UNITS):
                move(t - 1, u, lambda copy: copy.wait())

        ot[...] = dot(act, wb[...]).astype(BF16)
        pre_grad = (dot_nt(part, wb[...]) * slope).astype(BF16)
        dt[...] = dot_nt(pre_grad, wi[...]).astype(BF16)
        for u in range(UNITS):
            move(t, u, lambda copy: copy.start())
        gwb[...] += dot_tn(act, part)
        gwi[...] += dot_tn(xt[...], pre_grad)
        gb_ref[...] += jnp.sum(pre_grad.astype(F32), axis=0, keepdims=True)
        return carry

    tiles = (total + UNITS - 1) // UNITS
    lax.fori_loop(0, tiles, tile, 0)

    @pl.when(tiles > 0)
    def _():
        for u in range(UNITS):
            move(tiles - 1, u, lambda copy: copy.wait())

    for z in range(depth):
        for y_of in range(2):
            rows = slice((2 * z + y_of) * height, (2 * z + y_of + 1) * height)
            for flag, target in ((y == y_of, mine_ref), (y != y_of, other_ref)):
                @pl.when(flag)
                def _():
                    target[z, :height, :] = gwi[rows, :].astype(BF16)
                    target[z, height:, :] = gwb[rows, :].astype(BF16)


def ffn(table, total, where, xs, cs, weights, bias, before):
    size = xs[0].shape[0]
    first = before is None
    quarter = bias.shape[1]
    tokens = jax.ShapeDtypeStruct((2 * size, D), BF16)
    grads = jax.ShapeDtypeStruct(weights[0].shape, BF16)
    args = [table, total, where, *xs, *cs, *weights, bias] + ([] if first else list(before))
    return pl.pallas_call(
        functools.partial(ffn_kernel, first),
        out_shape=(tokens,) * 4 + (grads, grads, jax.ShapeDtypeStruct((1, quarter), F32)),
        in_specs=[SMEM] * 3 + [ANY] * 10 + [VMEM] + [ANY] * (0 if first else 4),
        out_specs=(ANY,) * 4 + (VMEM,) * 3,
        scratch_shapes=[
            pltpu.VMEM((4 * size, D), BF16),
            pltpu.VMEM((4 * size, D), BF16),
            pltpu.VMEM((D, quarter), BF16),
            pltpu.VMEM((quarter, D), BF16),
            pltpu.VMEM((D, quarter), F32),
            pltpu.VMEM((quarter, D), F32),
            pltpu.VMEM((TILE, D), BF16),
            pltpu.VMEM((TILE, D), BF16),
            pltpu.VMEM((TILE, D), BF16),
            pltpu.VMEM((TILE, D), BF16),
            pltpu.SemaphoreType.DMA((2, 4)),
            pltpu.SemaphoreType.DMA((2, weights[0].shape[0], 2)),
            pltpu.SemaphoreType.DMA((2, UNITS)),
        ],
        input_output_aliases={} if first else {14 + i: i for i in range(4)},
        compiler_params=pltpu.CompilerParams(vmem_limit_bytes=48 * 1024 * 1024),
        cost_estimate=pl.CostEstimate(flops=12 * 1024 * D * quarter, bytes_accessed=20 * 1024 * 1024, transcendentals=0),
        name="ffn",
    )(*args)


def attn_bwd_kernel(core_ref, tok_ref, cot_ref, mid_ref, dxs_ref, unperm_ref, q_ref, k_ref, v_ref, mixed_ref,
                    probs_ref, vec_ref, hot_ref, w_ref,
                    gtok_ref, keep_ref, send_ref, gvec_ref,
                    mg, mxg, dq, dk, dv):
    norm2_grad = dot(unperm_ref[...], dxs_ref[...])
    scaled_two, inverse_two = norm_stats(mid_ref[...])
    gvec_ref[3:4, :] = jnp.sum(norm2_grad * scaled_two, axis=0, keepdims=True)
    gvec_ref[4:5, :] = jnp.sum(norm2_grad, axis=0, keepdims=True)
    mid_grad = cot_ref[...].astype(F32) + norm_backward(norm2_grad * vec_ref[3:4, :], scaled_two, inverse_two)
    mg[...] = mid_grad
    branch = mid_grad.astype(BF16)
    gvec_ref[2:3, :] = jnp.sum(branch.astype(F32), axis=0, keepdims=True)
    gvec_ref[5:8, :] = dot(hot_ref[...], cot_ref[...])[:3]
    core = core_ref[0]

    def put(matrix, value):
        low = value.astype(BF16)

        @pl.when(core == matrix // 2)
        def _():
            keep_ref[matrix % 2] = low

        @pl.when(core != matrix // 2)
        def _():
            send_ref[matrix % 2] = low

    put(3, dot_tn(mixed_ref[...], branch))
    mxg[...] = dot_nt(branch, w_ref[3]).astype(BF16)
    seqs = tok_ref.shape[0] // SEQ
    scale = HEAD_DIM ** -0.5
    for seq in range(seqs):
        rows = slice(seq * SEQ, (seq + 1) * SEQ)

        def step(pair, carry):
            cols = pl.ds(pl.multiple_of(pair * 128, 128), 128)
            probs = probs_ref[seq * PAIRS + pair]
            grads = two_heads(mxg[rows, cols])
            dv[rows, cols] = dot_tn(probs, grads).astype(BF16)
            prob_grad = dot_nt(grads, v_ref[rows, cols])
            wide = probs.astype(F32)
            inner = jnp.sum(wide * prob_grad, axis=-1, keepdims=True)
            score_grad = (wide * (prob_grad - inner)).astype(BF16)
            dq[rows, cols] = (merge_heads(dot(score_grad, k_ref[rows, cols])) * scale).astype(BF16)
            dk[rows, cols] = (dot_tn(score_grad, two_heads(q_ref[rows, cols])) * scale).astype(BF16)
            return carry

        lax.fori_loop(0, PAIRS, step, 0)
    scaled, inverse = norm_stats(tok_ref[...].astype(F32))
    normed = (scaled * vec_ref[0:1, :] + vec_ref[1:2, :]).astype(BF16)
    put(0, dot_tn(normed, dq[...]))
    put(1, dot_tn(normed, dk[...]))
    put(2, dot_tn(normed, dv[...]))
    norm1_grad = dot_nt(dq[...], w_ref[0]) + dot_nt(dk[...], w_ref[1]) + dot_nt(dv[...], w_ref[2])
    gvec_ref[0:1, :] = jnp.sum(norm1_grad * scaled, axis=0, keepdims=True)
    gvec_ref[1:2, :] = jnp.sum(norm1_grad, axis=0, keepdims=True)
    gtok_ref[...] = (mg[...] + norm_backward(norm1_grad * vec_ref[0:1, :], scaled, inverse)).astype(BF16)


def attn_bwd(core, tokens, cot, middle, dxs, unperm, q, k, v, mixed, probs, vec, hot, weights):
    rows = tokens.shape[0]
    return pl.pallas_call(
        attn_bwd_kernel,
        out_shape=(
            jax.ShapeDtypeStruct((rows, D), BF16),
            jax.ShapeDtypeStruct((2, D, D), BF16),
            jax.ShapeDtypeStruct((2, D, D), BF16),
            jax.ShapeDtypeStruct((8, D), F32),
        ),
        in_specs=[SMEM] + [VMEM] * 13,
        out_specs=(VMEM,) * 4,
        scratch_shapes=[pltpu.VMEM((rows, D), F32)] + [pltpu.VMEM((rows, D), BF16)] * 4,
        compiler_params=pltpu.CompilerParams(vmem_limit_bytes=48 * 1024 * 1024),
        cost_estimate=pl.CostEstimate(flops=2 * rows * D * D * 10, bytes_accessed=20 * 1024 * 1024, transcendentals=0),
        name="attn_bwd",
    )(core, tokens, cot, middle, dxs, unperm, q, k, v, mixed, probs, vec, hot, weights)


def swap(value, axis):
    return lax.ppermute(value, axis, [(0, 1), (1, 0)])


def diagonal(value):
    return lax.ppermute(value, ("y", "x"), [(i, 3 - i) for i in range(4)])


def after_kernel(value_ref, other_ref, out_ref):
    pass


def after(value, other):
    return pl.pallas_call(
        after_kernel,
        out_shape=jax.ShapeDtypeStruct(value.shape, value.dtype),
        in_specs=[ANY, ANY],
        out_specs=ANY,
        input_output_aliases={0: 0},
        name="after",
    )(value, other)


def ordered(mine, other, index, axis):
    first = jnp.where(index == 0, mine, other)
    second = jnp.where(index == 0, other, mine)
    return jnp.stack([first, second], axis=axis)


def spread(block, count):
    return lax.all_to_all(jnp.broadcast_to(block[None], (count,) + block.shape), "z", 0, 0, tiled=True)


def halves(value, index, axis):
    mine = lax.dynamic_index_in_dim(value, index, axis, keepdims=False)
    other = lax.dynamic_index_in_dim(value, 1 - index, axis, keepdims=False)
    return mine, other


def running(values, axis):
    steps = [lax.index_in_dim(values, 0, axis, keepdims=False)]
    for i in range(1, values.shape[axis]):
        steps.append(steps[-1] + lax.index_in_dim(values, i, axis, keepdims=False))
    return jnp.stack(steps, axis=axis)


def add_low(a, b):
    return (a.astype(F32) + b.astype(F32)).astype(BF16)


def body(outer, depth, tokens, modality, lengths, ln1_gain, ln1_bias, w_qkv, w_out, out_bias, ln2_gain, ln2_bias,
         w_in, in_bias, w_back, back_bias, cotangent):
    rows = tokens.shape[0]
    share = w_qkv.shape[0]
    hidden = in_bias.shape[1]
    half = hidden // 2
    planes = 2 * depth
    core = lax.axis_index("c")
    y = lax.axis_index("y")
    x = lax.axis_index("x")

    parts = [w_qkv[:, :D], w_qkv[:, D:2 * D], w_qkv[:, 2 * D:], w_out]
    mat_a = jnp.where(core == 0, parts[0], parts[2])
    mat_b = jnp.where(core == 0, parts[1], parts[3])
    small = jnp.stack([ln1_gain, ln1_bias, out_bias, ln2_gain, ln2_bias, back_bias[0], back_bias[1], back_bias[2]])
    small = jnp.pad(small, ((0, 0), (0, 128 - share)))
    small = jnp.concatenate([small, jnp.pad(in_bias, ((0, 5), (0, D - 128 - hidden)))], axis=1)
    message = jnp.concatenate([mat_a, small, mat_b], axis=0)
    cut = share + 8
    first = spread(message, depth)
    near = [first, swap(first, "x"), swap(first, "y"), diagonal(first)]
    pieces = near + [swap(piece, "c") for piece in near]
    small_x = ordered(near[0][:, share:cut], near[1][:, share:cut], x, 1)
    small_other = ordered(near[2][:, share:cut], near[3][:, share:cut], x, 1)
    rows_all = ordered(small_x, small_other, y, 1).reshape(2 * planes, 8, D)
    vec = jnp.transpose(rows_all[:, :, :share], (1, 0, 2)).reshape(8, D).astype(F32)
    bias_all = rows_all[:, :EXPERTS, 128:128 + hidden].reshape(planes, 2, EXPERTS, 2, half)
    bias_mine = lax.dynamic_index_in_dim(bias_all, x, 1, keepdims=False)
    bias_mine = lax.dynamic_index_in_dim(bias_mine, core, 2, keepdims=False)
    bias_mine = jnp.transpose(bias_mine, (1, 0, 2)).reshape(EXPERTS, 1, planes * half).astype(F32)

    hot = modality.astype(F32)
    before = jnp.arange(rows, dtype=jnp.int32)
    triangle = (before[None, :] < before[:, None]).astype(BF16)
    rank = dot(triangle, hot.astype(BF16))
    counts = jnp.sum(modality, axis=0)
    units = (counts + UNIT - 1) // UNIT
    starts = running(units, 0) - units
    place = jnp.sum(hot * (rank + (starts * UNIT).astype(F32)[None, :]), axis=1).astype(jnp.int32)
    room = rows // UNIT + EXPERTS - 1
    slots = jnp.arange(room * UNIT, dtype=jnp.int32)
    perm = (slots[:, None] == place[None, :]).astype(BF16)
    unperm = (place[:, None] == slots[None, :]).astype(BF16)
    cs = dot(perm, cotangent).astype(BF16)

    def four(value):
        beside = swap(value, "x")
        return [value, beside, swap(value, "c"), swap(beside, "c")]

    units_all = jnp.stack(four(units.astype(F32))).astype(jnp.int32)
    starts_all = running(units_all, 1) - units_all + (jnp.arange(4, dtype=jnp.int32) * room)[:, None]
    ends = running(units_all, 0)
    begins = ends - units_all
    totals = ends[3]
    index = jnp.arange(4 * rows // UNIT + UNITS, dtype=jnp.int32)[:, None, None]
    inside = (index >= begins[None]) & (index < ends[None])
    table = jnp.sum(jnp.where(inside, starts_all[None] + index - begins[None], 0), axis=1).T

    cs_all = four(after(cs, near[3]))

    columns = w_in.reshape(EXPERTS, share, planes, 2, 2, half)
    columns = lax.dynamic_index_in_dim(columns, core, 4, keepdims=False)
    in_mine, in_other = halves(columns, x, 3)
    in_mine = in_mine.reshape(EXPERTS, share, planes * half)
    in_other = in_other.reshape(EXPERTS, share, planes * half)
    in_pair = ordered(in_mine, swap(in_other, "x"), x, 1).reshape(EXPERTS, 2 * share, planes * half)
    back_mine = lax.dynamic_slice_in_dim(w_back, core * half, half, 1)
    experts = []
    wait_for = [first, near[3], None]
    for e in range(EXPERTS):
        wait = experts[0][0] if e == 2 else wait_for[e]
        block = after(jnp.concatenate([in_pair[e], back_mine[e]], axis=0), wait)
        got = spread(block, depth)
        experts.append([got, swap(got, "y")])

    where = jnp.stack([core, y, x]).astype(jnp.int32)
    middle, xs, q, k, v, mixed, probs, weights = attn_fwd(where, lengths, tokens, vec, perm, pieces, share)
    xs_all = four(xs)

    state = None
    grads, bias_grads = [], []
    for e in range(EXPERTS):
        *state, mine, other, bias_grad = ffn(
            table[e], totals[e][None], where, xs_all, cs_all, experts[e], bias_mine[e], state
        )
        bias_grads.append(bias_grad)
        grads.append((mine, other))
    used = (jnp.sum(units) * UNIT).astype(jnp.int32)

    def home(near, far):
        near = add_low(near, swap(far, "c")).reshape(2, room * UNIT, D)
        total = near[0].astype(F32) + swap(near[1], "x").astype(F32)
        return jnp.where(slots[:, None] < used, total, 0.0).astype(BF16)

    dxs = home(state[2], state[3])
    shards = []
    for mine, other in grads:
        summed = add_low(mine, swap(other, "y"))
        summed = lax.all_to_all(summed, "z", 0, 0, tiled=True)
        shards.append(jnp.sum(summed.astype(F32), axis=0))

    hot_rows = jnp.pad(jnp.transpose(modality.astype(BF16)), ((0, 5), (0, 0)))
    grad_tokens, keep, send, gvec = attn_bwd(
        where, tokens, cotangent, middle, dxs, unperm, q, k, v, mixed, probs, vec, hot_rows, weights,
    )
    outs = home(state[0], state[1])
    output = (middle + dot(unperm, outs) + dot(hot.astype(BF16), vec[5:8].astype(BF16))).astype(BF16)

    vec_msg = jnp.transpose(gvec.reshape(8, 2 * planes, share), (1, 0, 2))
    vec_msg = jnp.pad(vec_msg, ((0, 0), (0, 0), (0, 128 - share)))
    in_grad = jnp.concatenate(bias_grads, axis=0).reshape(EXPERTS, planes, half)
    in_grad = jnp.transpose(in_grad, (1, 0, 2))[:, None, :, None, :]
    in_grad = in_grad * (jnp.arange(2) == x).astype(F32)[None, :, None, None, None]
    in_grad = in_grad * (jnp.arange(2) == core).astype(F32)[None, None, None, :, None]
    in_grad = in_grad.reshape(2 * planes, EXPERTS, hidden)
    in_grad = jnp.pad(in_grad, ((0, 0), (0, 5), (0, D - 128 - hidden)))
    vec_msg = jnp.concatenate([vec_msg, in_grad], axis=2).astype(BF16)
    keep = keep.reshape(2, 2 * planes, share, D)
    got = swap(send, "c").reshape(2, 2 * planes, share, D)
    vec_sum = add_low(vec_msg, swap(vec_msg, "c"))
    part = jnp.concatenate([add_low(keep[0], got[0]), vec_sum, add_low(keep[1], got[1])], axis=1)
    part = part.reshape(depth, 2, 2, cut + share, D)
    mine_y, other_y = halves(part, y, 1)
    mine, other_x = halves(mine_y, x, 1)
    only_y, other = halves(other_y, x, 1)
    part = mine.astype(F32) + swap(other_x, "x").astype(F32) + swap(only_y, "y").astype(F32)
    part = (part + diagonal(other).astype(F32)).astype(BF16)
    done = lax.all_to_all(part, "z", 0, 0, tiled=True)
    done = jnp.sum(done.astype(F32), axis=0)
    small = done[share:cut]
    done_low = done.astype(BF16)
    pair = jnp.stack([done_low[:share], done_low[cut:]])
    away = swap(pair, "c")
    grad_q = jnp.where(core == 0, pair[0], away[0])
    grad_k = jnp.where(core == 0, pair[1], away[1])
    grad_v = jnp.where(core == 0, away[0], pair[0])
    grad_o = jnp.where(core == 0, away[1], pair[1])
    grad_w_qkv = jnp.concatenate([grad_q, grad_k, grad_v], axis=1)

    shards = jnp.stack(shards).astype(BF16)
    in_mine, in_other = halves(shards[:, :2 * share].reshape(EXPERTS, 2, share, D), x, 1)
    in_pair = ordered(in_mine, swap(in_other, "x"), x, 2)
    in_pair_c, back_c = swap(in_pair, "c"), swap(shards[:, 2 * share:], "c")
    grad_w_in = ordered(in_pair, in_pair_c, core, 3)
    grad_w_in = grad_w_in.reshape(EXPERTS, share, 2, 2, planes, half)
    grad_w_in = jnp.transpose(grad_w_in, (0, 1, 4, 2, 3, 5)).reshape(EXPERTS, share, 2 * planes * hidden)
    grad_w_back = ordered(shards[:, 2 * share:], back_c, core, 1).reshape(EXPERTS, hidden, D)

    result = (
        small[0, :share], small[1, :share], grad_w_qkv, grad_o, small[2, :share], small[3, :share], small[4, :share],
        grad_w_in, small[:EXPERTS, 128:128 + hidden], grad_w_back, small[5:8, :share],
    )
    if outer > 1:
        result = tuple(lax.psum(item.astype(BF16), "ro") for item in result)
    return (output, grad_tokens) + tuple(item.astype(F32) for item in result)


def solution(mesh):
    reps, shards = mesh.shape["rep"], mesh.shape["fsdp"]
    grid = Mesh(mesh.devices.reshape(reps // 2, 2, shards // 4, 2, 2), ("ro", "c", "z", "y", "x"))
    fsdp = ("z", "y", "x")
    every = ("ro", "c", "z", "y", "x")
    vector, matrix, stack, lines = P(fsdp), P(fsdp, None), P(None, fsdp, None), P(None, fsdp)
    placed = (
        P(every, None), P(every, None), P(every), vector, vector, matrix, matrix, vector, vector, vector,
        stack, lines, stack, lines, P(every, None),
    )
    out = (
        P(every, None), P(every, None), vector, vector, matrix, matrix, vector, vector, vector,
        stack, lines, stack, lines,
    )
    return jax.shard_map(
        functools.partial(body, reps // 2, shards // 4), mesh=grid, in_specs=placed, out_specs=out, check_vma=False
    )
```

time: 1860 us -> 399 us (0.21)
  waiting for transfers between devices: 1300 us -> 145 us
  blocking collectives: 267 us -> 0 us
  matrix products: 171 us -> 5.77 us
  Pallas kernels: 0 us -> 91.5 us
  starting transfers between devices: 0.65 us -> 68.8 us
  local copies, waits for them, and re-layouts: 68.7 us -> 39.8 us
    unnamed x14 -> x0, waiting for transfers between devices: 643 us -> none
    reduce_scatter x3 -> x0, waiting for transfers between devices: 409 us -> none  [the longest x1 224 us: body(): lax.psum_scatter(grad_w_back.astype(jnp.bfloat16), 'fsdp', scatter_dimens...]
    all_gather x4 -> x0, waiting for transfers between devices: 228 us -> none  [the longest x1 115 us: body(): lax.all_gather(w_in, 'fsdp', axis=1, tiled=True)]
    unnamed x3 -> x0, blocking collectives: 191 us -> none
    dot_general x18 -> x4, matrix products: 171 us -> 5.77 us  [dot(): lax.dot_general(a, b, (((1,), (0,)), ((), ())), preferred_element_type=F32)]
    ppermute x0 -> x36, waiting for transfers between devices: none -> 103 us  [the longest x34 89.5 us: swap(): return lax.ppermute(value, axis, [(0, 1), (1, 0)])]
    pallas_call x0 -> x9, Pallas kernels: none -> 91.5 us  [the longest x3 44.4 us: ffn(): pl.pallas_call(functools.partial(ffn_kernel, first), out_shape=(tokens,)...]
    all_gather x2 -> x0, blocking collectives: 73.8 us -> none  [the longest x1 37.7 us: body(): lax.all_gather(back_bias, 'fsdp', axis=1, tiled=True)]
  transfers between devices with their start and end apart: 11 -> 44, of which waited for: 9 -> 16; matrix products, arithmetic and copies ran while one was open for 11% -> 16% of each run, Pallas kernels for 0% -> 23%
where the time goes in v1:
time: 399 us; the launch traced here: 392 us
  waiting for transfers between devices  145 us (36%)
  Pallas kernels  91.5 us (23%)
  starting transfers between devices  68.8 us (17%)
  local copies, waits for them, and re-layouts  39.8 us (10%)
  other arithmetic  37.2 us (9%)
  matrix products  5.77 us (1%)
  between operations  4.6 us (1%)
    ppermute x34, waiting for transfers between devices, swap(): return lax.ppermute(value, axis, [(0, 1), (1, 0)])  89.5 us
    pallas_call x3, Pallas kernels, ffn(): pl.pallas_call(functools.partial(ffn_kernel, first), out_shape=(tokens,)...  44.4 us
    pallas_call x1, Pallas kernels, attn_bwd(): pl.pallas_call(attn_bwd_kernel, out_shape=(jax.ShapeDtypeStruct((rows, D)...  25.8 us
    ppermute x34, starting transfers between devices, swap(): return lax.ppermute(value, axis, [(0, 1), (1, 0)])  25.4 us
    pallas_call x1, Pallas kernels, attn_fwd(): pl.pallas_call(functools.partial(attn_fwd_kernel, share), out_shape=(jax....  21.4 us
    all_to_all x4, starting transfers between devices, spread(): lax.all_to_all(jnp.broadcast_to(block[None], (count,) + block.shape), 'z'...  20.5 us
    all_to_all x3, waiting for transfers between devices, body(): summed = lax.all_to_all(summed, 'z', 0, 0, tiled=True)  20.3 us
    all_to_all x4, waiting for transfers between devices, spread(): lax.all_to_all(jnp.broadcast_to(block[None], (count,) + block.shape), 'z'...  20.1 us
  transfers between devices with their start and end apart: 44, of which 16 were waited for; matrix products, arithmetic and copies ran while one was open for 16% of the time, Pallas kernels for 23%

profile of v1, /device:TPU:0, one launch (start us, length us, event | category | flops | bytes accessed | tf_op | source)
XLA Modules:
  0.0 392.2 jit_solution(8292747457507760491)
XLA Ops:
  4.1 6.3 %all-to-all-start = ((bf16[4,104,768]{2,1,0:T(8,128)(2,1)}), bf16[4,104,768]{2,1,0:T(8,128)(2,1)S(1)}, u32[]{:S(2)}, u32[]{:S(2)}) async-start(bf16[4,104,768]{2,1,0:T(8,128)(2,1)} %broadcast_in_dim.24), calls=%async_computation | async-start | bytes 1277952 | tf_op jit(solution)/shard_map/all_to_all | solution.py:384
  11.6 3.9 dynamic-slice_reduce_fusion
  15.7 1.6 collective-permute-start.16
  18.2 4.4 %collective-permute-done.16 = bf16[3,48,768]{2,1,0:T(8,128)(2,1)S(1)} collective-permute-done((bf16[3,48,768]{2,1,0:T(8,128)(2,1)S(1)}, bf16[3,48,768]{2,1,0:T(8,128)(2,1)S(1)}, u32[]{:S(2)}, u32[]{:S(2)}) %collective-permute-start.16) | collective-permute-done | bytes 221216 | tf_op jit(solution)/shard_map/ppermute | solution.py:355
  23.5 3.9 all-to-all-done.rest_0_.other_ref
  28.2 2.1 broadcast_in_dim.27
  30.3 4.4 %all-to-all-start.1 = ((bf16[4,192,768]{2,1,0:T(8,128)(2,1)}), bf16[4,192,768]{2,1,0:T(8,128)(2,1)}, u32[]{:S(2)}, u32[]{:S(2)}) async-start(bf16[4,192,768]{2,1,0:T(8,128)(2,1)} %broadcast_in_dim.27), calls=%async_computation.1 | async-start | bytes 2359296 | tf_op jit(solution)/shard_map/all_to_all | solution.py:384
  46.7 13.0 %collective-permute-done.2.rest_3_.other_ref = bf16[4,104,768]{2,1,0:T(8,128)(2,1)} collective-permute-done((bf16[4,104,768]{2,1,0:T(8,128)(2,1)S(1)}, bf16[4,104,768]{2,1,0:T(8,128)(2,1)}, u32[]{:S(2)}, u32[]{:S(2)}) %collective-permute-start.2) | collective-permute-done | bytes 639008 | tf_op jit(solution)/shard_map/ppermute | solution.py:359
  59.7 3.2 all-to-all-done.1.other_ref.rest_8_
  62.8 2.0 broadcast_in_dim.29
  64.9 4.7 %all-to-all-start.3 = ((bf16[4,192,768]{2,1,0:T(8,128)(2,1)}), bf16[4,192,768]{2,1,0:T(8,128)(2,1)}, u32[]{:S(2)}, u32[]{:S(2)}) async-start(bf16[4,192,768]{2,1,0:T(8,128)(2,1)} %broadcast_in_dim.29), calls=%async_computation.3 | async-start | bytes 2359296 | tf_op jit(solution)/shard_map/all_to_all | solution.py:384
  79.1 21.4 %attn_fwd.1 = (f32[512,768]{1,0:T(8,128)}, bf16[544,768]{1,0:T(8,128)(2,1)}, bf16[512,768]{1,0:T(8,128)(2,1)}, bf16[512,768]{1,0:T(8,128)(2,1)}, bf16[512,768]{1...) custom-call(s32[3]{0:T(128)S(1)} %pad_add_fusion.1.where_ref.core_ref, ...), custom_call_target="tpu_custom_call" | custom-call | flops 3019898880 | bytes 14680064 | tf_op jit(solution)/shard_map/attn_fwd/pallas_call | solution.py:129
  101.4 2.2 broadcast_in_dim.28
  103.6 5.1 %all-to-all-start.2 = ((bf16[4,192,768]{2,1,0:T(8,128)(2,1)}), bf16[4,192,768]{2,1,0:T(8,128)(2,1)}, u32[]{:S(2)}, u32[]{:S(2)}) async-start(bf16[4,192,768]{2,1,0:T(8,128)(2,1)} %broadcast_in_dim.28), calls=%async_computation.2 | async-start | bytes 2359296 | tf_op jit(solution)/shard_map/all_to_all | solution.py:384
  110.1 1.5 collective-permute-start.19
  113.6 7.7 %collective-permute-done.10.rest_1_ = bf16[544,768]{1,0:T(8,128)(2,1)} collective-permute-done((bf16[544,768]{1,0:T(8,128)(2,1)}, bf16[544,768]{1,0:T(8,128)(2,1)}, u32[]{:S(2)}, u32[]{:S(2)}) %collective-permute-start.10) | collective-permute-done | bytes 835616 | tf_op jit(solution)/shard_map/ppermute | solution.py:355
  121.7 1.6 collective-permute-start.18
  124.3 13.1 %all-to-all-done.2.rest_8_ = bf16[4,192,768]{2,1,0:T(8,128)(2,1)} async-done(((bf16[4,192,768]{2,1,0:T(8,128)(2,1)}), bf16[4,192,768]{2,1,0:T(8,128)(2,1)}, u32[]{:S(2)}, u32[]{:S(2)}) %all-to-all-start.2) | async-done | bytes 1179680 | tf_op jit(solution)/shard_map/all_to_all | solution.py:384
  137.3 1.5 collective-permute-start.17
  139.1 14.7 %ffn.3 = (bf16[1088,768]{1,0:T(8,128)(2,1)}, bf16[1088,768]{1,0:T(8,128)(2,1)}, bf16[1088,768]{1,0:T(8,128)(2,1)}, bf16[1088,768]{1,0:T(8,128)(2,1)}, bf16[4,192...) custom-call(s32[144]{0:T(256)S(1)} %bitcast.145, s32[1]{0:T(128)} %bitcast.35.tot_ref, ...), custom_call_target="tpu_custom_call" | custom-call | flops 7247757312 | bytes 20971520 | tf_op jit(solution)/shard_map/ffn/pallas_call | solution.py:250
  153.9 1.6 collective-permute-start.30
  155.5 9.0 %collective-permute-done.18.rest_9_ = bf16[4,192,768]{2,1,0:T(8,128)(2,1)} collective-permute-done((bf16[4,192,768]{2,1,0:T(8,128)(2,1)}, bf16[4,192,768]{2,1,0:T(8,128)(2,1)}, u32[]{:S(2)}, u32[]{:S(2)}) %collective-permute-start.18) | collective-permute-done | bytes 1179680 | tf_op jit(solution)/shard_map/ppermute | solution.py:355
  164.4 14.9 %ffn.4 = (bf16[1088,768]{1,0:T(8,128)(2,1)}, bf16[1088,768]{1,0:T(8,128)(2,1)}, bf16[1088,768]{1,0:T(8,128)(2,1)}, bf16[1088,768]{1,0:T(8,128)(2,1)}, bf16[4,192...) custom-call(s32[144]{0:T(256)S(1)} %bitcast.144, ...), custom_call_target="tpu_custom_call", output_to_operand_aliasing={{0}: (14, {}), {1}: (15, {}), {2}: (16, {}), {3}: (17, {})} | custom-call | flops 7247757312 | bytes 20971520 | tf_op jit(solution)/shard_map/ffn/pallas_call | solution.py:250
  179.3 10.3 %collective-permute-done.17.rest_9_ = bf16[4,192,768]{2,1,0:T(8,128)(2,1)S(1)} collective-permute-done((bf16[4,192,768]{2,1,0:T(8,128)(2,1)}, bf16[4,192,768]{2,1,0:T(8,128)(2,1)S(1)}, u32[]{:S(2)}, u32[]{:S(2)}) %collective-permute-start.17) | collective-permute-done | bytes 1179680 | tf_op jit(solution)/shard_map/ppermute | solution.py:355
  190.6 14.8 %ffn.5 = (bf16[1088,768]{1,0:T(8,128)(2,1)}, bf16[1088,768]{1,0:T(8,128)(2,1)}, bf16[1088,768]{1,0:T(8,128)(2,1)}, bf16[1088,768]{1,0:T(8,128)(2,1)}, bf16[4,192...) custom-call(s32[144]{0:T(256)S(1)} %bitcast.143, ...), custom_call_target="tpu_custom_call", output_to_operand_aliasing={{0}: (14, {}), {1}: (15, {}), {2}: (16, {}), {3}: (17, {})} | custom-call | flops 7247757312 | bytes 20971520 | tf_op jit(solution)/shard_map/ffn/pallas_call | solution.py:250
  205.5 9.0 %collective-permute-done.30 = bf16[4,192,768]{2,1,0:T(8,128)(2,1)S(1)} collective-permute-done((bf16[4,192,768]{2,1,0:T(8,128)(2,1)}, bf16[4,192,768]{2,1,0:T(8,128)(2,1)S(1)}, u32[]{:S(2)}, u32[]{:S(2)}) %collective-permute-start.30) | collective-permute-done | bytes 1179680 | tf_op jit(solution)/shard_map/ppermute | solution.py:355
  215.8 5.1 %all-to-all-start.5 = ((bf16[4,192,768]{2,1,0:T(8,128)(2,1)}), bf16[4,192,768]{2,1,0:T(8,128)(2,1)}, u32[]{:S(2)}, u32[]{:S(2)}) async-start(bf16[4,192,768]{2,1,0:T(8,128)(2,1)} %add_convert_fusion.4), calls=%async_computation.5 | async-start | bytes 2359296 | tf_op jit(solution)/shard_map/all_to_all | solution.py:502
  220.9 1.5 collective-permute-start.31
  223.6 2.4 add_convert_fusion
  228.1 20.3 %collective-permute-done.31 = bf16[4,192,768]{2,1,0:T(8,128)(2,1)S(1)} collective-permute-done((bf16[4,192,768]{2,1,0:T(8,128)(2,1)}, bf16[4,192,768]{2,1,0:T(8,128)(2,1)S(1)}, u32[]{:S(2)}, u32[]{:S(2)}) %collective-permute-start.31) | collective-permute-done | bytes 1179680 | tf_op jit(solution)/shard_map/ppermute | solution.py:355
  249.8 5.0 %all-to-all-start.6 = ((bf16[4,192,768]{2,1,0:T(8,128)(2,1)}), bf16[4,192,768]{2,1,0:T(8,128)(2,1)}, u32[]{:S(2)}, u32[]{:S(2)}) async-start(bf16[4,192,768]{2,1,0:T(8,128)(2,1)} %add_convert_fusion.3), calls=%async_computation.6 | async-start | bytes 2359296 | tf_op jit(solution)/shard_map/all_to_all | solution.py:502
  255.5 1.6 collective-permute-start.32
  257.4 2.3 select_convert_fusion.dxs_ref
  263.1 25.8 %attn_bwd.1 = (bf16[512,768]{1,0:T(8,128)(2,1)}, bf16[2,768,768]{2,1,0:T(8,128)(2,1)}, bf16[2,768,768]{2,1,0:T(8,128)(2,1)}, f32[8,768]{1,0:T(8,128)S(1)}) custom-call(s32[3]{0:T(128)S(1)} %pad_add_fusion.1.where_ref.core_ref, bf16[512,768]{1,0:T(8,128)(2,1)S(1)} %copy-done.4, bf16[512,768]{1,0:T(8,128)(2,1)S(1)} %copy-done.6, ...), custom_call_target="tpu_custom_call" | custom-call | flops 6039797760 | bytes 20971520 | tf_op jit(solution)/shard_map/attn_bwd/pallas_call | solution.py:337
  290.7 5.2 %all-to-all-start.7 = ((bf16[4,192,768]{2,1,0:T(8,128)(2,1)}), bf16[4,192,768]{2,1,0:T(8,128)(2,1)}, u32[]{:S(2)}, u32[]{:S(2)}) async-start(bf16[4,192,768]{2,1,0:T(8,128)(2,1)} %add_convert_fusion.2), calls=%async_computation.7 | async-start | bytes 2359296 | tf_op jit(solution)/shard_map/all_to_all | solution.py:502
  296.5 1.5 reduce
  298.3 2.4 add_convert_fusion.1
  302.8 1.5 reduce.1
  304.5 20.3 %all-to-all-done.7 = bf16[4,192,768]{2,1,0:T(8,128)(2,1)} async-done(((bf16[4,192,768]{2,1,0:T(8,128)(2,1)}), bf16[4,192,768]{2,1,0:T(8,128)(2,1)}, u32[]{:S(2)}, u32[]{:S(2)}) %all-to-all-start.7) | async-done | bytes 1179680 | tf_op jit(solution)/shard_map/all_to_all | solution.py:502
  324.8 1.5 reduce.2
  328.0 2.2 add_convert_fusion.6
  332.3 1.7 collective-permute-start.28
  336.8 27.6 %collective-permute-done.33 = bf16[3,48,768]{2,1,0:T(8,128)(2,1)S(1)} collective-permute-done((bf16[3,48,768]{2,1,0:T(8,128)(2,1)S(1)}, bf16[3,48,768]{2,1,0:T(8,128)(2,1)S(1)}, u32[]{:S(2)}, u32[]{:S(2)}) %collective-permute-start.33) | collective-permute-done | bytes 221216 | tf_op jit(solution)/shard_map/ppermute | solution.py:355
  366.3 4.4 %all-to-all-start.4 = ((bf16[4,104,768]{2,1,0:T(8,128)(2,1)}), bf16[4,104,768]{2,1,0:T(8,128)(2,1)}, u32[]{:S(2)}, u32[]{:S(2)}) async-start(bf16[4,104,768]{2,1,0:T(8,128)(2,1)} %fusion.4), calls=%async_computation.4 | async-start | bytes 1277952 | tf_op jit(solution)/shard_map/all_to_all | solution.py:531
  371.8 3.6 fusion
  378.6 1.8 copy.89
  380.4 4.4 %reshape.528 = f32[3,48,3072]{2,1,0:T(8,128)} reshape(f32[3,48,8,2,2,96]{5,4,3,2,1,0:T(2,128)S(1)} %copy.89) | data formatting | bytes 3538944 | tf_op jit(solution)/shard_map/convert_element_type | solution.py:558
  384.8 1.6 all-to-all-done.4
  (233 shorter events, 66.2 us)
Async XLA Ops:
  4.1 23.3 %all-to-all-start = ((bf16[4,104,768]{2,1,0:T(8,128)(2,1)}), bf16[4,104,768]{2,1,0:T(8,128)(2,1)S(1)}, u32[]{:S(2)}, u32[]{:S(2)}) async-start(bf16[4,104,768]{2,1,0:T(8,128)(2,1)} %broadcast_in_dim.24), calls=%async_computation | async-start | bytes 1277952 | tf_op jit(solution)/shard_map/all_to_all | solution.py:384
  15.7 7.0 %collective-permute-start.16 = (bf16[3,48,768]{2,1,0:T(8,128)(2,1)S(1)}, bf16[3,48,768]{2,1,0:T(8,128)(2,1)S(1)}, u32[]{:S(2)}, u32[]{:S(2)}) collective-permute-start(bf16[3,48,768]{2,1,0:T(8,128)(2,1)S(1)} %reshape.520), channel_id=1, source_target_pairs={{0,1},{1,0},{2,3},{3,2},{4,5},{5,4},{6,7},{7,6},{8,9},{9,8},{10,11... | collective-permute-start | bytes 663560 | tf_op jit(solution)/shard_map/ppermute | solution.py:355
  30.3 32.5 %all-to-all-start.1 = ((bf16[4,192,768]{2,1,0:T(8,128)(2,1)}), bf16[4,192,768]{2,1,0:T(8,128)(2,1)}, u32[]{:S(2)}, u32[]{:S(2)}) async-start(bf16[4,192,768]{2,1,0:T(8,128)(2,1)} %broadcast_in_dim.27), calls=%async_computation.1 | async-start | bytes 2359296 | tf_op jit(solution)/shard_map/all_to_all | solution.py:384
  39.8 35.3 %collective-permute-start.7 = (f32[3]{0:T(128)}, f32[3]{0:T(128)}, u32[]{:S(2)}, u32[]{:S(2)}) collective-permute-start(f32[3]{0:T(128)} %get-tuple-element.142), channel_id=1, source_target_pairs={{0,1},{1,0},{2,3},{3,2},{4,5},{5,4},{6,7},{7,6},{8,9},{9,8},{10,11... | collective-permute-start | bytes 44 | tf_op jit(solution)/shard_map/ppermute | solution.py:355
  41.3 18.4 %collective-permute-start.2 = (bf16[4,104,768]{2,1,0:T(8,128)(2,1)S(1)}, bf16[4,104,768]{2,1,0:T(8,128)(2,1)}, u32[]{:S(2)}, u32[]{:S(2)}) collective-permute-start(bf16[4,104,768]{2,1,0:T(8,128)(2,1)S(1)} %copy-done.1), channel_id=1, source_target_pairs={{0,3},{1,2},{2,1},{3,0},{4,7},{5,6},{6,5},{7,4},{8,11},{9,10},{10,... | collective-permute-start | bytes 1916936 | tf_op jit(solution)/shard_map/ppermute | solution.py:359
  43.9 29.1 %collective-permute-start.1 = (bf16[4,104,768]{2,1,0:T(8,128)(2,1)S(1)}, bf16[4,104,768]{2,1,0:T(8,128)(2,1)S(1)}, u32[]{:S(2)}, u32[]{:S(2)}) collective-permute-start(bf16[4,104,768]{2,1,0:T(8,128)(2,1)S(1)} %copy-done.1), channel_id=1, source_target_pairs={{0,2},{2,0},{1,3},{3,1},{4,6},{6,4},{5,7},{7,5},{8,10},{10,8},{9,1... | collective-permute-start | bytes 1916936 | tf_op jit(solution)/shard_map/ppermute | solution.py:355
  44.5 28.5 %collective-permute-start = (bf16[4,104,768]{2,1,0:T(8,128)(2,1)S(1)}, bf16[4,104,768]{2,1,0:T(8,128)(2,1)S(1)}, u32[]{:S(2)}, u32[]{:S(2)}) collective-permute-start(bf16[4,104,768]{2,1,0:T(8,128)(2,1)S(1)} %copy-done.1), channel_id=1, source_target_pairs={{0,1},{1,0},{2,3},{3,2},{4,5},{5,4},{6,7},{7,6},{8,9},{9,8},{10,11... | collective-permute-start | bytes 1916936 | tf_op jit(solution)/shard_map/ppermute | solution.py:355
  64.9 36.5 %all-to-all-start.3 = ((bf16[4,192,768]{2,1,0:T(8,128)(2,1)}), bf16[4,192,768]{2,1,0:T(8,128)(2,1)}, u32[]{:S(2)}, u32[]{:S(2)}) async-start(bf16[4,192,768]{2,1,0:T(8,128)(2,1)} %broadcast_in_dim.29), calls=%async_computation.3 | async-start | bytes 2359296 | tf_op jit(solution)/shard_map/all_to_all | solution.py:384
  72.4 2.9 collective-permute-start.3
  72.4 4.1 %collective-permute-start.6 = (bf16[4,104,768]{2,1,0:T(8,128)(2,1)}, bf16[4,104,768]{2,1,0:T(8,128)(2,1)}, u32[]{:S(2)}, u32[]{:S(2)}) collective-permute-start(bf16[4,104,768]{2,1,0:T(8,128)(2,1)} %collective-permute-done.2.rest_3_.other_ref), channel_id=1, source_target_pairs={{0,16},{16,0},{1,17},{17,1},{2,18},{18,2},{3,19},{19,3},{4,20},{20... | collective-permute-start | bytes 1916936 | tf_op jit(solution)/shard_map/ppermute | solution.py:355
  72.9 5.1 %collective-permute-start.4 = (bf16[4,104,768]{2,1,0:T(8,128)(2,1)S(1)}, bf16[4,104,768]{2,1,0:T(8,128)(2,1)}, u32[]{:S(2)}, u32[]{:S(2)}) collective-permute-start(bf16[4,104,768]{2,1,0:T(8,128)(2,1)S(1)} %collective-permute-done.rest_1_), channel_id=1, source_target_pairs={{0,16},{16,0},{1,17},{17,1},{2,18},{18,2},{3,19},{19,3},{4,20},{20... | collective-permute-start | bytes 1916936 | tf_op jit(solution)/shard_map/ppermute | solution.py:355
  73.0 5.1 %collective-permute-start.5 = (bf16[4,104,768]{2,1,0:T(8,128)(2,1)S(1)}, bf16[4,104,768]{2,1,0:T(8,128)(2,1)}, u32[]{:S(2)}, u32[]{:S(2)}) collective-permute-start(bf16[4,104,768]{2,1,0:T(8,128)(2,1)S(1)} %collective-permute-done.1.rest_2_), channel_id=1, source_target_pairs={{0,16},{16,0},{1,17},{17,1},{2,18},{18,2},{3,19},{19,3},{4,20},{20... | collective-permute-start | bytes 1916936 | tf_op jit(solution)/shard_map/ppermute | solution.py:355
  75.1 33.5 %collective-permute-start.8 = (f32[3]{0:T(128)}, f32[3]{0:T(128)}, u32[]{:S(2)}, u32[]{:S(2)}) collective-permute-start(f32[3]{0:T(128)} %get-tuple-element.142), channel_id=1, source_target_pairs={{0,16},{16,0},{1,17},{17,1},{2,18},{18,2},{3,19},{19,3},{4,20},{20... | collective-permute-start | bytes 44 | tf_op jit(solution)/shard_map/ppermute | solution.py:355
  76.2 32.5 %collective-permute-start.9 = (f32[3]{0:T(128)}, f32[3]{0:T(128)S(1)}, u32[]{:S(2)}, u32[]{:S(2)}) collective-permute-start(f32[3]{0:T(128)} %collective-permute-done.7), channel_id=1, source_target_pairs={{0,16},{16,0},{1,17},{17,1},{2,18},{18,2},{3,19},{19,3},{4,20},{20... | collective-permute-start | bytes 44 | tf_op jit(solution)/shard_map/ppermute | solution.py:355
  76.6 36.7 %collective-permute-start.13 = (bf16[544,768]{1,0:T(8,128)(2,1)}, bf16[544,768]{1,0:T(8,128)(2,1)S(1)}, u32[]{:S(2)}, u32[]{:S(2)}) collective-permute-start(bf16[544,768]{1,0:T(8,128)(2,1)} %after.4.rest_4_), channel_id=1, source_target_pairs={{0,1},{1,0},{2,3},{3,2},{4,5},{5,4},{6,7},{7,6},{8,9},{9,8},{10,11... | collective-permute-start | bytes 2506760 | tf_op jit(solution)/shard_map/ppermute | solution.py:355
  100.5 20.8 %collective-permute-start.10 = (bf16[544,768]{1,0:T(8,128)(2,1)}, bf16[544,768]{1,0:T(8,128)(2,1)}, u32[]{:S(2)}, u32[]{:S(2)}) collective-permute-start(bf16[544,768]{1,0:T(8,128)(2,1)} %get-tuple-element.47.rest_0_), channel_id=1, source_target_pairs={{0,1},{1,0},{2,3},{3,2},{4,5},{5,4},{6,7},{7,6},{8,9},{9,8},{10,11... | collective-permute-start | bytes 2506760 | tf_op jit(solution)/shard_map/ppermute | solution.py:355
  103.6 33.7 %all-to-all-start.2 = ((bf16[4,192,768]{2,1,0:T(8,128)(2,1)}), bf16[4,192,768]{2,1,0:T(8,128)(2,1)}, u32[]{:S(2)}, u32[]{:S(2)}) async-start(bf16[4,192,768]{2,1,0:T(8,128)(2,1)} %broadcast_in_dim.28), calls=%async_computation.2 | async-start | bytes 2359296 | tf_op jit(solution)/shard_map/all_to_all | solution.py:384
  109.9 11.8 %collective-permute-start.14 = (bf16[544,768]{1,0:T(8,128)(2,1)S(1)}, bf16[544,768]{1,0:T(8,128)(2,1)}, u32[]{:S(2)}, u32[]{:S(2)}) collective-permute-start(bf16[544,768]{1,0:T(8,128)(2,1)S(1)} %copy-done.2), channel_id=1, source_target_pairs={{0,16},{16,0},{1,17},{17,1},{2,18},{18,2},{3,19},{19,3},{4,20},{20... | collective-permute-start | bytes 2506760 | tf_op jit(solution)/shard_map/ppermute | solution.py:355
  110.1 29.1 %collective-permute-start.19 = (bf16[4,192,768]{2,1,0:T(8,128)(2,1)}, bf16[4,192,768]{2,1,0:T(8,128)(2,1)}, u32[]{:S(2)}, u32[]{:S(2)}) collective-permute-start(bf16[4,192,768]{2,1,0:T(8,128)(2,1)} %all-to-all-done.1.other_ref.rest_8_), channel_id=1, source_target_pairs={{0,2},{2,0},{1,3},{3,1},{4,6},{6,4},{5,7},{7,5},{8,10},{10,8},{9,1... | collective-permute-start | bytes 3538952 | tf_op jit(solution)/shard_map/ppermute | solution.py:355
  113.0 11.2 %collective-permute-start.11 = (bf16[544,768]{1,0:T(8,128)(2,1)S(1)}, bf16[544,768]{1,0:T(8,128)(2,1)}, u32[]{:S(2)}, u32[]{:S(2)}) collective-permute-start(bf16[544,768]{1,0:T(8,128)(2,1)S(1)} %copy-done.3), channel_id=1, source_target_pairs={{0,16},{16,0},{1,17},{17,1},{2,18},{18,2},{3,19},{19,3},{4,20},{20... | collective-permute-start | bytes 2506760 | tf_op jit(solution)/shard_map/ppermute | solution.py:355
  113.3 25.6 %collective-permute-start.15 = (bf16[544,768]{1,0:T(8,128)(2,1)S(1)}, bf16[544,768]{1,0:T(8,128)(2,1)}, u32[]{:S(2)}, u32[]{:S(2)}) collective-permute-start(bf16[544,768]{1,0:T(8,128)(2,1)S(1)} %collective-permute-done.13.rest_5_), channel_id=1, source_target_pairs={{0,16},{16,0},{1,17},{17,1},{2,18},{18,2},{3,19},{19,3},{4,20},{20... | collective-permute-start | bytes 2506760 | tf_op jit(solution)/shard_map/ppermute | solution.py:355
  121.3 17.6 %collective-permute-start.12 = (bf16[544,768]{1,0:T(8,128)(2,1)}, bf16[544,768]{1,0:T(8,128)(2,1)}, u32[]{:S(2)}, u32[]{:S(2)}) collective-permute-start(bf16[544,768]{1,0:T(8,128)(2,1)} %collective-permute-done.10.rest_1_), channel_id=1, source_target_pairs={{0,16},{16,0},{1,17},{17,1},{2,18},{18,2},{3,19},{19,3},{4,20},{20... | collective-permute-start | bytes 2506760 | tf_op jit(solution)/shard_map/ppermute | solution.py:355
  121.7 42.7 %collective-permute-start.18 = (bf16[4,192,768]{2,1,0:T(8,128)(2,1)}, bf16[4,192,768]{2,1,0:T(8,128)(2,1)}, u32[]{:S(2)}, u32[]{:S(2)}) collective-permute-start(bf16[4,192,768]{2,1,0:T(8,128)(2,1)} %all-to-all-done.3.rest_8_), channel_id=1, source_target_pairs={{0,2},{2,0},{1,3},{3,1},{4,6},{6,4},{5,7},{7,5},{8,10},{10,8},{9,1... | collective-permute-start | bytes 3538952 | tf_op jit(solution)/shard_map/ppermute | solution.py:355
  137.3 52.3 %collective-permute-start.17 = (bf16[4,192,768]{2,1,0:T(8,128)(2,1)}, bf16[4,192,768]{2,1,0:T(8,128)(2,1)S(1)}, u32[]{:S(2)}, u32[]{:S(2)}) collective-permute-start(bf16[4,192,768]{2,1,0:T(8,128)(2,1)} %all-to-all-done.2.rest_8_), channel_id=1, source_target_pairs={{0,2},{2,0},{1,3},{3,1},{4,6},{6,4},{5,7},{7,5},{8,10},{10,8},{9,1... | collective-permute-start | bytes 3538952 | tf_op jit(solution)/shard_map/ppermute | solution.py:355
  153.9 60.6 %collective-permute-start.30 = (bf16[4,192,768]{2,1,0:T(8,128)(2,1)}, bf16[4,192,768]{2,1,0:T(8,128)(2,1)S(1)}, u32[]{:S(2)}, u32[]{:S(2)}) collective-permute-start(bf16[4,192,768]{2,1,0:T(8,128)(2,1)} %get-tuple-element.74), channel_id=1, source_target_pairs={{0,2},{2,0},{1,3},{3,1},{4,6},{6,4},{5,7},{7,5},{8,10},{10,8},{9,1... | collective-permute-start | bytes 3538952 | tf_op jit(solution)/shard_map/ppermute | solution.py:355
  190.6 23.9 %copy-start.22 = (bf16[4,192,768]{2,1,0:T(8,128)(2,1)S(1)}, bf16[4,192,768]{2,1,0:T(8,128)(2,1)}, u32[]{:S(2)}) copy-start(bf16[4,192,768]{2,1,0:T(8,128)(2,1)} %get-tuple-element.73) | copy-start | bytes 3538948
  205.4 17.0 %collective-permute-start.22 = (bf16[1088,768]{1,0:T(8,128)(2,1)}, bf16[1088,768]{1,0:T(8,128)(2,1)S(1)}, u32[]{:S(2)}, u32[]{:S(2)}) collective-permute-start(bf16[1088,768]{1,0:T(8,128)(2,1)} %get-tuple-element.59), channel_id=1, source_target_pairs={{0,16},{16,0},{1,17},{17,1},{2,18},{18,2},{3,19},{19,3},{4,20},{20... | collective-permute-start | bytes 5013512 | tf_op jit(solution)/shard_map/ppermute | solution.py:355
  215.8 34.0 %all-to-all-start.5 = ((bf16[4,192,768]{2,1,0:T(8,128)(2,1)}), bf16[4,192,768]{2,1,0:T(8,128)(2,1)}, u32[]{:S(2)}, u32[]{:S(2)}) async-start(bf16[4,192,768]{2,1,0:T(8,128)(2,1)} %add_convert_fusion.4), calls=%async_computation.5 | async-start | bytes 2359296 | tf_op jit(solution)/shard_map/all_to_all | solution.py:502
  220.9 27.5 %collective-permute-start.31 = (bf16[4,192,768]{2,1,0:T(8,128)(2,1)}, bf16[4,192,768]{2,1,0:T(8,128)(2,1)S(1)}, u32[]{:S(2)}, u32[]{:S(2)}) collective-permute-start(bf16[4,192,768]{2,1,0:T(8,128)(2,1)} %get-tuple-element.76), channel_id=1, source_target_pairs={{0,2},{2,0},{1,3},{3,1},{4,6},{6,4},{5,7},{7,5},{8,10},{10,8},{9,1... | collective-permute-start | bytes 3538952 | tf_op jit(solution)/shard_map/ppermute | solution.py:355
  225.9 23.8 %copy-start.14 = (bf16[1088,768]{1,0:T(8,128)(2,1)}, bf16[1088,768]{1,0:T(8,128)(2,1)S(1)}, u32[]{:S(2)}) copy-start(bf16[1088,768]{1,0:T(8,128)(2,1)S(1)} %add_convert_fusion) | copy-start | bytes 5013508
  225.9 22.4 %copy-start.21 = (bf16[4,192,768]{2,1,0:T(8,128)(2,1)S(1)}, bf16[4,192,768]{2,1,0:T(8,128)(2,1)}, u32[]{:S(2)}) copy-start(bf16[4,192,768]{2,1,0:T(8,128)(2,1)} %get-tuple-element.75) | copy-start | bytes 3538948
  226.9 30.5 %collective-permute-start.23 = (bf16[544,768]{1,0:T(8,128)(2,1)}, bf16[544,768]{1,0:T(8,128)(2,1)S(1)}, u32[]{:S(2)}, u32[]{:S(2)}) collective-permute-start(bf16[544,768]{1,0:T(8,128)(2,1)} %slice.287), channel_id=1, source_target_pairs={{0,1},{1,0},{2,3},{3,2},{4,5},{5,4},{6,7},{7,6},{8,9},{9,8},{10,11... | collective-permute-start | bytes 2506760 | tf_op jit(solution)/shard_map/ppermute | solution.py:355
  249.8 41.0 %all-to-all-start.6 = ((bf16[4,192,768]{2,1,0:T(8,128)(2,1)}), bf16[4,192,768]{2,1,0:T(8,128)(2,1)}, u32[]{:S(2)}, u32[]{:S(2)}) async-start(bf16[4,192,768]{2,1,0:T(8,128)(2,1)} %add_convert_fusion.3), calls=%async_computation.6 | async-start | bytes 2359296 | tf_op jit(solution)/shard_map/all_to_all | solution.py:502
  255.5 33.9 %collective-permute-start.32 = (bf16[4,192,768]{2,1,0:T(8,128)(2,1)}, bf16[4,192,768]{2,1,0:T(8,128)(2,1)S(1)}, u32[]{:S(2)}, u32[]{:S(2)}) collective-permute-start(bf16[4,192,768]{2,1,0:T(8,128)(2,1)} %get-tuple-element.78), channel_id=1, source_target_pairs={{0,2},{2,0},{1,3},{3,1},{4,6},{6,4},{5,7},{7,5},{8,10},{10,8},{9,1... | collective-permute-start | bytes 3538952 | tf_op jit(solution)/shard_map/ppermute | solution.py:355
  257.3 41.0 %collective-permute-start.20 = (bf16[1088,768]{1,0:T(8,128)(2,1)}, bf16[1088,768]{1,0:T(8,128)(2,1)}, u32[]{:S(2)}, u32[]{:S(2)}) collective-permute-start(bf16[1088,768]{1,0:T(8,128)(2,1)} %get-tuple-element.57), channel_id=1, source_target_pairs={{0,16},{16,0},{1,17},{17,1},{2,18},{18,2},{3,19},{19,3},{4,20},{20... | collective-permute-start | bytes 5013512 | tf_op jit(solution)/shard_map/ppermute | solution.py:355
  263.1 26.2 %copy-start.20 = (bf16[4,192,768]{2,1,0:T(8,128)(2,1)S(1)}, bf16[4,192,768]{2,1,0:T(8,128)(2,1)}, u32[]{:S(2)}) copy-start(bf16[4,192,768]{2,1,0:T(8,128)(2,1)} %get-tuple-element.77) | copy-start | bytes 3538948
  288.9 37.7 %collective-permute-start.24 = (bf16[2,768,768]{2,1,0:T(8,128)(2,1)}, bf16[2,768,768]{2,1,0:T(8,128)(2,1)}, u32[]{:S(2)}, u32[]{:S(2)}) collective-permute-start(bf16[2,768,768]{2,1,0:T(8,128)(2,1)} %get-tuple-element.68), channel_id=1, source_target_pairs={{0,16},{16,0},{1,17},{17,1},{2,18},{18,2},{3,19},{19,3},{4,20},{20... | collective-permute-start | bytes 7077896 | tf_op jit(solution)/shard_map/ppermute | solution.py:355
  290.7 34.1 %all-to-all-start.7 = ((bf16[4,192,768]{2,1,0:T(8,128)(2,1)}), bf16[4,192,768]{2,1,0:T(8,128)(2,1)}, u32[]{:S(2)}, u32[]{:S(2)}) async-start(bf16[4,192,768]{2,1,0:T(8,128)(2,1)} %add_convert_fusion.2), calls=%async_computation.7 | async-start | bytes 2359296 | tf_op jit(solution)/shard_map/all_to_all | solution.py:502
  298.2 6.1 %collective-permute-start.25 = (bf16[16,8,768]{2,0,1:T(8,128)(2,1)S(1)}, bf16[16,8,768]{2,0,1:T(8,128)(2,1)S(1)}, u32[]{:S(2)}, u32[]{:S(2)}) collective-permute-start(bf16[16,8,768]{2,0,1:T(8,128)(2,1)S(1)} %fusion.22), channel_id=1, source_target_pairs={{0,16},{16,0},{1,17},{17,1},{2,18},{18,2},{3,19},{19,3},{4,20},{20... | collective-permute-start | bytes 589832 | tf_op jit(solution)/shard_map/ppermute | solution.py:355
  301.6 70.2 %collective-permute-start.21 = (bf16[544,768]{1,0:T(8,128)(2,1)}, bf16[544,768]{1,0:T(8,128)(2,1)}, u32[]{:S(2)}, u32[]{:S(2)}) collective-permute-start(bf16[544,768]{1,0:T(8,128)(2,1)} %slice.284), channel_id=1, source_target_pairs={{0,1},{1,0},{2,3},{3,2},{4,5},{5,4},{6,7},{7,6},{8,9},{9,8},{10,11... | collective-permute-start | bytes 2506760 | tf_op jit(solution)/shard_map/ppermute | solution.py:355
  326.5 7.6 %collective-permute-start.35 = (bf16[3,96,768]{2,1,0:T(8,128)(2,1)S(1)}, bf16[3,96,768]{2,1,0:T(8,128)(2,1)S(1)}, u32[]{:S(2)}, u32[]{:S(2)}) collective-permute-start(bf16[3,96,768]{2,1,0:T(8,128)(2,1)S(1)} %slice.301), channel_id=1, source_target_pairs={{0,16},{16,0},{1,17},{17,1},{2,18},{18,2},{3,19},{19,3},{4,20},{20... | collective-permute-start | bytes 1327112 | tf_op jit(solution)/shard_map/ppermute | solution.py:355
  330.5 34.6 %collective-permute-start.26 = (bf16[4,104,768]{2,1,0:T(8,128)(2,1)S(1)}, bf16[4,104,768]{2,1,0:T(8,128)(2,1)S(1)}, u32[]{:S(2)}, u32[]{:S(2)}) collective-permute-start(bf16[4,104,768]{2,1,0:T(8,128)(2,1)S(1)} %get-tuple-element.90), channel_id=1, source_target_pairs={{0,1},{1,0},{2,3},{3,2},{4,5},{5,4},{6,7},{7,6},{8,9},{9,8},{10,11... | collective-permute-start | bytes 1916936 | tf_op jit(solution)/shard_map/ppermute | solution.py:355
  331.8 33.3 %collective-permute-start.27 = (bf16[4,104,768]{2,1,0:T(8,128)(2,1)S(1)}, bf16[4,104,768]{2,1,0:T(8,128)(2,1)S(1)}, u32[]{:S(2)}, u32[]{:S(2)}) collective-permute-start(bf16[4,104,768]{2,1,0:T(8,128)(2,1)S(1)} %get-tuple-element.92), channel_id=1, source_target_pairs={{0,2},{2,0},{1,3},{3,1},{4,6},{6,4},{5,7},{7,5},{8,10},{10,8},{9,1... | collective-permute-start | bytes 1916936 | tf_op jit(solution)/shard_map/ppermute | solution.py:355
  332.3 32.8 %collective-permute-start.28 = (bf16[4,104,768]{2,1,0:T(8,128)(2,1)S(1)}, bf16[4,104,768]{2,1,0:T(8,128)(2,1)S(1)}, u32[]{:S(2)}, u32[]{:S(2)}) collective-permute-start(bf16[4,104,768]{2,1,0:T(8,128)(2,1)S(1)} %get-tuple-element.91), channel_id=1, source_target_pairs={{0,3},{1,2},{2,1},{3,0},{4,7},{5,6},{6,5},{7,4},{8,11},{9,10},{10,... | collective-permute-start | bytes 1916936 | tf_op jit(solution)/shard_map/ppermute | solution.py:359
  335.1 29.3 %collective-permute-start.33 = (bf16[3,48,768]{2,1,0:T(8,128)(2,1)S(1)}, bf16[3,48,768]{2,1,0:T(8,128)(2,1)S(1)}, u32[]{:S(2)}, u32[]{:S(2)}) collective-permute-start(bf16[3,48,768]{2,1,0:T(8,128)(2,1)S(1)} %dynamic-slice_bitcast_fusion.3), channel_id=1, source_target_pairs={{0,1},{1,0},{2,3},{3,2},{4,5},{5,4},{6,7},{7,6},{8,9},{9,8},{10,11... | collective-permute-start | bytes 663560 | tf_op jit(solution)/shard_map/ppermute | solution.py:355
  366.3 20.0 %all-to-all-start.4 = ((bf16[4,104,768]{2,1,0:T(8,128)(2,1)}), bf16[4,104,768]{2,1,0:T(8,128)(2,1)}, u32[]{:S(2)}, u32[]{:S(2)}) async-start(bf16[4,104,768]{2,1,0:T(8,128)(2,1)} %fusion.4), calls=%async_computation.4 | async-start | bytes 1277952 | tf_op jit(solution)/shard_map/all_to_all | solution.py:531
  371.7 5.1 %collective-permute-start.34 = (bf16[3,48,2,768]{3,1,0,2:T(8,128)(2,1)S(1)}, bf16[3,48,2,768]{3,1,0,2:T(8,128)(2,1)S(1)}, u32[]{:S(2)}, u32[]{:S(2)}) collective-permute-start(bf16[3,48,2,768]{3,1,0,2:T(8,128)(2,1)S(1)} %pad_maximum_fusion.2), channel_id=1, source_target_pairs={{0,16},{16,0},{1,17},{17,1},{2,18},{18,2},{3,19},{19,3},{4,20},{20... | collective-permute-start | bytes 1327112 | tf_op jit(solution)/shard_map/ppermute | solution.py:355
  388.8 1.4 collective-permute-start.29
  (30 other events, 153.0 us)

commit v2 on v1

v2 whole, which is shorter than its diff:
```python
import functools
import math

import jax
import jax.numpy as jnp
from jax import lax
from jax.experimental import pallas as pl
from jax.experimental.pallas import tpu as pltpu
from jax.sharding import Mesh
from jax.sharding import PartitionSpec as P

HEADS = 12
HEAD_DIM = 64
SEQ = 256
D = 768
EXPERTS = 3
UNIT = 16
TILE = 256
UNITS = TILE // UNIT

INV_ROOT_TWO = 1.0 / math.sqrt(2.0)
INV_ROOT_TAU = 1.0 / math.sqrt(2.0 * math.pi)
F32 = jnp.float32
BF16 = jnp.bfloat16

VMEM = pl.BlockSpec(memory_space=pltpu.VMEM)
SMEM = pl.BlockSpec(memory_space=pltpu.SMEM)
ANY = pl.BlockSpec(memory_space=pl.ANY)

SMALL_LANES = 128
SMALL = pl.CostEstimate(flops=1, bytes_accessed=1, transcendentals=0)


def dot(a, b):
    return lax.dot_general(a, b, (((1,), (0,)), ((), ())), preferred_element_type=F32)


def dot_nt(a, b):
    return lax.dot_general(a, b, (((1,), (1,)), ((), ())), preferred_element_type=F32)


def dot_tn(a, b):
    return lax.dot_general(a, b, (((0,), (0,)), ((), ())), preferred_element_type=F32)


def norm_stats(values):
    average = jnp.mean(values, axis=-1, keepdims=True)
    centred = values - average
    inverse = lax.rsqrt(jnp.mean(centred * centred, axis=-1, keepdims=True) + 1e-05)
    return centred * inverse, inverse


def norm_backward(weighted, scaled, inverse):
    first = jnp.mean(weighted, axis=-1, keepdims=True)
    second = jnp.mean(weighted * scaled, axis=-1, keepdims=True)
    return inverse * (weighted - first - scaled * second)


def two_heads(block):
    low = lax.broadcasted_iota(jnp.int32, block.shape, 1) < HEAD_DIM
    nothing = jnp.zeros_like(block)
    return jnp.concatenate([jnp.where(low, block, nothing), jnp.where(low, nothing, block)], axis=0)


def merge_heads(block):
    low = lax.broadcasted_iota(jnp.int32, (SEQ, 2 * HEAD_DIM), 1) < HEAD_DIM
    return jnp.where(low, block[:SEQ], block[SEQ:])


PAIRS = HEADS // 2


def attn_fwd_kernel(share, where_ref, len_ref, place_ref, tok_ref, *rest):
    pieces = rest[:8]
    mid_ref, xs_a, xs_b, q_ref, k_ref, v_ref, mixed_ref, probs_ref, w_ref, vec_ref, bias_ref = rest[8:19]
    tok, low, sems, own_sems = rest[19:]
    fetch_tok = pltpu.make_async_copy(tok_ref, tok, own_sems.at[0])
    fetch_tok.start()
    fetch_low = [
        pltpu.make_async_copy(pieces[n].at[:, pl.ds(share, 8)], low.at[n], own_sems.at[1 + n]) for n in range(4)
    ]
    for copy in fetch_low:
        copy.start()
    core, y, x = where_ref[0], where_ref[1], where_ref[2]
    copies = ([], [])
    for matrix in range(2):
        for n, piece in enumerate(pieces):
            far, y_of, x_of = n // 4, (n // 2) % 2, n % 2
            slot = 2 * jnp.where(far == 1, 1 - core, core) + matrix
            place = 2 * jnp.where(y_of == 1, 1 - y, y) + jnp.where(x_of == 1, 1 - x, x)
            copies[matrix].append(pltpu.make_async_copy(
                piece.at[:, pl.ds(matrix * (share + 8), share)], w_ref.at[slot, :, place], sems.at[matrix, n]))
    for copy in copies[0] + copies[1]:
        copy.start()

    def weight(slot):
        return w_ref[slot].reshape(D, D)

    for copy in fetch_low:
        copy.wait()
    gather_small(share, core, y, x, low, vec_ref, bias_ref)
    fetch_tok.wait()
    values = tok[...].astype(F32)
    scaled, _ = norm_stats(values)
    normed = (scaled * vec_ref[0:1, :] + vec_ref[1:2, :]).astype(BF16)
    for copy in copies[0]:
        copy.wait()
    q_ref[...] = dot(normed, weight(0)).astype(BF16)
    v_ref[...] = dot(normed, weight(2)).astype(BF16)
    for copy in copies[1]:
        copy.wait()
    k_ref[...] = dot(normed, weight(1)).astype(BF16)
    seqs = tok_ref.shape[0] // SEQ
    for seq in range(seqs):
        length = len_ref[seq]
        rows = slice(seq * SEQ, (seq + 1) * SEQ)

        def step(pair, carry):
            cols = pl.ds(pl.multiple_of(pair * 128, 128), 128)
            both = two_heads(q_ref[rows, cols])
            scores = dot_nt(both, k_ref[rows, cols]) * (HEAD_DIM ** -0.5)
            valid = lax.broadcasted_iota(jnp.int32, scores.shape, 1) < length
            scores = jnp.where(valid, scores, -1e30)
            top = jnp.max(scores, axis=-1, keepdims=True)
            grown = jnp.exp(scores - top)
            total = jnp.sum(grown, axis=-1, keepdims=True)
            probs = (grown * (1.0 / total)).astype(BF16)
            probs_ref[seq * PAIRS + pair] = probs
            mixed_ref[rows, cols] = merge_heads(dot(probs, v_ref[rows, cols])).astype(BF16)
            return carry

        lax.fori_loop(0, PAIRS, step, 0)
    middle = tok[...].astype(F32) + dot(mixed_ref[...], weight(3)) + vec_ref[2:3, :]
    mid_ref[...] = middle
    scaled_two, _ = norm_stats(middle)
    normed_two = (scaled_two * vec_ref[3:4, :] + vec_ref[4:5, :]).astype(BF16)
    for n, target in enumerate((xs_a, xs_b)):
        slot = lax.broadcasted_iota(jnp.int32, (target.shape[0], tok.shape[0]), 0) + n * target.shape[0]
        perm = jnp.where(slot == place_ref[...], 1.0, 0.0).astype(BF16)
        target[...] = dot(perm, normed_two).astype(BF16)


def gather_small(share, core, y, x, low, vec_ref, bias_ref):
    depth = low.shape[1]
    half = D // (2 * depth)
    lane = lax.broadcasted_iota(jnp.int32, (8, D), 1)
    bias_lane = SMALL_LANES + core * half
    vec = jnp.zeros((8, D), F32)
    bias = jnp.zeros((8, D), F32)
    for n in range(4):
        place_y = 1 - y if n // 2 else y
        place_x = 1 - x if n % 2 else x
        for z in range(depth):
            rows = low[n, z].astype(F32)
            shift = (4 * z + 2 * place_y + place_x) * share
            vec += pltpu.roll(jnp.where(lane < share, rows, 0.0), shift, 1)
            if n % 2 == 0:
                mine = jnp.where((lane >= bias_lane) & (lane < bias_lane + half), rows, 0.0)
                bias += pltpu.roll(mine, lax.rem((2 * z + place_y) * half - bias_lane + D, D), 1)
    vec_ref[...] = vec
    bias_ref[...] = bias


def scatter_small(share, core, y, x, vec, bias, low):
    depth = low.shape[1]
    half = D // (2 * depth)
    lane = lax.broadcasted_iota(jnp.int32, (8, D), 1)
    bias_lane = SMALL_LANES + core * half
    for n in range(4):
        place_y = 1 - y if n // 2 else y
        place_x = 1 - x if n % 2 else x
        for z in range(depth):
            shift = (4 * z + 2 * place_y + place_x) * share
            rows = jnp.where(lane < share, pltpu.roll(vec, lax.rem(D - shift, D), 1), 0.0)
            if n % 2 == 0:
                mine = pltpu.roll(bias, lax.rem(bias_lane - (2 * z + place_y) * half + D, D), 1)
                rows += jnp.where((lane >= bias_lane) & (lane < bias_lane + half), mine, 0.0)
            low[n, z] = rows.astype(BF16)


def attn_fwd(where, lengths, place, tokens, pieces, share, room):
    rows = tokens.shape[0]
    seqs = rows // SEQ
    low = jax.ShapeDtypeStruct((rows, D), BF16)
    return pl.pallas_call(
        functools.partial(attn_fwd_kernel, share),
        out_shape=(
            jax.ShapeDtypeStruct((rows, D), F32),
            jax.ShapeDtypeStruct((room * UNIT // 2, D), BF16),
            jax.ShapeDtypeStruct((room * UNIT // 2, D), BF16),
            low, low, low, low,
            jax.ShapeDtypeStruct((seqs * PAIRS, 2 * SEQ, SEQ), BF16),
            jax.ShapeDtypeStruct((4, pieces[0].shape[0], 4, share, D), BF16),
            jax.ShapeDtypeStruct((8, D), F32),
            jax.ShapeDtypeStruct((8, D), F32),
        ),
        in_specs=[SMEM] * 2 + [VMEM] + [ANY] * 9,
        out_specs=(VMEM,) * 11,
        scratch_shapes=[
            pltpu.VMEM(tokens.shape, BF16),
            pltpu.VMEM((4, pieces[0].shape[0], 8, D), BF16),
            pltpu.SemaphoreType.DMA((2, 8)),
            pltpu.SemaphoreType.DMA((5,)),
        ],
        compiler_params=pltpu.CompilerParams(vmem_limit_bytes=60 * 1024 * 1024),
        cost_estimate=pl.CostEstimate(flops=6 * 10**9, bytes_accessed=1, transcendentals=0),
        name="attn_fwd",
    )(where, lengths, place, tokens, *pieces)


def ffn_kernel(e, first, count, whole, tab_ref, tot_ref, where_ref, *rest):
    xs, cs, ws, b_ref = rest[0:8], rest[8:12], rest[12:12 + count], rest[12 + count]
    rest = rest[13 + count:] if first else rest[25 + count:]
    outs, mine_ref, other_ref, gb_ref = rest[:12], rest[12], rest[-15], rest[-14]
    xv, cv, wi, wb, gwi, gwb, xt, ct, ot, dt, in_sems, w_sems, out_sems = rest[-13:]
    y = where_ref[1]
    height = mine_ref.shape[1] // 2
    depth = D // height // 2
    size = cs[0].shape[0]
    weights, tokens = [], []
    for part, target in enumerate((wi, wb)):
        held = pl.ds(part * height, height)
        for n, piece in enumerate(ws):
            place = target if count == 1 else target.at[:, y if n == 0 else 1 - y]
            weights.append(pltpu.make_async_copy(piece.at[:, held], place, w_sems.at[n, part]))
    for n in range(8):
        part = pl.ds(n * (size // 2), size // 2)
        tokens.append(pltpu.make_async_copy(xs[n], xv.at[part], in_sems.at[0, n]))
    for n in range(4):
        tokens.append(pltpu.make_async_copy(cs[n], cv.at[pl.ds(n * size, size)], in_sems.at[1, n]))
    for copy in tokens + weights:
        copy.start()
    gwi[...] = jnp.zeros_like(gwi)
    gwb[...] = jnp.zeros_like(gwb)
    gb_ref[...] = jnp.zeros_like(gb_ref)
    for copy in tokens + weights:
        copy.wait()
    total = tot_ref[0]
    room = size // UNIT

    def pick(low, high, value, found):
        if high - low == 1:
            found(low)
            return
        middle = (low + high) // 2
        lax.cond(
            value < middle, lambda: pick(low, middle, value, found), lambda: pick(middle, high, value, found)
        )

    def send(t, u):
        unit = t * UNITS + u
        held = slice(u * UNIT, (u + 1) * UNIT)

        @pl.when(unit < total)
        def _():
            dst = tab_ref[unit]
            half_of = lax.div(2 * dst, room)

            def found(n):
                for m, (tile_ref, target, first_unit) in enumerate(
                    ((ot, outs[n // 2], n // 2 * room), (dt, outs[4 + n], n * (room // 2)))
                ):
                    rows = pl.ds(pl.multiple_of((dst - first_unit) * UNIT, UNIT), UNIT)
                    pltpu.make_async_copy(tile_ref.at[held], target.at[rows], out_sems.at[m, u]).start()

            pick(0, 8, half_of, found)

    def settle(t, u):
        @pl.when(t * UNITS + u < total)
        def _():
            held = slice(u * UNIT, (u + 1) * UNIT)
            for m, (tile_ref, target) in enumerate(((ot, outs[0]), (dt, outs[4]))):
                pltpu.make_async_copy(tile_ref.at[held], target.at[pl.ds(0, UNIT)], out_sems.at[m, u]).wait()

    def tile(t, carry):
        for u in range(UNITS):
            src = pl.multiple_of(tab_ref[t * UNITS + u] * UNIT, UNIT)
            xt[u * UNIT:(u + 1) * UNIT, :] = xv[pl.ds(src, UNIT), :]
            ct[u * UNIT:(u + 1) * UNIT, :] = cv[pl.ds(src, UNIT), :]
        left = (total - t * UNITS) * UNIT
        row = lax.broadcasted_iota(jnp.int32, (TILE, D), 0)
        part = jnp.where(row < left, ct[...], jnp.zeros_like(ct))
        pre = dot(xt[...], wi[...].reshape(D, -1)) + b_ref[e:e + 1, :]
        share = 0.5 * (1.0 + lax.erf(pre * INV_ROOT_TWO))
        act = (pre * share).astype(BF16)
        slope = share + pre * jnp.exp(-0.5 * pre * pre) * INV_ROOT_TAU

        @pl.when(t > 0)
        def _():
            for u in range(UNITS):
                settle(t - 1, u)

        ot[...] = dot(act, wb[...].reshape(-1, D)).astype(BF16)
        pre_grad = (dot_nt(part, wb[...].reshape(-1, D)) * slope).astype(BF16)
        dt[...] = dot_nt(pre_grad, wi[...].reshape(D, -1)).astype(BF16)
        for u in range(UNITS):
            send(t, u)
        gwb[...] += dot_tn(act, part)
        gwi[...] += dot_tn(xt[...], pre_grad)
        gb_ref[...] += jnp.sum(pre_grad.astype(F32), axis=0, keepdims=True)
        return carry

    tiles = (total + UNITS - 1) // UNITS
    lax.fori_loop(0, tiles, tile, 0)

    @pl.when(tiles > 0)
    def _():
        for u in range(UNITS):
            settle(tiles - 1, u)

    if whole:
        for b in range(2 * depth):
            mine_ref[b, :height, :] = gwi[b * height:(b + 1) * height, :].astype(BF16)
            mine_ref[b, height:, :] = gwb[b * height:(b + 1) * height, :].astype(BF16)
        return
    for z in range(depth):
        for y_of in range(2):
            rows = slice((2 * z + y_of) * height, (2 * z + y_of + 1) * height)
            for flag, target in ((y == y_of, mine_ref), (y != y_of, other_ref)):
                @pl.when(flag)
                def _():
                    target[z, :height, :] = gwi[rows, :].astype(BF16)
                    target[z, height:, :] = gwb[rows, :].astype(BF16)


def ffn(e, table, total, where, xs, cs, weights, bias, before, whole):
    size = cs[0].shape[0]
    first = before is None
    quarter = bias.shape[1]
    tokens = [jax.ShapeDtypeStruct((size, D), BF16)] * 4 + [jax.ShapeDtypeStruct((size // 2, D), BF16)] * 8
    height = weights[0].shape[-2] // 2
    blocked = (D // height, height, D) if len(weights) == 1 else (D // height // 2, 2, height, D)
    blocks = D // height
    grads = [jax.ShapeDtypeStruct((blocks if whole else blocks // 2, 2 * height, D), BF16)] * (1 if whole else 2)
    args = [table, total, where, *xs, *cs, *weights, bias] + ([] if first else list(before))
    return pl.pallas_call(
        functools.partial(ffn_kernel, e, first, len(weights), whole),
        out_shape=(*tokens, *grads, jax.ShapeDtypeStruct((1, quarter), F32)),
        in_specs=[SMEM] * 3 + [ANY] * (12 + len(weights)) + [VMEM] + [ANY] * (0 if first else 12),
        out_specs=(ANY,) * 12 + (VMEM,) * (1 + len(grads)),
        scratch_shapes=[
            pltpu.VMEM((4 * size, D), BF16),
            pltpu.VMEM((4 * size, D), BF16),
            pltpu.VMEM(blocked, BF16),
            pltpu.VMEM(blocked, BF16),
            pltpu.VMEM((D, quarter), F32),
            pltpu.VMEM((quarter, D), F32),
            pltpu.VMEM((TILE, D), BF16),
            pltpu.VMEM((TILE, D), BF16),
            pltpu.VMEM((TILE, D), BF16),
            pltpu.VMEM((TILE, D), BF16),
            pltpu.SemaphoreType.DMA((2, 8)),
            pltpu.SemaphoreType.DMA((len(weights), 2)),
            pltpu.SemaphoreType.DMA((2, UNITS)),
        ],
        input_output_aliases={} if first else {16 + len(weights) + i: i for i in range(12)},
        compiler_params=pltpu.CompilerParams(vmem_limit_bytes=60 * 1024 * 1024),
        cost_estimate=SMALL,
        name="ffn",
    )(*args)


def attn_bwd_kernel(share, where_ref, vec_ref, hot_ref, place_ref, bias_a, bias_b, bias_c, *rest):
    far, outs, held = rest[:11], rest[11:20], rest[20:31]
    gtok_ref, keeps, sends = outs[0], outs[1:5], outs[5:9]
    mg, mxg, dq, dk, dv, gw, gvec_ref, small, sems, out_sems = rest[31:]
    core, y, x = where_ref[0], where_ref[1], where_ref[2]
    leaving = []
    copies = [pltpu.make_async_copy(a, b, sems.at[n]) for n, (a, b) in enumerate(zip(far, held))]
    for copy in copies:
        copy.start()
    dx_a, dx_b, mid, cot, mixed, w_ref, q_ref, k_ref, v_ref, probs_ref, tok = held
    slot = lax.broadcasted_iota(jnp.int32, (tok.shape[0], 2 * dx_a.shape[0]), 1)
    unperm = jnp.where(slot == place_ref[...], 1.0, 0.0).astype(BF16)
    for copy in copies[:4]:
        copy.wait()
    norm2_grad = dot(unperm, jnp.concatenate([dx_a[...], dx_b[...]], axis=0))
    scaled_two, inverse_two = norm_stats(mid[...])
    gvec_ref[3:4, :] = jnp.sum(norm2_grad * scaled_two, axis=0, keepdims=True)
    gvec_ref[4:5, :] = jnp.sum(norm2_grad, axis=0, keepdims=True)
    mid_grad = cot[...].astype(F32) + norm_backward(norm2_grad * vec_ref[3:4, :], scaled_two, inverse_two)
    mg[...] = mid_grad
    branch = mid_grad.astype(BF16)
    gvec_ref[2:3, :] = jnp.sum(branch.astype(F32), axis=0, keepdims=True)
    gvec_ref[5:8, :] = dot(hot_ref[...], cot[...])[:3]
    for copy in copies[4:6]:
        copy.wait()

    def put(matrix, value):
        gw[matrix] = value.astype(BF16).reshape(gw.shape[1:])
        rows = pl.ds((matrix % 2) * (share + 8), share)
        for n in range(4):
            place = 2 * (1 - y if n // 2 else y) + (1 - x if n % 2 else x)
            for flag, target in ((core == matrix // 2, keeps[n]), (core != matrix // 2, sends[n])):
                def copy(target=target, place=place, n=n):
                    return pltpu.make_async_copy(gw.at[matrix, :, place], target.at[:, rows], out_sems.at[matrix, n])

                pl.when(flag)(lambda: copy().start())
                leaving.append((flag, copy))

    put(3, dot_tn(mixed[...], branch))
    mxg[...] = dot_nt(branch, w_ref[3].reshape(D, D)).astype(BF16)
    for copy in copies[6:]:
        copy.wait()
    seqs = tok.shape[0] // SEQ
    scale = HEAD_DIM ** -0.5
    for seq in range(seqs):
        rows = slice(seq * SEQ, (seq + 1) * SEQ)

        def step(pair, carry):
            cols = pl.ds(pl.multiple_of(pair * 128, 128), 128)
            probs = probs_ref[seq * PAIRS + pair]
            grads = two_heads(mxg[rows, cols])
            dv[rows, cols] = dot_tn(probs, grads).astype(BF16)
            prob_grad = dot_nt(grads, v_ref[rows, cols])
            wide = probs.astype(F32)
            inner = jnp.sum(wide * prob_grad, axis=-1, keepdims=True)
            score_grad = (wide * (prob_grad - inner)).astype(BF16)
            dq[rows, cols] = (merge_heads(dot(score_grad, k_ref[rows, cols])) * scale).astype(BF16)
            dk[rows, cols] = (dot_tn(score_grad, two_heads(q_ref[rows, cols])) * scale).astype(BF16)
            return carry

        lax.fori_loop(0, PAIRS, step, 0)
    scaled, inverse = norm_stats(tok[...].astype(F32))
    normed = (scaled * vec_ref[0:1, :] + vec_ref[1:2, :]).astype(BF16)
    put(0, dot_tn(normed, dq[...]))
    put(1, dot_tn(normed, dk[...]))
    put(2, dot_tn(normed, dv[...]))
    norm1_grad = dot_nt(dq[...], w_ref[0].reshape(D, D)) + dot_nt(dk[...], w_ref[1].reshape(D, D)) + dot_nt(dv[...], w_ref[2].reshape(D, D))
    gvec_ref[0:1, :] = jnp.sum(norm1_grad * scaled, axis=0, keepdims=True)
    gvec_ref[1:2, :] = jnp.sum(norm1_grad, axis=0, keepdims=True)
    bias = jnp.concatenate([bias_a[...], bias_b[...], bias_c[...], jnp.zeros((5, D), F32)], axis=0)
    scatter_small(share, core, y, x, gvec_ref[...], bias, small)
    for n in range(4):
        for m, target in enumerate((keeps[n], sends[n])):
            copy = pltpu.make_async_copy(small.at[n], target.at[:, pl.ds(share, 8)], out_sems.at[4 + m, n])
            copy.start()
            leaving.append((None, copy))
    gtok_ref[...] = (mg[...] + norm_backward(norm1_grad * vec_ref[0:1, :], scaled, inverse)).astype(BF16)
    for flag, copy in leaving:
        if flag is None:
            copy.wait()
        else:
            pl.when(flag)(lambda copy=copy: copy().wait())


def attn_bwd(share, where, vec, hot, place, bias_grads, far):
    rows = far[-1].shape[0]
    depth = D // share // 4
    part = jax.ShapeDtypeStruct((depth, 2 * share + 8, D), BF16)
    return pl.pallas_call(
        functools.partial(attn_bwd_kernel, share),
        out_shape=(jax.ShapeDtypeStruct((rows, D), BF16),) + (part,) * 8,
        in_specs=[SMEM] + [VMEM] * 6 + [ANY] * 11,
        out_specs=(VMEM,) + (ANY,) * 8,
        scratch_shapes=[pltpu.VMEM(item.shape, item.dtype) for item in far]
        + [pltpu.VMEM((rows, D), F32)] + [pltpu.VMEM((rows, D), BF16)] * 4
        + [
            pltpu.VMEM((4, depth, 4, share, D), BF16),
            pltpu.VMEM((8, D), F32),
            pltpu.VMEM((4, depth, 8, D), BF16),
            pltpu.SemaphoreType.DMA((11,)),
            pltpu.SemaphoreType.DMA((6, 4)),
        ],
        compiler_params=pltpu.CompilerParams(vmem_limit_bytes=60 * 1024 * 1024),
        cost_estimate=SMALL,
        name="attn_bwd",
    )(where, vec, hot, place, *bias_grads, *far)


def swap(value, axis):
    return lax.ppermute(value, axis, [(0, 1), (1, 0)])


def diagonal(value):
    return lax.ppermute(value, ("y", "x"), [(i, 3 - i) for i in range(4)])


def after_kernel(*refs):
    pass


def after(value, *others):
    return pl.pallas_call(
        after_kernel,
        out_shape=jax.ShapeDtypeStruct(value.shape, value.dtype),
        in_specs=[ANY] * (1 + len(others)),
        out_specs=ANY,
        input_output_aliases={0: 0},
        cost_estimate=SMALL,
        name="after",
    )(value, *others)


def ordered(mine, other, index, axis):
    first = jnp.where(index == 0, mine, other)
    second = jnp.where(index == 0, other, mine)
    return jnp.stack([first, second], axis=axis)


def spread(block, count, *wait):
    copies = jnp.broadcast_to(block[None], (count,) + block.shape)
    return lax.all_to_all(after(copies, *wait) if wait else copies, "z", 0, 0, tiled=True)


def halves(value, index, axis):
    mine = lax.dynamic_index_in_dim(value, index, axis, keepdims=False)
    other = lax.dynamic_index_in_dim(value, 1 - index, axis, keepdims=False)
    return mine, other


def running(values, axis):
    steps = [lax.index_in_dim(values, 0, axis, keepdims=False)]
    for i in range(1, values.shape[axis]):
        steps.append(steps[-1] + lax.index_in_dim(values, i, axis, keepdims=False))
    return jnp.stack(steps, axis=axis)


def add_low(a, b):
    return (a.astype(F32) + b.astype(F32)).astype(BF16)


def body(outer, depth, tokens, modality, lengths, ln1_gain, ln1_bias, w_qkv, w_out, out_bias, ln2_gain, ln2_bias,
         w_in, in_bias, w_back, back_bias, cotangent):
    rows = tokens.shape[0]
    share = w_qkv.shape[0]
    hidden = in_bias.shape[1]
    half = hidden // 2
    planes = 2 * depth
    core = lax.axis_index("c")
    y = lax.axis_index("y")
    x = lax.axis_index("x")

    hot = modality.astype(F32)
    before = jnp.arange(rows, dtype=jnp.int32)
    triangle = (before[None, :] < before[:, None]).astype(BF16)
    rank = dot(triangle, hot.astype(BF16))
    counts = jnp.sum(modality, axis=0)
    units = (counts + UNIT - 1) // UNIT
    starts = running(units, 0) - units
    place = jnp.sum(hot * (rank + (starts * UNIT).astype(F32)[None, :]), axis=1).astype(jnp.int32)
    room = rows // UNIT + EXPERTS - 1
    slots = jnp.arange(room * UNIT, dtype=jnp.int32)
    perm = (slots[:, None] == place[None, :]).astype(BF16)
    unperm = (place[:, None] == slots[None, :]).astype(BF16)
    cs = dot(perm, cotangent).astype(BF16)

    parts = [w_qkv[:, :D], w_qkv[:, D:2 * D], w_qkv[:, 2 * D:], w_out]
    mat_a = jnp.where(core == 0, parts[0], parts[2])
    mat_b = jnp.where(core == 0, parts[1], parts[3])
    small = jnp.stack([ln1_gain, ln1_bias, out_bias, ln2_gain, ln2_bias, back_bias[0], back_bias[1], back_bias[2]])
    small = jnp.pad(small, ((0, 0), (0, SMALL_LANES - share)))
    small = jnp.concatenate([small, jnp.pad(in_bias, ((0, 5), (0, D - SMALL_LANES - hidden)))], axis=1)
    message = jnp.concatenate([mat_a, small, mat_b], axis=0)
    cut = share + 8
    first = after(spread(message, depth), cs)
    near = [first, swap(first, "x"), swap(first, "y"), diagonal(first)]
    pieces = near + [swap(piece, "c") for piece in near]
    def four(value):
        beside = swap(value, "x")
        return [value, beside, swap(value, "c"), swap(beside, "c")]

    units_all = jnp.stack(four(units.astype(F32))).astype(jnp.int32)
    starts_all = running(units_all, 1) - units_all + (jnp.arange(4, dtype=jnp.int32) * room)[:, None]
    ends = running(units_all, 0)
    begins = ends - units_all
    totals = ends[3]
    index = jnp.arange(4 * rows // UNIT + UNITS, dtype=jnp.int32)[:, None, None]
    inside = (index >= begins[None]) & (index < ends[None])
    table = jnp.sum(jnp.where(inside, starts_all[None] + index - begins[None], 0), axis=1).T

    cs_all = four(after(cs, near[3]))

    columns = w_in.reshape(EXPERTS, share, planes, 2, 2, half)
    columns = lax.dynamic_index_in_dim(columns, core, 4, keepdims=False)
    in_mine, in_other = halves(columns, x, 3)
    in_mine = in_mine.reshape(EXPERTS, share, planes * half)
    in_other = in_other.reshape(EXPERTS, share, planes * half)
    in_pair = ordered(in_mine, swap(in_other, "x"), x, 1).reshape(EXPERTS, 2 * share, planes * half)
    back_mine = lax.dynamic_slice_in_dim(w_back, core * half, half, 1)
    block = [jnp.concatenate([in_pair[e], back_mine[e]], axis=0) for e in range(EXPERTS)]
    blocks = (planes, 2 * share + half, D)
    beside = swap(jnp.concatenate([in_mine[2], back_mine[2]], axis=0), "y")
    beside_in = ordered(beside[:share], diagonal(in_other[2]), x, 0).reshape(2 * share, planes * half)
    beside = jnp.concatenate([beside_in, beside[share:]], axis=0)
    first_in = spread(block[0], depth, pieces[4])
    second_in = spread(block[1], depth, *near[1:])
    third = lax.all_gather(after(ordered(block[2], beside, y, 0), *near[1:]), "z", axis=0).reshape(blocks)

    where = jnp.stack([core, y, x]).astype(jnp.int32)
    middle, *xs, q, k, v, mixed, probs, weights, vec, bias_mine = attn_fwd(
        where, lengths, after(place[None, :], first_in), tokens, pieces, share, room
    )
    xs_all = [item for pair in zip(*(four(part) for part in xs)) for item in pair]

    state = None
    grads, bias_grads = [None] * EXPERTS, [None] * EXPERTS
    second_in = after(second_in, xs_all[2])
    experts = [[first_in, swap(first_in, "y")], [second_in, swap(second_in, "y")], [third]]
    for e in range(EXPERTS):
        *results, bias_grads[e] = ffn(
            e, table[e], totals[e][None], where, xs_all, cs_all, experts[e], bias_mine, state, e != 2
        )
        state, grads[e] = results[:12], results[12:]
    used = (jnp.sum(units) * UNIT).astype(jnp.int32)

    def pair_sums(own, beside, across, corner):
        beside = add_low(beside, swap(corner, "c"))
        return add_low(own, swap(across, "c")), beside

    def home(own, beside, first=0):
        total = own.astype(F32) + swap(beside, "x").astype(F32)
        line = slots[first:first + own.shape[0], None]
        return jnp.where(line < used, total, 0.0).astype(BF16)

    def scatter_z(parts):
        return lax.all_to_all(parts.reshape(depth, -1, D), "z", 0, 0, tiled=True)

    last = scatter_z(grads[1][0])
    other_sum = swap(grads[2][1], "y")
    shard_low = lax.psum_scatter(grads[0][0], ("z", "y"), scatter_dimension=0)
    dx_pairs = [pair_sums(*state[4 + part::2]) for part in range(2)]
    out_pair = pair_sums(*state[:4])
    dxs = [home(*pair, part * room * UNIT // 2) for part, pair in enumerate(dx_pairs)]
    dxs[0] = after(dxs[0], *out_pair)

    hot_rows = jnp.pad(jnp.transpose(modality.astype(BF16)), ((0, 5), (0, 0)))
    grad_tokens, *parts = attn_bwd(
        share, where, vec, hot_rows, place[:, None], bias_grads,
        (*dxs, middle, cotangent, mixed, weights, q, k, v, probs, tokens),
    )
    outs = home(*out_pair)
    output = (middle + dot(unperm, outs) + dot(hot.astype(BF16), vec[5:8].astype(BF16))).astype(BF16)

    summed = [add_low(parts[n], swap(parts[4 + n], "c")) for n in (3, 1, 2, 0)]
    summed[0] = after(summed[0], shard_low)
    moved = [diagonal(summed[0]), swap(summed[1], "x"), swap(summed[2], "y"), summed[3]]
    part = (moved[0].astype(F32) + moved[1].astype(F32) + moved[2].astype(F32) + moved[3].astype(F32)).astype(BF16)
    last = jnp.sum(after(last, summed[3]).astype(F32), axis=0).reshape(2, -1, D)
    mine, other = halves(last, y, 0)
    last = mine + swap(other.astype(BF16), "y").astype(F32)
    other_sum = scatter_z(add_low(after(grads[2][0], grad_tokens), other_sum))
    shards = [shard_low.astype(F32), last, jnp.sum(other_sum.astype(F32), axis=0)]
    done = lax.all_to_all(part, "z", 0, 0, tiled=True)
    done = jnp.sum(done.astype(F32), axis=0)
    small = done[share:cut]
    done_low = done.astype(BF16)
    pair = jnp.stack([done_low[:share], done_low[cut:]])
    away = swap(pair, "c")
    grad_q = jnp.where(core == 0, pair[0], away[0])
    grad_k = jnp.where(core == 0, pair[1], away[1])
    grad_v = jnp.where(core == 0, away[0], pair[0])
    grad_o = jnp.where(core == 0, away[1], pair[1])
    grad_w_qkv = jnp.concatenate([grad_q, grad_k, grad_v], axis=1)

    shards = jnp.stack(shards).astype(BF16)
    in_mine, in_other = halves(shards[:, :2 * share].reshape(EXPERTS, 2, share, D), x, 1)
    in_pair = ordered(in_mine, swap(in_other, "x"), x, 2)
    in_pair_c, back_c = swap(in_pair, "c"), swap(shards[:, 2 * share:], "c")
    grad_w_in = ordered(in_pair, in_pair_c, core, 3)
    grad_w_in = grad_w_in.reshape(EXPERTS, share, 2, 2, planes, half)
    grad_w_in = jnp.transpose(grad_w_in, (0, 1, 4, 2, 3, 5)).reshape(EXPERTS, share, 2 * planes * hidden)
    grad_w_back = ordered(shards[:, 2 * share:], back_c, core, 1).reshape(EXPERTS, hidden, D)

    result = (
        small[0, :share], small[1, :share], grad_w_qkv, grad_o, small[2, :share], small[3, :share], small[4, :share],
        grad_w_in, small[:EXPERTS, SMALL_LANES:SMALL_LANES + hidden], grad_w_back, small[5:8, :share],
    )
    if outer > 1:
        result = tuple(lax.psum(item.astype(BF16), "ro") for item in result)
    return (output, grad_tokens) + tuple(item.astype(F32) for item in result)


def solution(mesh):
    reps, shards = mesh.shape["rep"], mesh.shape["fsdp"]
    grid = Mesh(mesh.devices.reshape(reps // 2, 2, shards // 4, 2, 2), ("ro", "c", "z", "y", "x"))
    fsdp = ("z", "y", "x")
    every = ("ro", "c", "z", "y", "x")
    vector, matrix, stack, lines = P(fsdp), P(fsdp, None), P(None, fsdp, None), P(None, fsdp)
    placed = (
        P(every, None), P(every, None), P(every), vector, vector, matrix, matrix, vector, vector, vector,
        stack, lines, stack, lines, P(every, None),
    )
    out = (
        P(every, None), P(every, None), vector, vector, matrix, matrix, vector, vector, vector,
        stack, lines, stack, lines,
    )
    return jax.shard_map(
        functools.partial(body, reps // 2, shards // 4), mesh=grid, in_specs=placed, out_specs=out, check_vma=False
    )
```

time: 399 us -> 351 us (0.88)
  waiting for transfers between devices: 145 us -> 103 us
  between operations: 4.6 us -> 19.2 us
  local copies, waits for them, and re-layouts: 39.8 us -> 29.1 us
  starting transfers between devices: 68.8 us -> 59.1 us
    all_to_all x7 -> x5, waiting for transfers between devices: 40.4 us -> 8.7 us  [the longest x3 8.69 us: spread(): lax.all_to_all(after(copies, *wait) if wait else copies, 'z', 0, 0, tiled...]
    all_to_all x7 -> x5, starting transfers between devices: 35.8 us -> 22 us  [the longest x3 13.4 us: spread(): lax.all_to_all(after(copies, *wait) if wait else copies, 'z', 0, 0, tiled...]
    ppermute x34 -> x43, waiting for transfers between devices: 89.5 us -> 79.7 us  [swap(): return lax.ppermute(value, axis, [(0, 1), (1, 0)])]
    unnamed x68 -> x59, local copies, waits for them, and re-layouts: 10.3 us -> 5.06 us
    all_to_all x1, waiting for transfers between devices: 1.56 us -> 6.83 us  [body(): done = lax.all_to_all(part, 'z', 0, 0, tiled=True)]
    ppermute x2 -> x3, waiting for transfers between devices: 13 us -> 8.17 us  [diagonal(): return lax.ppermute(value, ('y', 'x'), [(i, 3 - i) for i in range(4)])]
    pallas_call x4, Pallas kernels: 70.1 us -> 74.6 us  [the longest x3 52.1 us: ffn(): pl.pallas_call(functools.partial(ffn_kernel, e, first, len(weights), whol...]
    broadcast_in_dim x4 -> x3, local copies, waits for them, and re-layouts: 7.21 us -> 3.17 us  [spread(): copies = jnp.broadcast_to(block[None], (count,) + block.shape)]
  transfers between devices with their start and end apart: 44 -> 54, of which waited for: 16 -> 19; matrix products, arithmetic and copies ran while one was open for 16% -> 15% of each run, Pallas kernels for 23% -> 27%
where the time goes in v2:
time: 351 us; the launch traced here: 345 us
  waiting for transfers between devices  103 us (29%)
  Pallas kernels  93.2 us (27%)
  starting transfers between devices  59.1 us (17%)
  other arithmetic  35.4 us (10%)
  local copies, waits for them, and re-layouts  29.1 us (8%)
  between operations  19.2 us (5%)
  matrix products  5.21 us (1%)
    ppermute x43, waiting for transfers between devices, swap(): return lax.ppermute(value, axis, [(0, 1), (1, 0)])  79.7 us
    pallas_call x3, Pallas kernels, ffn(): pl.pallas_call(functools.partial(ffn_kernel, e, first, len(weights), whol...  52.1 us
    ppermute x43, starting transfers between devices, swap(): return lax.ppermute(value, axis, [(0, 1), (1, 0)])  25.7 us
    pallas_call x1, Pallas kernels, attn_bwd(): pl.pallas_call(functools.partial(attn_bwd_kernel, share), out_shape=(jax....  22.5 us
    pallas_call x1, Pallas kernels, attn_fwd(): pl.pallas_call(functools.partial(attn_fwd_kernel, share), out_shape=(jax....  18.6 us
    convert_element_type x8, other arithmetic, add_low(): return (a.astype(F32) + b.astype(F32)).astype(BF16)  14 us
    all_to_all x3, starting transfers between devices, spread(): lax.all_to_all(after(copies, *wait) if wait else copies, 'z', 0, 0, tiled...  13.4 us
    all_to_all x3, waiting for transfers between devices, spread(): lax.all_to_all(after(copies, *wait) if wait else copies, 'z', 0, 0, tiled...  8.69 us
  transfers between devices with their start and end apart: 54, of which 19 were waited for; matrix products, arithmetic and copies ran while one was open for 15% of the time, Pallas kernels for 27%

profile of v2, /device:TPU:0, one launch (start us, length us, event | category | flops | bytes accessed | tf_op | source)
XLA Modules:
  0.0 344.7 jit_solution(519712427029734140)
XLA Ops:
  11.4 6.3 %all-to-all-start = ((bf16[4,104,768]{2,1,0:T(8,128)(2,1)}), bf16[4,104,768]{2,1,0:T(8,128)(2,1)S(1)}, u32[]{:S(2)}, u32[]{:S(2)}) async-start(bf16[4,104,768]{2,1,0:T(8,128)(2,1)} %broadcast_in_dim.37), calls=%async_computation | async-start | bytes 1277952 | tf_op jit(solution)/shard_map/all_to_all | solution.py:503
  21.0 2.4 collective-permute-start.21
  30.8 1.5 convolution_convert_fusion.refs_1_.refs_0_
  32.3 2.4 all-to-all-done.refs_0_
  35.7 2.5 collective-permute-start.4
  41.4 3.5 %all-to-all-start.1 = ((bf16[4,192,768]{2,1,0:T(8,128)(2,1)}), bf16[4,192,768]{2,1,0:T(8,128)(2,1)S(1)}, u32[]{:S(2)}, u32[]{:S(2)}) async-start(bf16[4,192,768]{2,1,0:T(8,128)(2,1)} %after.12), calls=%async_computation.1 | async-start | bytes 2359296 | tf_op jit(solution)/shard_map/all_to_all | solution.py:503
  46.0 8.2 %collective-permute-done.4.rest_3_.refs_1_.refs_3_ = bf16[4,104,768]{2,1,0:T(8,128)(2,1)} collective-permute-done((bf16[4,104,768]{2,1,0:T(8,128)(2,1)}, bf16[4,104,768]{2,1,0:T(8,128)(2,1)}, u32[]{:S(2)}, u32[]{:S(2)}) %collective-permute-start.4) | collective-permute-done | bytes 639008 | tf_op jit(solution)/shard_map/ppermute | solution.py:476
  54.2 13.3 %collective-permute-done.3.rest_2_.refs_2_ = bf16[4,104,768]{2,1,0:T(8,128)(2,1)} collective-permute-done((bf16[4,104,768]{2,1,0:T(8,128)(2,1)}, bf16[4,104,768]{2,1,0:T(8,128)(2,1)}, u32[]{:S(2)}, u32[]{:S(2)}) %collective-permute-start.3) | collective-permute-done | bytes 639008 | tf_op jit(solution)/shard_map/ppermute | solution.py:472
  67.7 1.6 collective-permute-start.17
  71.7 1.8 all-to-all-done.1.refs_1_.rest_12_
  73.6 3.5 %all-to-all-start.2 = ((bf16[4,192,768]{2,1,0:T(8,128)(2,1)}), bf16[4,192,768]{2,1,0:T(8,128)(2,1)S(1)}, u32[]{:S(2)}, u32[]{:S(2)}) async-start(bf16[4,192,768]{2,1,0:T(8,128)(2,1)} %after.16), calls=%async_computation.2 | async-start | bytes 2359296 | tf_op jit(solution)/shard_map/all_to_all | solution.py:503
  78.2 1.5 collective-permute-start.8
  79.7 9.3 %collective-permute-done.8 = f32[3]{0:T(128)S(1)} collective-permute-done((f32[3]{0:T(128)S(1)}, f32[3]{0:T(128)S(1)}, u32[]{:S(2)}, u32[]{:S(2)}) %collective-permute-start.8) | collective-permute-done | bytes 44 | tf_op jit(solution)/shard_map/ppermute | solution.py:472
  90.9 1.4 collective-permute-start.23
  92.3 18.6 %attn_fwd.1 = (f32[512,768]{1,0:T(8,128)}, bf16[272,768]{1,0:T(8,128)(2,1)}, bf16[272,768]{1,0:T(8,128)(2,1)}, bf16[512,768]{1,0:T(8,128)(2,1)}, bf16[512,768]{1...) custom-call(s32[3]{0:T(128)} %pad_add_fusion.1.where_ref, ...), custom_call_target="tpu_custom_call" | custom-call | flops 6000000000 | bytes 1 | tf_op jit(solution)/shard_map/attn_fwd/pallas_call | solution.py:185
  113.9 9.8 %collective-permute-done.11.refs_1_.rest_2_ = bf16[272,768]{1,0:T(8,128)(2,1)S(1)} collective-permute-done((bf16[272,768]{1,0:T(8,128)(2,1)}, bf16[272,768]{1,0:T(8,128)(2,1)S(1)}, u32[]{:S(2)}, u32[]{:S(2)}) %collective-permute-start.11) | collective-permute-done | bytes 417824 | tf_op jit(solution)/shard_map/ppermute | solution.py:472
  123.7 7.9 %collective-permute-done.12.rest_3_ = bf16[272,768]{1,0:T(8,128)(2,1)S(1)} collective-permute-done((bf16[272,768]{1,0:T(8,128)(2,1)}, bf16[272,768]{1,0:T(8,128)(2,1)S(1)}, u32[]{:S(2)}, u32[]{:S(2)}) %collective-permute-start.12) | collective-permute-done | bytes 417824 | tf_op jit(solution)/shard_map/ppermute | solution.py:472
  131.8 4.5 %all-to-all-done.2.refs_0_ = bf16[4,192,768]{2,1,0:T(8,128)(2,1)S(1)} async-done(((bf16[4,192,768]{2,1,0:T(8,128)(2,1)}), bf16[4,192,768]{2,1,0:T(8,128)(2,1)S(1)}, u32[]{:S(2)}, u32[]{:S(2)}) %all-to-all-start.2) | async-done | bytes 1179680 | tf_op jit(solution)/shard_map/all_to_all | solution.py:503
  137.3 1.5 collective-permute-start.22
  140.7 17.1 %ffn.3 = (bf16[544,768]{1,0:T(8,128)(2,1)}, bf16[544,768]{1,0:T(8,128)(2,1)}, bf16[544,768]{1,0:T(8,128)(2,1)}, bf16[544,768]{1,0:T(8,128)(2,1)}, bf16[272,768]{...) custom-call(s32[144]{0:T(256)} %bitcast.170, ...), custom_call_target="tpu_custom_call" | custom-call | flops 1 | bytes 1 | tf_op jit(solution)/shard_map/ffn/pallas_call | solution.py:336
  157.9 6.4 %collective-permute-done.22.rest_13_ = bf16[4,192,768]{2,1,0:T(8,128)(2,1)S(1)} collective-permute-done((bf16[4,192,768]{2,1,0:T(8,128)(2,1)}, bf16[4,192,768]{2,1,0:T(8,128)(2,1)S(1)}, u32[]{:S(2)}, u32[]{:S(2)}) %collective-permute-start.22) | collective-permute-done | bytes 1179680 | tf_op jit(solution)/shard_map/ppermute | solution.py:472
  165.3 17.5 %ffn.4 = (bf16[544,768]{1,0:T(8,128)(2,1)}, bf16[544,768]{1,0:T(8,128)(2,1)}, bf16[544,768]{1,0:T(8,128)(2,1)}, bf16[544,768]{1,0:T(8,128)(2,1)}, bf16[272,768]{...) custom-call(s32[144]{0:T(256)} %bitcast.169, ...), custom_call_target="tpu_custom_call", output_to_operand_aliasing={{0}: (18, {}), {1}: (19, {}), {2}: (20, {}), {3}: (21, {}),... | custom-call | flops 1 | bytes 1 | tf_op jit(solution)/shard_map/ffn/pallas_call | solution.py:336
  182.8 3.6 %all-to-all-start.4 = ((bf16[4,384,768]{2,1,0:T(8,128)(2,1)}), bf16[4,384,768]{2,1,0:T(8,128)(2,1)S(1)}, u32[]{:S(2)}, u32[]{:S(2)}) async-start(bf16[4,384,768]{2,1,0:T(8,128)(2,1)} %bitcast.145), calls=%async_computation.5 | async-start | bytes 4718592 | tf_op jit(solution)/shard_map/all_to_all | solution.py:617
  187.1 17.5 %ffn.5 = (bf16[544,768]{1,0:T(8,128)(2,1)}, bf16[544,768]{1,0:T(8,128)(2,1)}, bf16[544,768]{1,0:T(8,128)(2,1)}, bf16[544,768]{1,0:T(8,128)(2,1)}, bf16[272,768]{...) custom-call(s32[144]{0:T(256)} %bitcast.168, ...), custom_call_target="tpu_custom_call", output_to_operand_aliasing={{0}: (17, {}), {1}: (18, {}), {2}: (19, {}), {3}: (20, {}),... | custom-call | flops 1 | bytes 1 | tf_op jit(solution)/shard_map/ffn/pallas_call | solution.py:336
  208.5 1.5 collective-permute-start.29
  210.8 1.4 collective-permute-start.42
  212.2 2.3 add_convert_fusion.2.refs_1_
  215.1 5.9 %collective-permute-done.29 = bf16[272,768]{1,0:T(8,128)(2,1)S(1)} collective-permute-done((bf16[272,768]{1,0:T(8,128)(2,1)S(1)}, bf16[272,768]{1,0:T(8,128)(2,1)S(1)}, u32[]{:S(2)}, u32[]{:S(2)}) %collective-permute-start.29) | collective-permute-done | bytes 417824 | tf_op jit(solution)/shard_map/ppermute | solution.py:472
  223.7 5.5 %collective-permute-done.32 = bf16[272,768]{1,0:T(8,128)(2,1)} collective-permute-done((bf16[272,768]{1,0:T(8,128)(2,1)}, bf16[272,768]{1,0:T(8,128)(2,1)}, u32[]{:S(2)}, u32[]{:S(2)}) %collective-permute-start.32) | collective-permute-done | bytes 417824 | tf_op jit(solution)/shard_map/ppermute | solution.py:472
  229.2 2.0 select_convert_fusion.2.rest_1_
  231.2 22.5 %attn_bwd.1 = (bf16[512,768]{1,0:T(8,128)(2,1)}, bf16[4,104,768]{2,1,0:T(8,128)(2,1)}, bf16[4,104,768]{2,1,0:T(8,128)(2,1)}, bf16[4,104,768]{2,1,0:T(8,128)(2,1)...) custom-call(s32[3]{0:T(128)} %pad_add_fusion.1.where_ref, ...), custom_call_target="tpu_custom_call" | custom-call | flops 1 | bytes 1 | tf_op jit(solution)/shard_map/attn_bwd/pallas_call | solution.py:451
  254.8 3.0 add_convert_fusion
  257.8 2.2 add_convert_fusion.6
  259.9 1.5 collective-permute-start.36
  262.4 1.4 collective-permute-start.38
  263.8 4.9 %all-to-all-start.5 = ((bf16[4,192,768]{2,1,0:T(8,128)(2,1)}), bf16[4,192,768]{2,1,0:T(8,128)(2,1)S(1)}, u32[]{:S(2)}, u32[]{:S(2)}) async-start(bf16[4,192,768]{2,1,0:T(8,128)(2,1)} %add_convert_fusion), calls=%async_computation.6 | async-start | bytes 2359296 | tf_op jit(solution)/shard_map/all_to_all | solution.py:617
  268.7 2.3 add_convert_fusion.7.refs_0_
  273.2 4.3 %collective-permute-done.36 = bf16[4,104,768]{2,1,0:T(8,128)(2,1)} collective-permute-done((bf16[4,104,768]{2,1,0:T(8,128)(2,1)}, bf16[4,104,768]{2,1,0:T(8,128)(2,1)}, u32[]{:S(2)}, u32[]{:S(2)}) %collective-permute-start.36) | collective-permute-done | bytes 639008 | tf_op jit(solution)/shard_map/ppermute | solution.py:472
  277.5 15.0 %collective-permute-done.38 = bf16[4,104,768]{2,1,0:T(8,128)(2,1)} collective-permute-done((bf16[4,104,768]{2,1,0:T(8,128)(2,1)}, bf16[4,104,768]{2,1,0:T(8,128)(2,1)}, u32[]{:S(2)}, u32[]{:S(2)}) %collective-permute-start.38) | collective-permute-done | bytes 639008 | tf_op jit(solution)/shard_map/ppermute | solution.py:472
  292.5 3.1 add_convert_fusion.3
  295.6 2.1 convert_reduce_fusion
  298.5 1.4 collective-permute-start.41
  300.8 5.3 %all-to-all-start.3 = ((bf16[4,104,768]{2,1,0:T(8,128)(2,1)}), bf16[4,104,768]{2,1,0:T(8,128)(2,1)S(1)}, u32[]{:S(2)}, u32[]{:S(2)}) async-start(bf16[4,104,768]{2,1,0:T(8,128)(2,1)} %get-tuple-element.139), calls=%async_computation.4 | async-start | bytes 1277952 | tf_op jit(solution)/shard_map/all_to_all | solution.py:644
  308.4 2.1 fusion.1
  312.0 1.3 collective-permute-start.43
  314.8 6.8 %all-to-all-done.3 = bf16[4,104,768]{2,1,0:T(8,128)(2,1)S(1)} async-done(((bf16[4,104,768]{2,1,0:T(8,128)(2,1)}), bf16[4,104,768]{2,1,0:T(8,128)(2,1)S(1)}, u32[]{:S(2)}, u32[]{:S(2)}) %all-to-all-start.3) | async-done | bytes 639008 | tf_op jit(solution)/shard_map/all_to_all | solution.py:644
  329.4 3.0 convert_bitcast_fusion
  332.4 4.4 %reshape.440 = f32[3,48,3072]{2,1,0:T(8,128)} reshape(f32[3,48,8,2,2,96]{5,4,3,2,1,0:T(2,128)S(1)} %convert_bitcast_fusion) | data formatting | bytes 3538944 | tf_op jit(solution)/shard_map/convert_element_type | solution.py:671
  (232 shorter events, 56.5 us)
Async XLA Ops:
  11.4 23.3 %all-to-all-start = ((bf16[4,104,768]{2,1,0:T(8,128)(2,1)}), bf16[4,104,768]{2,1,0:T(8,128)(2,1)S(1)}, u32[]{:S(2)}, u32[]{:S(2)}) async-start(bf16[4,104,768]{2,1,0:T(8,128)(2,1)} %broadcast_in_dim.37), calls=%async_computation | async-start | bytes 1277952 | tf_op jit(solution)/shard_map/all_to_all | solution.py:503
  21.0 18.3 %collective-permute-start.21 = (bf16[48,768]{1,0:T(8,128)(2,1)}, bf16[48,768]{1,0:T(8,128)(2,1)}, u32[]{:S(2)}, u32[]{:S(2)}) collective-permute-start(bf16[48,768]{1,0:T(8,128)(2,1)} %squeeze.87), channel_id=1, source_target_pairs={{0,3},{1,2},{2,1},{3,0},{4,7},{5,6},{6,5},{7,4},{8,11},{9,10},{10,... | collective-permute-start | bytes 221192 | tf_op jit(solution)/shard_map/ppermute | solution.py:476
  23.6 8.7 %collective-permute-start = (bf16[3,48,768]{2,1,0:T(8,128)(2,1)S(1)}, bf16[3,48,768]{2,1,0:T(8,128)(2,1)S(1)}, u32[]{:S(2)}, u32[]{:S(2)}) collective-permute-start(bf16[3,48,768]{2,1,0:T(8,128)(2,1)S(1)} %reshape.435), channel_id=1, source_target_pairs={{0,1},{1,0},{2,3},{3,2},{4,5},{5,4},{6,7},{7,6},{8,9},{9,8},{10,11... | collective-permute-start | bytes 663560 | tf_op jit(solution)/shard_map/ppermute | solution.py:472
  25.6 10.0 %collective-permute-start.20 = (bf16[144,768]{1,0:T(8,128)(2,1)S(1)}, bf16[144,768]{1,0:T(8,128)(2,1)S(1)}, u32[]{:S(2)}, u32[]{:S(2)}) collective-permute-start(bf16[144,768]{1,0:T(8,128)(2,1)S(1)} %pad_maximum_fusion.7), channel_id=1, source_target_pairs={{0,2},{2,0},{1,3},{3,1},{4,6},{6,4},{5,7},{7,5},{8,10},{10,8},{9,1... | collective-permute-start | bytes 663560 | tf_op jit(solution)/shard_map/ppermute | solution.py:472
  35.6 4.6 %collective-permute-start.1 = (bf16[4,104,768]{2,1,0:T(8,128)(2,1)}, bf16[4,104,768]{2,1,0:T(8,128)(2,1)S(1)}, u32[]{:S(2)}, u32[]{:S(2)}) collective-permute-start(bf16[4,104,768]{2,1,0:T(8,128)(2,1)} %after.11.rest_0_), channel_id=1, source_target_pairs={{0,16},{16,0},{1,17},{17,1},{2,18},{18,2},{3,19},{19,3},{4,20},{20... | collective-permute-start | bytes 1916936 | tf_op jit(solution)/shard_map/ppermute | solution.py:472
  35.7 18.5 %collective-permute-start.4 = (bf16[4,104,768]{2,1,0:T(8,128)(2,1)}, bf16[4,104,768]{2,1,0:T(8,128)(2,1)}, u32[]{:S(2)}, u32[]{:S(2)}) collective-permute-start(bf16[4,104,768]{2,1,0:T(8,128)(2,1)} %after.11.rest_0_), channel_id=1, source_target_pairs={{0,3},{1,2},{2,1},{3,0},{4,7},{5,6},{6,5},{7,4},{8,11},{9,10},{10,... | collective-permute-start | bytes 1916936 | tf_op jit(solution)/shard_map/ppermute | solution.py:476
  38.2 29.3 %collective-permute-start.3 = (bf16[4,104,768]{2,1,0:T(8,128)(2,1)}, bf16[4,104,768]{2,1,0:T(8,128)(2,1)}, u32[]{:S(2)}, u32[]{:S(2)}) collective-permute-start(bf16[4,104,768]{2,1,0:T(8,128)(2,1)} %after.11.rest_0_), channel_id=1, source_target_pairs={{0,2},{2,0},{1,3},{3,1},{4,6},{6,4},{5,7},{7,5},{8,10},{10,8},{9,1... | collective-permute-start | bytes 1916936 | tf_op jit(solution)/shard_map/ppermute | solution.py:472
  38.7 28.8 %collective-permute-start.2 = (bf16[4,104,768]{2,1,0:T(8,128)(2,1)}, bf16[4,104,768]{2,1,0:T(8,128)(2,1)}, u32[]{:S(2)}, u32[]{:S(2)}) collective-permute-start(bf16[4,104,768]{2,1,0:T(8,128)(2,1)} %after.11.rest_0_), channel_id=1, source_target_pairs={{0,1},{1,0},{2,3},{3,2},{4,5},{5,4},{6,7},{7,6},{8,9},{9,8},{10,11... | collective-permute-start | bytes 1916936 | tf_op jit(solution)/shard_map/ppermute | solution.py:472
  41.4 32.1 %all-to-all-start.1 = ((bf16[4,192,768]{2,1,0:T(8,128)(2,1)}), bf16[4,192,768]{2,1,0:T(8,128)(2,1)S(1)}, u32[]{:S(2)}, u32[]{:S(2)}) async-start(bf16[4,192,768]{2,1,0:T(8,128)(2,1)} %after.12), calls=%async_computation.1 | async-start | bytes 2359296 | tf_op jit(solution)/shard_map/all_to_all | solution.py:503
  45.0 142.2 %all-gather.3.cloned.1.call-start = ((), (), s32[]{:S(2)}) async-start(), calls=%async_computation.8 | async-start | bytes 2949120 | tf_op jit(solution)/shard_map/all_gather | solution.py:588
  67.6 10.7 %collective-permute-start.9 = (f32[3]{0:T(128)S(1)}, f32[3]{0:T(128)S(1)}, u32[]{:S(2)}, u32[]{:S(2)}) collective-permute-start(f32[3]{0:T(128)S(1)} %get-tuple-element.192), channel_id=1, source_target_pairs={{0,16},{16,0},{1,17},{17,1},{2,18},{18,2},{3,19},{19,3},{4,20},{20... | collective-permute-start | bytes 44 | tf_op jit(solution)/shard_map/ppermute | solution.py:472
  67.7 22.8 %collective-permute-start.17 = (bf16[544,768]{1,0:T(8,128)(2,1)}, bf16[544,768]{1,0:T(8,128)(2,1)}, u32[]{:S(2)}, u32[]{:S(2)}) collective-permute-start(bf16[544,768]{1,0:T(8,128)(2,1)} %after.14.rest_8_), channel_id=1, source_target_pairs={{0,1},{1,0},{2,3},{3,2},{4,5},{5,4},{6,7},{7,6},{8,9},{9,8},{10,11... | collective-permute-start | bytes 2506760 | tf_op jit(solution)/shard_map/ppermute | solution.py:472
  69.8 21.0 %collective-permute-start.7 = (bf16[4,104,768]{2,1,0:T(8,128)(2,1)}, bf16[4,104,768]{2,1,0:T(8,128)(2,1)}, u32[]{:S(2)}, u32[]{:S(2)}) collective-permute-start(bf16[4,104,768]{2,1,0:T(8,128)(2,1)} %collective-permute-done.4.rest_3_.refs_1_.refs_3_), channel_id=1, source_target_pairs={{0,16},{16,0},{1,17},{17,1},{2,18},{18,2},{3,19},{19,3},{4,20},{20... | collective-permute-start | bytes 1916936 | tf_op jit(solution)/shard_map/ppermute | solution.py:472
  70.1 22.2 %collective-permute-start.6 = (bf16[4,104,768]{2,1,0:T(8,128)(2,1)}, bf16[4,104,768]{2,1,0:T(8,128)(2,1)}, u32[]{:S(2)}, u32[]{:S(2)}) collective-permute-start(bf16[4,104,768]{2,1,0:T(8,128)(2,1)} %collective-permute-done.3.rest_2_.refs_2_), channel_id=1, source_target_pairs={{0,16},{16,0},{1,17},{17,1},{2,18},{18,2},{3,19},{19,3},{4,20},{20... | collective-permute-start | bytes 1916936 | tf_op jit(solution)/shard_map/ppermute | solution.py:472
  70.4 21.9 %collective-permute-start.5 = (bf16[4,104,768]{2,1,0:T(8,128)(2,1)}, bf16[4,104,768]{2,1,0:T(8,128)(2,1)}, u32[]{:S(2)}, u32[]{:S(2)}) collective-permute-start(bf16[4,104,768]{2,1,0:T(8,128)(2,1)} %collective-permute-done.2.rest_1_.refs_1_), channel_id=1, source_target_pairs={{0,16},{16,0},{1,17},{17,1},{2,18},{18,2},{3,19},{19,3},{4,20},{20... | collective-permute-start | bytes 1916936 | tf_op jit(solution)/shard_map/ppermute | solution.py:472
  73.6 62.7 %all-to-all-start.2 = ((bf16[4,192,768]{2,1,0:T(8,128)(2,1)}), bf16[4,192,768]{2,1,0:T(8,128)(2,1)S(1)}, u32[]{:S(2)}, u32[]{:S(2)}) async-start(bf16[4,192,768]{2,1,0:T(8,128)(2,1)} %after.16), calls=%async_computation.2 | async-start | bytes 2359296 | tf_op jit(solution)/shard_map/all_to_all | solution.py:503
  77.1 193.9 %reduce-scatter.2.cloned.1.call-start = ((), (), s32[]{:S(2)}) async-start(), calls=%async_computation.7 | async-start | bytes 2654208 | tf_op jit(solution)/shard_map/reduce_scatter | solution.py:621
  78.2 10.8 %collective-permute-start.8 = (f32[3]{0:T(128)S(1)}, f32[3]{0:T(128)S(1)}, u32[]{:S(2)}, u32[]{:S(2)}) collective-permute-start(f32[3]{0:T(128)S(1)} %get-tuple-element.192), channel_id=1, source_target_pairs={{0,1},{1,0},{2,3},{3,2},{4,5},{5,4},{6,7},{7,6},{8,9},{9,8},{10,11... | collective-permute-start | bytes 44 | tf_op jit(solution)/shard_map/ppermute | solution.py:472
  90.3 22.9 %collective-permute-start.18 = (bf16[544,768]{1,0:T(8,128)(2,1)S(1)}, bf16[544,768]{1,0:T(8,128)(2,1)}, u32[]{:S(2)}, u32[]{:S(2)}) collective-permute-start(bf16[544,768]{1,0:T(8,128)(2,1)S(1)} %copy-done.1), channel_id=1, source_target_pairs={{0,16},{16,0},{1,17},{17,1},{2,18},{18,2},{3,19},{19,3},{4,20},{20... | collective-permute-start | bytes 2506760 | tf_op jit(solution)/shard_map/ppermute | solution.py:472
  90.5 22.9 %collective-permute-start.19 = (bf16[544,768]{1,0:T(8,128)(2,1)}, bf16[544,768]{1,0:T(8,128)(2,1)}, u32[]{:S(2)}, u32[]{:S(2)}) collective-permute-start(bf16[544,768]{1,0:T(8,128)(2,1)} %collective-permute-done.17.rest_9_), channel_id=1, source_target_pairs={{0,16},{16,0},{1,17},{17,1},{2,18},{18,2},{3,19},{19,3},{4,20},{20... | collective-permute-start | bytes 2506760 | tf_op jit(solution)/shard_map/ppermute | solution.py:472
  90.9 49.1 %collective-permute-start.23 = (bf16[4,192,768]{2,1,0:T(8,128)(2,1)}, bf16[4,192,768]{2,1,0:T(8,128)(2,1)}, u32[]{:S(2)}, u32[]{:S(2)}) collective-permute-start(bf16[4,192,768]{2,1,0:T(8,128)(2,1)} %copy-done.3), channel_id=1, source_target_pairs={{0,2},{2,0},{1,3},{3,1},{4,6},{6,4},{5,7},{7,5},{8,10},{10,8},{9,1... | collective-permute-start | bytes 3538952 | tf_op jit(solution)/shard_map/ppermute | solution.py:472
  110.9 12.8 %collective-permute-start.11 = (bf16[272,768]{1,0:T(8,128)(2,1)}, bf16[272,768]{1,0:T(8,128)(2,1)S(1)}, u32[]{:S(2)}, u32[]{:S(2)}) collective-permute-start(bf16[272,768]{1,0:T(8,128)(2,1)} %get-tuple-element.77.rest_0_), channel_id=1, source_target_pairs={{0,1},{1,0},{2,3},{3,2},{4,5},{5,4},{6,7},{7,6},{8,9},{9,8},{10,11... | collective-permute-start | bytes 1253384 | tf_op jit(solution)/shard_map/ppermute | solution.py:472
  111.8 19.9 %collective-permute-start.12 = (bf16[272,768]{1,0:T(8,128)(2,1)}, bf16[272,768]{1,0:T(8,128)(2,1)S(1)}, u32[]{:S(2)}, u32[]{:S(2)}) collective-permute-start(bf16[272,768]{1,0:T(8,128)(2,1)} %get-tuple-element.78.rest_1_), channel_id=1, source_target_pairs={{0,1},{1,0},{2,3},{3,2},{4,5},{5,4},{6,7},{7,6},{8,9},{9,8},{10,11... | collective-permute-start | bytes 1253384 | tf_op jit(solution)/shard_map/ppermute | solution.py:472
  113.1 24.1 %collective-permute-start.13 = (bf16[272,768]{1,0:T(8,128)(2,1)}, bf16[272,768]{1,0:T(8,128)(2,1)S(1)}, u32[]{:S(2)}, u32[]{:S(2)}) collective-permute-start(bf16[272,768]{1,0:T(8,128)(2,1)} %get-tuple-element.77.rest_0_), channel_id=1, source_target_pairs={{0,16},{16,0},{1,17},{17,1},{2,18},{18,2},{3,19},{19,3},{4,20},{20... | collective-permute-start | bytes 1253384 | tf_op jit(solution)/shard_map/ppermute | solution.py:472
  113.4 26.5 %collective-permute-start.14 = (bf16[272,768]{1,0:T(8,128)(2,1)}, bf16[272,768]{1,0:T(8,128)(2,1)S(1)}, u32[]{:S(2)}, u32[]{:S(2)}) collective-permute-start(bf16[272,768]{1,0:T(8,128)(2,1)} %get-tuple-element.78.rest_1_), channel_id=1, source_target_pairs={{0,16},{16,0},{1,17},{17,1},{2,18},{18,2},{3,19},{19,3},{4,20},{20... | collective-permute-start | bytes 1253384 | tf_op jit(solution)/shard_map/ppermute | solution.py:472
  123.7 16.2 %collective-permute-start.15 = (bf16[272,768]{1,0:T(8,128)(2,1)S(1)}, bf16[272,768]{1,0:T(8,128)(2,1)}, u32[]{:S(2)}, u32[]{:S(2)}) collective-permute-start(bf16[272,768]{1,0:T(8,128)(2,1)S(1)} %collective-permute-done.11.refs_1_.rest_2_), channel_id=1, source_target_pairs={{0,16},{16,0},{1,17},{17,1},{2,18},{18,2},{3,19},{19,3},{4,20},{20... | collective-permute-start | bytes 1253384 | tf_op jit(solution)/shard_map/ppermute | solution.py:472
  131.7 8.3 %collective-permute-start.16 = (bf16[272,768]{1,0:T(8,128)(2,1)S(1)}, bf16[272,768]{1,0:T(8,128)(2,1)}, u32[]{:S(2)}, u32[]{:S(2)}) collective-permute-start(bf16[272,768]{1,0:T(8,128)(2,1)S(1)} %collective-permute-done.12.rest_3_), channel_id=1, source_target_pairs={{0,16},{16,0},{1,17},{17,1},{2,18},{18,2},{3,19},{19,3},{4,20},{20... | collective-permute-start | bytes 1253384 | tf_op jit(solution)/shard_map/ppermute | solution.py:472
  137.3 27.0 %collective-permute-start.22 = (bf16[4,192,768]{2,1,0:T(8,128)(2,1)}, bf16[4,192,768]{2,1,0:T(8,128)(2,1)S(1)}, u32[]{:S(2)}, u32[]{:S(2)}) collective-permute-start(bf16[4,192,768]{2,1,0:T(8,128)(2,1)} %after.17.rest_12_), channel_id=1, source_target_pairs={{0,2},{2,0},{1,3},{3,1},{4,6},{6,4},{5,7},{7,5},{8,10},{10,8},{9,1... | collective-permute-start | bytes 3538952 | tf_op jit(solution)/shard_map/ppermute | solution.py:472
  182.8 81.0 %all-to-all-start.4 = ((bf16[4,384,768]{2,1,0:T(8,128)(2,1)}), bf16[4,384,768]{2,1,0:T(8,128)(2,1)S(1)}, u32[]{:S(2)}, u32[]{:S(2)}) async-start(bf16[4,384,768]{2,1,0:T(8,128)(2,1)} %bitcast.145), calls=%async_computation.5 | async-start | bytes 4718592 | tf_op jit(solution)/shard_map/all_to_all | solution.py:617
  204.7 6.1 %collective-permute-start.24 = (bf16[544,768]{1,0:T(8,128)(2,1)}, bf16[544,768]{1,0:T(8,128)(2,1)}, u32[]{:S(2)}, u32[]{:S(2)}) collective-permute-start(bf16[544,768]{1,0:T(8,128)(2,1)} %get-tuple-element.105), channel_id=1, source_target_pairs={{0,16},{16,0},{1,17},{17,1},{2,18},{18,2},{3,19},{19,3},{4,20},{20... | collective-permute-start | bytes 2506760 | tf_op jit(solution)/shard_map/ppermute | solution.py:472
  206.3 8.3 %collective-permute-start.27 = (bf16[272,768]{1,0:T(8,128)(2,1)}, bf16[272,768]{1,0:T(8,128)(2,1)S(1)}, u32[]{:S(2)}, u32[]{:S(2)}) collective-permute-start(bf16[272,768]{1,0:T(8,128)(2,1)} %get-tuple-element.113), channel_id=1, source_target_pairs={{0,16},{16,0},{1,17},{17,1},{2,18},{18,2},{3,19},{19,3},{4,20},{20... | collective-permute-start | bytes 1253384 | tf_op jit(solution)/shard_map/ppermute | solution.py:472
  206.7 17.0 %collective-permute-start.30 = (bf16[272,768]{1,0:T(8,128)(2,1)}, bf16[272,768]{1,0:T(8,128)(2,1)S(1)}, u32[]{:S(2)}, u32[]{:S(2)}) collective-permute-start(bf16[272,768]{1,0:T(8,128)(2,1)} %get-tuple-element.117), channel_id=1, source_target_pairs={{0,16},{16,0},{1,17},{17,1},{2,18},{18,2},{3,19},{19,3},{4,20},{20... | collective-permute-start | bytes 1253384 | tf_op jit(solution)/shard_map/ppermute | solution.py:472
  206.8 15.2 %collective-permute-start.25 = (bf16[544,768]{1,0:T(8,128)(2,1)}, bf16[544,768]{1,0:T(8,128)(2,1)S(1)}, u32[]{:S(2)}, u32[]{:S(2)}) collective-permute-start(bf16[544,768]{1,0:T(8,128)(2,1)} %get-tuple-element.107), channel_id=1, source_target_pairs={{0,16},{16,0},{1,17},{17,1},{2,18},{18,2},{3,19},{19,3},{4,20},{20... | collective-permute-start | bytes 2506760 | tf_op jit(solution)/shard_map/ppermute | solution.py:472
  208.5 12.6 %collective-permute-start.29 = (bf16[272,768]{1,0:T(8,128)(2,1)S(1)}, bf16[272,768]{1,0:T(8,128)(2,1)S(1)}, u32[]{:S(2)}, u32[]{:S(2)}) collective-permute-start(bf16[272,768]{1,0:T(8,128)(2,1)S(1)} %add_convert_fusion.10), channel_id=1, source_target_pairs={{0,1},{1,0},{2,3},{3,2},{4,5},{5,4},{6,7},{7,6},{8,9},{9,8},{10,11... | collective-permute-start | bytes 1253384 | tf_op jit(solution)/shard_map/ppermute | solution.py:472
  210.8 43.9 %collective-permute-start.42 = (bf16[4,192,768]{2,1,0:T(8,128)(2,1)}, bf16[4,192,768]{2,1,0:T(8,128)(2,1)}, u32[]{:S(2)}, u32[]{:S(2)}) collective-permute-start(bf16[4,192,768]{2,1,0:T(8,128)(2,1)} %get-tuple-element.138), channel_id=1, source_target_pairs={{0,2},{2,0},{1,3},{3,1},{4,6},{6,4},{5,7},{7,5},{8,10},{10,8},{9,1... | collective-permute-start | bytes 3538952 | tf_op jit(solution)/shard_map/ppermute | solution.py:472
  214.6 14.7 %collective-permute-start.32 = (bf16[272,768]{1,0:T(8,128)(2,1)}, bf16[272,768]{1,0:T(8,128)(2,1)}, u32[]{:S(2)}, u32[]{:S(2)}) collective-permute-start(bf16[272,768]{1,0:T(8,128)(2,1)} %add_convert_fusion.8), channel_id=1, source_target_pairs={{0,1},{1,0},{2,3},{3,2},{4,5},{5,4},{6,7},{7,6},{8,9},{9,8},{10,11... | collective-permute-start | bytes 1253384 | tf_op jit(solution)/shard_map/ppermute | solution.py:472
  253.8 7.6 %collective-permute-start.37 = (bf16[4,104,768]{2,1,0:T(8,128)(2,1)}, bf16[4,104,768]{2,1,0:T(8,128)(2,1)S(1)}, u32[]{:S(2)}, u32[]{:S(2)}) collective-permute-start(bf16[4,104,768]{2,1,0:T(8,128)(2,1)} %get-tuple-element.133), channel_id=1, source_target_pairs={{0,16},{16,0},{1,17},{17,1},{2,18},{18,2},{3,19},{19,3},{4,20},{20... | collective-permute-start | bytes 1916936 | tf_op jit(solution)/shard_map/ppermute | solution.py:472
  254.2 14.4 %collective-permute-start.33 = (bf16[4,104,768]{2,1,0:T(8,128)(2,1)}, bf16[4,104,768]{2,1,0:T(8,128)(2,1)}, u32[]{:S(2)}, u32[]{:S(2)}) collective-permute-start(bf16[4,104,768]{2,1,0:T(8,128)(2,1)} %get-tuple-element.128), channel_id=1, source_target_pairs={{0,16},{16,0},{1,17},{17,1},{2,18},{18,2},{3,19},{19,3},{4,20},{20... | collective-permute-start | bytes 1916936 | tf_op jit(solution)/shard_map/ppermute | solution.py:472
  254.3 18.8 %collective-permute-start.39 = (bf16[4,104,768]{2,1,0:T(8,128)(2,1)}, bf16[4,104,768]{2,1,0:T(8,128)(2,1)}, u32[]{:S(2)}, u32[]{:S(2)}) collective-permute-start(bf16[4,104,768]{2,1,0:T(8,128)(2,1)} %get-tuple-element.135), channel_id=1, source_target_pairs={{0,16},{16,0},{1,17},{17,1},{2,18},{18,2},{3,19},{19,3},{4,20},{20... | collective-permute-start | bytes 1916936 | tf_op jit(solution)/shard_map/ppermute | solution.py:472
  259.9 17.6 %collective-permute-start.36 = (bf16[4,104,768]{2,1,0:T(8,128)(2,1)}, bf16[4,104,768]{2,1,0:T(8,128)(2,1)}, u32[]{:S(2)}, u32[]{:S(2)}) collective-permute-start(bf16[4,104,768]{2,1,0:T(8,128)(2,1)} %add_convert_fusion.6), channel_id=1, source_target_pairs={{0,1},{1,0},{2,3},{3,2},{4,5},{5,4},{6,7},{7,6},{8,9},{9,8},{10,11... | collective-permute-start | bytes 1916936 | tf_op jit(solution)/shard_map/ppermute | solution.py:472
  262.4 30.1 %collective-permute-start.38 = (bf16[4,104,768]{2,1,0:T(8,128)(2,1)}, bf16[4,104,768]{2,1,0:T(8,128)(2,1)}, u32[]{:S(2)}, u32[]{:S(2)}) collective-permute-start(bf16[4,104,768]{2,1,0:T(8,128)(2,1)} %add_convert_fusion.5), channel_id=1, source_target_pairs={{0,2},{2,0},{1,3},{3,1},{4,6},{6,4},{5,7},{7,5},{8,10},{10,8},{9,1... | collective-permute-start | bytes 1916936 | tf_op jit(solution)/shard_map/ppermute | solution.py:472
  263.8 36.1 %all-to-all-start.5 = ((bf16[4,192,768]{2,1,0:T(8,128)(2,1)}), bf16[4,192,768]{2,1,0:T(8,128)(2,1)S(1)}, u32[]{:S(2)}, u32[]{:S(2)}) async-start(bf16[4,192,768]{2,1,0:T(8,128)(2,1)} %add_convert_fusion), calls=%async_computation.6 | async-start | bytes 2359296 | tf_op jit(solution)/shard_map/all_to_all | solution.py:617
  271.0 21.5 %collective-permute-start.34 = (bf16[4,104,768]{2,1,0:T(8,128)(2,1)}, bf16[4,104,768]{2,1,0:T(8,128)(2,1)}, u32[]{:S(2)}, u32[]{:S(2)}) collective-permute-start(bf16[4,104,768]{2,1,0:T(8,128)(2,1)} %after.19), channel_id=1, source_target_pairs={{0,3},{1,2},{2,1},{3,0},{4,7},{5,6},{6,5},{7,4},{8,11},{9,10},{10,... | collective-permute-start | bytes 1916936 | tf_op jit(solution)/shard_map/ppermute | solution.py:476
  272.1 36.1 %collective-permute-start.26 = (bf16[544,768]{1,0:T(8,128)(2,1)S(1)}, bf16[544,768]{1,0:T(8,128)(2,1)}, u32[]{:S(2)}, u32[]{:S(2)}) collective-permute-start(bf16[544,768]{1,0:T(8,128)(2,1)S(1)} %copy-done.15), channel_id=1, source_target_pairs={{0,1},{1,0},{2,3},{3,2},{4,5},{5,4},{6,7},{7,6},{8,9},{9,8},{10,11... | collective-permute-start | bytes 2506760 | tf_op jit(solution)/shard_map/ppermute | solution.py:472
  298.5 7.8 %collective-permute-start.41 = (bf16[192,768]{1,0:T(8,128)(2,1)}, bf16[192,768]{1,0:T(8,128)(2,1)}, u32[]{:S(2)}, u32[]{:S(2)}) collective-permute-start(bf16[192,768]{1,0:T(8,128)(2,1)} %fusion.14), channel_id=1, source_target_pairs={{0,2},{2,0},{1,3},{3,1},{4,6},{6,4},{5,7},{7,5},{8,10},{10,8},{9,1... | collective-permute-start | bytes 884744 | tf_op jit(solution)/shard_map/ppermute | solution.py:472
  300.8 20.8 %all-to-all-start.3 = ((bf16[4,104,768]{2,1,0:T(8,128)(2,1)}), bf16[4,104,768]{2,1,0:T(8,128)(2,1)S(1)}, u32[]{:S(2)}, u32[]{:S(2)}) async-start(bf16[4,104,768]{2,1,0:T(8,128)(2,1)} %get-tuple-element.139), calls=%async_computation.4 | async-start | bytes 1277952 | tf_op jit(solution)/shard_map/all_to_all | solution.py:644
  307.5 4.4 %collective-permute-start.45 = (bf16[3,96,768]{2,1,0:T(8,128)(2,1)S(1)}, bf16[3,96,768]{2,1,0:T(8,128)(2,1)S(1)}, u32[]{:S(2)}, u32[]{:S(2)}) collective-permute-start(bf16[3,96,768]{2,1,0:T(8,128)(2,1)S(1)} %slice.237), channel_id=1, source_target_pairs={{0,16},{16,0},{1,17},{17,1},{2,18},{18,2},{3,19},{19,3},{4,20},{20... | collective-permute-start | bytes 1327112 | tf_op jit(solution)/shard_map/ppermute | solution.py:472
  312.0 11.6 %collective-permute-start.43 = (bf16[3,48,768]{2,1,0:T(8,128)(2,1)S(1)}, bf16[3,48,768]{2,1,0:T(8,128)(2,1)S(1)}, u32[]{:S(2)}, u32[]{:S(2)}) collective-permute-start(bf16[3,48,768]{2,1,0:T(8,128)(2,1)S(1)} %dynamic-slice_bitcast_fusion), channel_id=1, source_target_pairs={{0,1},{1,0},{2,3},{3,2},{4,5},{5,4},{6,7},{7,6},{8,9},{9,8},{10,11... | collective-permute-start | bytes 663560 | tf_op jit(solution)/shard_map/ppermute | solution.py:472
  (34 other events, 186.8 us)
Sparse Core Ops, SparseCore 0:
  67.7 73.6 all-gather.2
Sparse Core Ops, SparseCore 1:
  158.0 84.7 reduce-scatter.1

commit v3 on v2

--- a/solution.py
+++ b/solution.py
@@ -129,7 +129,7 @@
             mixed_ref[rows, cols] = merge_heads(dot(probs, v_ref[rows, cols])).astype(BF16)
             return carry
 
-        lax.fori_loop(0, PAIRS, step, 0)
+        lax.fori_loop(0, PAIRS, step, 0, unroll=3)
     middle = tok[...].astype(F32) + dot(mixed_ref[...], weight(3)) + vec_ref[2:3, :]
     mid_ref[...] = middle
     scaled_two, _ = norm_stats(middle)
@@ -420,7 +420,7 @@
             dk[rows, cols] = (dot_tn(score_grad, two_heads(q_ref[rows, cols])) * scale).astype(BF16)
             return carry
 
-        lax.fori_loop(0, PAIRS, step, 0)
+        lax.fori_loop(0, PAIRS, step, 0, unroll=3)
     scaled, inverse = norm_stats(tok[...].astype(F32))
     normed = (scaled * vec_ref[0:1, :] + vec_ref[1:2, :]).astype(BF16)
     put(0, dot_tn(normed, dq[...]))
@@ -596,6 +596,7 @@
     state = None
     grads, bias_grads = [None] * EXPERTS, [None] * EXPERTS
     second_in = after(second_in, xs_all[2])
+    first_in = after(first_in, xs[0])
     experts = [[first_in, swap(first_in, "y")], [second_in, swap(second_in, "y")], [third]]
     for e in range(EXPERTS):
         *results, bias_grads[e] = ffn(
@@ -622,7 +623,7 @@
     dx_pairs = [pair_sums(*state[4 + part::2]) for part in range(2)]
     out_pair = pair_sums(*state[:4])
     dxs = [home(*pair, part * room * UNIT // 2) for part, pair in enumerate(dx_pairs)]
-    dxs[0] = after(dxs[0], *out_pair)
+    dxs[0] = after(dxs[0], out_pair[1])
 
     hot_rows = jnp.pad(jnp.transpose(modality.astype(BF16)), ((0, 5), (0, 0)))
     grad_tokens, *parts = attn_bwd(

time: 351 us -> 348 us (level)
  Pallas kernels: 93.2 us -> 87.9 us
  waiting for transfers between devices: 103 us -> 107 us
    convert_element_type x8 -> x7, other arithmetic: 14 us -> 11.6 us  [add_low(): return (a.astype(F32) + b.astype(F32)).astype(BF16)]
  transfers between devices with their start and end apart: 54 -> 54, of which waited for: 19 -> 17; matrix products, arithmetic and copies ran while one was open for 15% -> 14% of each run, Pallas kernels for 27% -> 26%
where the time goes in v3:
time: 348 us; the launch traced here: 342 us
  waiting for transfers between devices  107 us (31%)
  Pallas kernels  87.9 us (25%)
  starting transfers between devices  60 us (17%)
  other arithmetic  33 us (9%)
  local copies, waits for them, and re-layouts  29.2 us (8%)
  between operations  19.3 us (6%)
  matrix products  5.65 us (2%)
    ppermute x43, waiting for transfers between devices, swap(): return lax.ppermute(value, axis, [(0, 1), (1, 0)])  80.3 us
    pallas_call x3, Pallas kernels, ffn(): pl.pallas_call(functools.partial(ffn_kernel, e, first, len(weights), whol...  51.9 us
    ppermute x43, starting transfers between devices, swap(): return lax.ppermute(value, axis, [(0, 1), (1, 0)])  26.3 us
    pallas_call x1, Pallas kernels, attn_bwd(): pl.pallas_call(functools.partial(attn_bwd_kernel, share), out_shape=(jax....  20.5 us
    pallas_call x1, Pallas kernels, attn_fwd(): pl.pallas_call(functools.partial(attn_fwd_kernel, share), out_shape=(jax....  15.5 us
    all_to_all x3, starting transfers between devices, spread(): lax.all_to_all(after(copies, *wait) if wait else copies, 'z', 0, 0, tiled...  13.4 us
    all_to_all x3, waiting for transfers between devices, spread(): lax.all_to_all(after(copies, *wait) if wait else copies, 'z', 0, 0, tiled...  11.9 us
    convert_element_type x7, other arithmetic, add_low(): return (a.astype(F32) + b.astype(F32)).astype(BF16)  11.6 us
  transfers between devices with their start and end apart: 54, of which 17 were waited for; matrix products, arithmetic and copies ran while one was open for 14% of the time, Pallas kernels for 26%

profile of v3, /device:TPU:0, one launch (start us, length us, event | category | flops | bytes accessed | tf_op | source)
XLA Modules:
  0.0 342.2 jit_solution(949763349699654841)
XLA Ops:
  11.4 6.3 %all-to-all-start = ((bf16[4,104,768]{2,1,0:T(8,128)(2,1)}), bf16[4,104,768]{2,1,0:T(8,128)(2,1)S(1)}, u32[]{:S(2)}, u32[]{:S(2)}) async-start(bf16[4,104,768]{2,1,0:T(8,128)(2,1)} %broadcast_in_dim.37), calls=%async_computation | async-start | bytes 1277952 | tf_op jit(solution)/shard_map/all_to_all | solution.py:503
  21.0 2.4 collective-permute-start.21
  30.8 1.5 convolution_convert_fusion.refs_1_.refs_0_
  32.3 2.4 all-to-all-done.refs_0_
  35.7 2.5 collective-permute-start.4
  41.4 3.5 %all-to-all-start.1 = ((bf16[4,192,768]{2,1,0:T(8,128)(2,1)}), bf16[4,192,768]{2,1,0:T(8,128)(2,1)S(1)}, u32[]{:S(2)}, u32[]{:S(2)}) async-start(bf16[4,192,768]{2,1,0:T(8,128)(2,1)} %after.13), calls=%async_computation.1 | async-start | bytes 2359296 | tf_op jit(solution)/shard_map/all_to_all | solution.py:503
  46.0 8.2 %collective-permute-done.4.rest_3_.refs_1_.refs_3_ = bf16[4,104,768]{2,1,0:T(8,128)(2,1)} collective-permute-done((bf16[4,104,768]{2,1,0:T(8,128)(2,1)}, bf16[4,104,768]{2,1,0:T(8,128)(2,1)}, u32[]{:S(2)}, u32[]{:S(2)}) %collective-permute-start.4) | collective-permute-done | bytes 639008 | tf_op jit(solution)/shard_map/ppermute | solution.py:476
  54.2 13.3 %collective-permute-done.3.rest_2_.refs_2_ = bf16[4,104,768]{2,1,0:T(8,128)(2,1)} collective-permute-done((bf16[4,104,768]{2,1,0:T(8,128)(2,1)}, bf16[4,104,768]{2,1,0:T(8,128)(2,1)}, u32[]{:S(2)}, u32[]{:S(2)}) %collective-permute-start.3) | collective-permute-done | bytes 639008 | tf_op jit(solution)/shard_map/ppermute | solution.py:472
  67.6 1.6 collective-permute-start.17
  71.9 1.7 all-to-all-done.1.refs_1_.refs_0_
  73.6 3.5 %all-to-all-start.2 = ((bf16[4,192,768]{2,1,0:T(8,128)(2,1)}), bf16[4,192,768]{2,1,0:T(8,128)(2,1)S(1)}, u32[]{:S(2)}, u32[]{:S(2)}) async-start(bf16[4,192,768]{2,1,0:T(8,128)(2,1)} %after.17), calls=%async_computation.2 | async-start | bytes 2359296 | tf_op jit(solution)/shard_map/all_to_all | solution.py:503
  78.2 1.5 collective-permute-start.8
  79.7 8.7 %collective-permute-done.8 = f32[3]{0:T(128)S(1)} collective-permute-done((f32[3]{0:T(128)S(1)}, f32[3]{0:T(128)S(1)}, u32[]{:S(2)}, u32[]{:S(2)}) %collective-permute-start.8) | collective-permute-done | bytes 44 | tf_op jit(solution)/shard_map/ppermute | solution.py:472
  90.1 15.5 %attn_fwd.1 = (f32[512,768]{1,0:T(8,128)}, bf16[272,768]{1,0:T(8,128)(2,1)}, bf16[272,768]{1,0:T(8,128)(2,1)}, bf16[512,768]{1,0:T(8,128)(2,1)}, bf16[512,768]{1...) custom-call(s32[3]{0:T(128)} %pad_add_fusion.1.where_ref, ...), custom_call_target="tpu_custom_call" | custom-call | flops 6000000000 | bytes 1 | tf_op jit(solution)/shard_map/attn_fwd/pallas_call | solution.py:185
  105.6 1.6 collective-permute-start.23
  110.2 17.6 %collective-permute-done.12.rest_3_ = bf16[272,768]{1,0:T(8,128)(2,1)} collective-permute-done((bf16[272,768]{1,0:T(8,128)(2,1)}, bf16[272,768]{1,0:T(8,128)(2,1)}, u32[]{:S(2)}, u32[]{:S(2)}) %collective-permute-start.12) | collective-permute-done | bytes 417824 | tf_op jit(solution)/shard_map/ppermute | solution.py:472
  128.5 7.8 %all-to-all-done.2.refs_0_ = bf16[4,192,768]{2,1,0:T(8,128)(2,1)S(1)} async-done(((bf16[4,192,768]{2,1,0:T(8,128)(2,1)}), bf16[4,192,768]{2,1,0:T(8,128)(2,1)S(1)}, u32[]{:S(2)}, u32[]{:S(2)}) %all-to-all-start.2) | async-done | bytes 1179680 | tf_op jit(solution)/shard_map/all_to_all | solution.py:503
  137.3 1.5 collective-permute-start.22
  140.7 17.3 %ffn.3 = (bf16[544,768]{1,0:T(8,128)(2,1)}, bf16[544,768]{1,0:T(8,128)(2,1)}, bf16[544,768]{1,0:T(8,128)(2,1)}, bf16[544,768]{1,0:T(8,128)(2,1)}, bf16[272,768]{...) custom-call(s32[144]{0:T(256)} %bitcast.170, ...), custom_call_target="tpu_custom_call" | custom-call | flops 1 | bytes 1 | tf_op jit(solution)/shard_map/ffn/pallas_call | solution.py:336
  158.0 6.3 %collective-permute-done.22.rest_13_ = bf16[4,192,768]{2,1,0:T(8,128)(2,1)S(1)} collective-permute-done((bf16[4,192,768]{2,1,0:T(8,128)(2,1)}, bf16[4,192,768]{2,1,0:T(8,128)(2,1)S(1)}, u32[]{:S(2)}, u32[]{:S(2)}) %collective-permute-start.22) | collective-permute-done | bytes 1179680 | tf_op jit(solution)/shard_map/ppermute | solution.py:472
  165.3 17.5 %ffn.4 = (bf16[544,768]{1,0:T(8,128)(2,1)}, bf16[544,768]{1,0:T(8,128)(2,1)}, bf16[544,768]{1,0:T(8,128)(2,1)}, bf16[544,768]{1,0:T(8,128)(2,1)}, bf16[272,768]{...) custom-call(s32[144]{0:T(256)} %bitcast.169, ...), custom_call_target="tpu_custom_call", output_to_operand_aliasing={{0}: (18, {}), {1}: (19, {}), {2}: (20, {}), {3}: (21, {}),... | custom-call | flops 1 | bytes 1 | tf_op jit(solution)/shard_map/ffn/pallas_call | solution.py:336
  182.8 3.7 %all-to-all-start.4 = ((bf16[4,384,768]{2,1,0:T(8,128)(2,1)}), bf16[4,384,768]{2,1,0:T(8,128)(2,1)S(1)}, u32[]{:S(2)}, u32[]{:S(2)}) async-start(bf16[4,384,768]{2,1,0:T(8,128)(2,1)} %bitcast.145), calls=%async_computation.5 | async-start | bytes 4718592 | tf_op jit(solution)/shard_map/all_to_all | solution.py:618
  186.5 17.1 %ffn.5 = (bf16[544,768]{1,0:T(8,128)(2,1)}, bf16[544,768]{1,0:T(8,128)(2,1)}, bf16[544,768]{1,0:T(8,128)(2,1)}, bf16[544,768]{1,0:T(8,128)(2,1)}, bf16[272,768]{...) custom-call(s32[144]{0:T(256)} %bitcast.168, ...), custom_call_target="tpu_custom_call", output_to_operand_aliasing={{0}: (17, {}), {1}: (18, {}), {2}: (19, {}), {3}: (20, {}),... | custom-call | flops 1 | bytes 1 | tf_op jit(solution)/shard_map/ffn/pallas_call | solution.py:336
  207.6 1.5 collective-permute-start.29
  209.2 1.5 collective-permute-start.42
  212.2 7.9 %collective-permute-done.29 = bf16[272,768]{1,0:T(8,128)(2,1)S(1)} collective-permute-done((bf16[272,768]{1,0:T(8,128)(2,1)S(1)}, bf16[272,768]{1,0:T(8,128)(2,1)S(1)}, u32[]{:S(2)}, u32[]{:S(2)}) %collective-permute-start.29) | collective-permute-done | bytes 417824 | tf_op jit(solution)/shard_map/ppermute | solution.py:472
  222.8 5.4 %collective-permute-done.32 = bf16[272,768]{1,0:T(8,128)(2,1)S(1)} collective-permute-done((bf16[272,768]{1,0:T(8,128)(2,1)}, bf16[272,768]{1,0:T(8,128)(2,1)S(1)}, u32[]{:S(2)}, u32[]{:S(2)}) %collective-permute-start.32) | collective-permute-done | bytes 417824 | tf_op jit(solution)/shard_map/ppermute | solution.py:472
  228.2 2.0 select_convert_fusion.2.rest_1_
  230.2 20.5 %attn_bwd.1 = (bf16[512,768]{1,0:T(8,128)(2,1)}, bf16[4,104,768]{2,1,0:T(8,128)(2,1)}, bf16[4,104,768]{2,1,0:T(8,128)(2,1)}, bf16[4,104,768]{2,1,0:T(8,128)(2,1)...) custom-call(s32[3]{0:T(128)} %pad_add_fusion.1.where_ref, ...), custom_call_target="tpu_custom_call" | custom-call | flops 1 | bytes 1 | tf_op jit(solution)/shard_map/attn_bwd/pallas_call | solution.py:451
  251.8 3.0 add_convert_fusion
  254.8 2.1 add_convert_fusion.6
  257.0 1.5 collective-permute-start.36
  259.4 1.4 collective-permute-start.38
  260.9 5.1 %all-to-all-start.5 = ((bf16[4,192,768]{2,1,0:T(8,128)(2,1)}), bf16[4,192,768]{2,1,0:T(8,128)(2,1)S(1)}, u32[]{:S(2)}, u32[]{:S(2)}) async-start(bf16[4,192,768]{2,1,0:T(8,128)(2,1)} %add_convert_fusion), calls=%async_computation.6 | async-start | bytes 2359296 | tf_op jit(solution)/shard_map/all_to_all | solution.py:618
  265.9 2.3 add_convert_fusion.7.refs_0_
  270.5 4.0 %collective-permute-done.36 = bf16[4,104,768]{2,1,0:T(8,128)(2,1)} collective-permute-done((bf16[4,104,768]{2,1,0:T(8,128)(2,1)}, bf16[4,104,768]{2,1,0:T(8,128)(2,1)}, u32[]{:S(2)}, u32[]{:S(2)}) %collective-permute-start.36) | collective-permute-done | bytes 639008 | tf_op jit(solution)/shard_map/ppermute | solution.py:472
  274.5 15.0 %collective-permute-done.38 = bf16[4,104,768]{2,1,0:T(8,128)(2,1)} collective-permute-done((bf16[4,104,768]{2,1,0:T(8,128)(2,1)}, bf16[4,104,768]{2,1,0:T(8,128)(2,1)}, u32[]{:S(2)}, u32[]{:S(2)}) %collective-permute-start.38) | collective-permute-done | bytes 639008 | tf_op jit(solution)/shard_map/ppermute | solution.py:472
  289.5 3.1 add_convert_fusion.3
  292.6 2.1 convert_reduce_fusion
  295.5 1.4 collective-permute-start.41
  297.9 5.4 %all-to-all-start.3 = ((bf16[4,104,768]{2,1,0:T(8,128)(2,1)}), bf16[4,104,768]{2,1,0:T(8,128)(2,1)S(1)}, u32[]{:S(2)}, u32[]{:S(2)}) async-start(bf16[4,104,768]{2,1,0:T(8,128)(2,1)} %get-tuple-element.139), calls=%async_computation.4 | async-start | bytes 1277952 | tf_op jit(solution)/shard_map/all_to_all | solution.py:645
  305.6 2.6 fusion.1
  308.2 1.3 fusion
  309.6 1.3 collective-permute-start.43
  311.0 1.3 copy.96
  312.3 6.8 %all-to-all-done.3 = bf16[4,104,768]{2,1,0:T(8,128)(2,1)S(1)} async-done(((bf16[4,104,768]{2,1,0:T(8,128)(2,1)}), bf16[4,104,768]{2,1,0:T(8,128)(2,1)S(1)}, u32[]{:S(2)}, u32[]{:S(2)}) %all-to-all-start.3) | async-done | bytes 639008 | tf_op jit(solution)/shard_map/all_to_all | solution.py:645
  326.9 3.0 convert_bitcast_fusion
  329.9 4.4 %reshape.440 = f32[3,48,3072]{2,1,0:T(8,128)} reshape(f32[3,48,8,2,2,96]{5,4,3,2,1,0:T(2,128)S(1)} %convert_bitcast_fusion) | data formatting | bytes 3538944 | tf_op jit(solution)/shard_map/convert_element_type | solution.py:672
  (230 shorter events, 54.0 us)
Async XLA Ops:
  11.4 23.3 %all-to-all-start = ((bf16[4,104,768]{2,1,0:T(8,128)(2,1)}), bf16[4,104,768]{2,1,0:T(8,128)(2,1)S(1)}, u32[]{:S(2)}, u32[]{:S(2)}) async-start(bf16[4,104,768]{2,1,0:T(8,128)(2,1)} %broadcast_in_dim.37), calls=%async_computation | async-start | bytes 1277952 | tf_op jit(solution)/shard_map/all_to_all | solution.py:503
  21.0 18.3 %collective-permute-start.21 = (bf16[48,768]{1,0:T(8,128)(2,1)}, bf16[48,768]{1,0:T(8,128)(2,1)}, u32[]{:S(2)}, u32[]{:S(2)}) collective-permute-start(bf16[48,768]{1,0:T(8,128)(2,1)} %squeeze.87), channel_id=1, source_target_pairs={{0,3},{1,2},{2,1},{3,0},{4,7},{5,6},{6,5},{7,4},{8,11},{9,10},{10,... | collective-permute-start | bytes 221192 | tf_op jit(solution)/shard_map/ppermute | solution.py:476
  23.6 8.7 %collective-permute-start = (bf16[3,48,768]{2,1,0:T(8,128)(2,1)S(1)}, bf16[3,48,768]{2,1,0:T(8,128)(2,1)S(1)}, u32[]{:S(2)}, u32[]{:S(2)}) collective-permute-start(bf16[3,48,768]{2,1,0:T(8,128)(2,1)S(1)} %reshape.435), channel_id=1, source_target_pairs={{0,1},{1,0},{2,3},{3,2},{4,5},{5,4},{6,7},{7,6},{8,9},{9,8},{10,11... | collective-permute-start | bytes 663560 | tf_op jit(solution)/shard_map/ppermute | solution.py:472
  25.6 10.0 %collective-permute-start.20 = (bf16[144,768]{1,0:T(8,128)(2,1)S(1)}, bf16[144,768]{1,0:T(8,128)(2,1)S(1)}, u32[]{:S(2)}, u32[]{:S(2)}) collective-permute-start(bf16[144,768]{1,0:T(8,128)(2,1)S(1)} %pad_maximum_fusion.7), channel_id=1, source_target_pairs={{0,2},{2,0},{1,3},{3,1},{4,6},{6,4},{5,7},{7,5},{8,10},{10,8},{9,1... | collective-permute-start | bytes 663560 | tf_op jit(solution)/shard_map/ppermute | solution.py:472
  35.6 4.6 %collective-permute-start.1 = (bf16[4,104,768]{2,1,0:T(8,128)(2,1)}, bf16[4,104,768]{2,1,0:T(8,128)(2,1)S(1)}, u32[]{:S(2)}, u32[]{:S(2)}) collective-permute-start(bf16[4,104,768]{2,1,0:T(8,128)(2,1)} %after.12.rest_0_), channel_id=1, source_target_pairs={{0,16},{16,0},{1,17},{17,1},{2,18},{18,2},{3,19},{19,3},{4,20},{20... | collective-permute-start | bytes 1916936 | tf_op jit(solution)/shard_map/ppermute | solution.py:472
  35.7 18.5 %collective-permute-start.4 = (bf16[4,104,768]{2,1,0:T(8,128)(2,1)}, bf16[4,104,768]{2,1,0:T(8,128)(2,1)}, u32[]{:S(2)}, u32[]{:S(2)}) collective-permute-start(bf16[4,104,768]{2,1,0:T(8,128)(2,1)} %after.12.rest_0_), channel_id=1, source_target_pairs={{0,3},{1,2},{2,1},{3,0},{4,7},{5,6},{6,5},{7,4},{8,11},{9,10},{10,... | collective-permute-start | bytes 1916936 | tf_op jit(solution)/shard_map/ppermute | solution.py:476
  38.2 29.3 %collective-permute-start.3 = (bf16[4,104,768]{2,1,0:T(8,128)(2,1)}, bf16[4,104,768]{2,1,0:T(8,128)(2,1)}, u32[]{:S(2)}, u32[]{:S(2)}) collective-permute-start(bf16[4,104,768]{2,1,0:T(8,128)(2,1)} %after.12.rest_0_), channel_id=1, source_target_pairs={{0,2},{2,0},{1,3},{3,1},{4,6},{6,4},{5,7},{7,5},{8,10},{10,8},{9,1... | collective-permute-start | bytes 1916936 | tf_op jit(solution)/shard_map/ppermute | solution.py:472
  38.7 28.8 %collective-permute-start.2 = (bf16[4,104,768]{2,1,0:T(8,128)(2,1)}, bf16[4,104,768]{2,1,0:T(8,128)(2,1)}, u32[]{:S(2)}, u32[]{:S(2)}) collective-permute-start(bf16[4,104,768]{2,1,0:T(8,128)(2,1)} %after.12.rest_0_), channel_id=1, source_target_pairs={{0,1},{1,0},{2,3},{3,2},{4,5},{5,4},{6,7},{7,6},{8,9},{9,8},{10,11... | collective-permute-start | bytes 1916936 | tf_op jit(solution)/shard_map/ppermute | solution.py:472
  41.4 32.1 %all-to-all-start.1 = ((bf16[4,192,768]{2,1,0:T(8,128)(2,1)}), bf16[4,192,768]{2,1,0:T(8,128)(2,1)S(1)}, u32[]{:S(2)}, u32[]{:S(2)}) async-start(bf16[4,192,768]{2,1,0:T(8,128)(2,1)} %after.13), calls=%async_computation.1 | async-start | bytes 2359296 | tf_op jit(solution)/shard_map/all_to_all | solution.py:503
  45.0 141.5 %all-gather.3.cloned.1.call-start = ((), (), s32[]{:S(2)}) async-start(), calls=%async_computation.8 | async-start | bytes 2949120 | tf_op jit(solution)/shard_map/all_gather | solution.py:588
  67.6 22.3 %collective-permute-start.17 = (bf16[544,768]{1,0:T(8,128)(2,1)}, bf16[544,768]{1,0:T(8,128)(2,1)}, u32[]{:S(2)}, u32[]{:S(2)}) collective-permute-start(bf16[544,768]{1,0:T(8,128)(2,1)} %after.15.rest_8_), channel_id=1, source_target_pairs={{0,1},{1,0},{2,3},{3,2},{4,5},{5,4},{6,7},{7,6},{8,9},{9,8},{10,11... | collective-permute-start | bytes 2506760 | tf_op jit(solution)/shard_map/ppermute | solution.py:472
  69.1 9.1 %collective-permute-start.9 = (f32[3]{0:T(128)S(1)}, f32[3]{0:T(128)S(1)}, u32[]{:S(2)}, u32[]{:S(2)}) collective-permute-start(f32[3]{0:T(128)S(1)} %get-tuple-element.192), channel_id=1, source_target_pairs={{0,16},{16,0},{1,17},{17,1},{2,18},{18,2},{3,19},{19,3},{4,20},{20... | collective-permute-start | bytes 44 | tf_op jit(solution)/shard_map/ppermute | solution.py:472
  69.7 20.4 %collective-permute-start.7 = (bf16[4,104,768]{2,1,0:T(8,128)(2,1)}, bf16[4,104,768]{2,1,0:T(8,128)(2,1)}, u32[]{:S(2)}, u32[]{:S(2)}) collective-permute-start(bf16[4,104,768]{2,1,0:T(8,128)(2,1)} %collective-permute-done.4.rest_3_.refs_1_.refs_3_), channel_id=1, source_target_pairs={{0,16},{16,0},{1,17},{17,1},{2,18},{18,2},{3,19},{19,3},{4,20},{20... | collective-permute-start | bytes 1916936 | tf_op jit(solution)/shard_map/ppermute | solution.py:472
  70.2 19.9 %collective-permute-start.6 = (bf16[4,104,768]{2,1,0:T(8,128)(2,1)}, bf16[4,104,768]{2,1,0:T(8,128)(2,1)}, u32[]{:S(2)}, u32[]{:S(2)}) collective-permute-start(bf16[4,104,768]{2,1,0:T(8,128)(2,1)} %collective-permute-done.3.rest_2_.refs_2_), channel_id=1, source_target_pairs={{0,16},{16,0},{1,17},{17,1},{2,18},{18,2},{3,19},{19,3},{4,20},{20... | collective-permute-start | bytes 1916936 | tf_op jit(solution)/shard_map/ppermute | solution.py:472
  70.2 19.9 %collective-permute-start.5 = (bf16[4,104,768]{2,1,0:T(8,128)(2,1)}, bf16[4,104,768]{2,1,0:T(8,128)(2,1)}, u32[]{:S(2)}, u32[]{:S(2)}) collective-permute-start(bf16[4,104,768]{2,1,0:T(8,128)(2,1)} %collective-permute-done.2.rest_1_.refs_1_), channel_id=1, source_target_pairs={{0,16},{16,0},{1,17},{17,1},{2,18},{18,2},{3,19},{19,3},{4,20},{20... | collective-permute-start | bytes 1916936 | tf_op jit(solution)/shard_map/ppermute | solution.py:472
  73.6 62.7 %all-to-all-start.2 = ((bf16[4,192,768]{2,1,0:T(8,128)(2,1)}), bf16[4,192,768]{2,1,0:T(8,128)(2,1)S(1)}, u32[]{:S(2)}, u32[]{:S(2)}) async-start(bf16[4,192,768]{2,1,0:T(8,128)(2,1)} %after.17), calls=%async_computation.2 | async-start | bytes 2359296 | tf_op jit(solution)/shard_map/all_to_all | solution.py:503
  77.1 191.1 %reduce-scatter.2.cloned.1.call-start = ((), (), s32[]{:S(2)}) async-start(), calls=%async_computation.7 | async-start | bytes 2654208 | tf_op jit(solution)/shard_map/reduce_scatter | solution.py:622
  78.2 10.2 %collective-permute-start.8 = (f32[3]{0:T(128)S(1)}, f32[3]{0:T(128)S(1)}, u32[]{:S(2)}, u32[]{:S(2)}) collective-permute-start(f32[3]{0:T(128)S(1)} %get-tuple-element.192), channel_id=1, source_target_pairs={{0,1},{1,0},{2,3},{3,2},{4,5},{5,4},{6,7},{7,6},{8,9},{9,8},{10,11... | collective-permute-start | bytes 44 | tf_op jit(solution)/shard_map/ppermute | solution.py:472
  89.5 19.9 %collective-permute-start.18 = (bf16[544,768]{1,0:T(8,128)(2,1)S(1)}, bf16[544,768]{1,0:T(8,128)(2,1)}, u32[]{:S(2)}, u32[]{:S(2)}) collective-permute-start(bf16[544,768]{1,0:T(8,128)(2,1)S(1)} %copy-done.1), channel_id=1, source_target_pairs={{0,16},{16,0},{1,17},{17,1},{2,18},{18,2},{3,19},{19,3},{4,20},{20... | collective-permute-start | bytes 2506760 | tf_op jit(solution)/shard_map/ppermute | solution.py:472
  89.8 19.9 %collective-permute-start.19 = (bf16[544,768]{1,0:T(8,128)(2,1)}, bf16[544,768]{1,0:T(8,128)(2,1)}, u32[]{:S(2)}, u32[]{:S(2)}) collective-permute-start(bf16[544,768]{1,0:T(8,128)(2,1)} %collective-permute-done.17.rest_9_), channel_id=1, source_target_pairs={{0,16},{16,0},{1,17},{17,1},{2,18},{18,2},{3,19},{19,3},{4,20},{20... | collective-permute-start | bytes 2506760 | tf_op jit(solution)/shard_map/ppermute | solution.py:472
  105.6 34.3 %collective-permute-start.23 = (bf16[4,192,768]{2,1,0:T(8,128)(2,1)}, bf16[4,192,768]{2,1,0:T(8,128)(2,1)}, u32[]{:S(2)}, u32[]{:S(2)}) collective-permute-start(bf16[4,192,768]{2,1,0:T(8,128)(2,1)} %after.19.rest_12_), channel_id=1, source_target_pairs={{0,2},{2,0},{1,3},{3,1},{4,6},{6,4},{5,7},{7,5},{8,10},{10,8},{9,1... | collective-permute-start | bytes 3538952 | tf_op jit(solution)/shard_map/ppermute | solution.py:472
  107.3 20.5 %collective-permute-start.11 = (bf16[272,768]{1,0:T(8,128)(2,1)S(1)}, bf16[272,768]{1,0:T(8,128)(2,1)S(1)}, u32[]{:S(2)}, u32[]{:S(2)}) collective-permute-start(bf16[272,768]{1,0:T(8,128)(2,1)S(1)} %copy-done.5), channel_id=1, source_target_pairs={{0,1},{1,0},{2,3},{3,2},{4,5},{5,4},{6,7},{7,6},{8,9},{9,8},{10,11... | collective-permute-start | bytes 1253384 | tf_op jit(solution)/shard_map/ppermute | solution.py:472
  108.1 19.7 %collective-permute-start.12 = (bf16[272,768]{1,0:T(8,128)(2,1)}, bf16[272,768]{1,0:T(8,128)(2,1)}, u32[]{:S(2)}, u32[]{:S(2)}) collective-permute-start(bf16[272,768]{1,0:T(8,128)(2,1)} %get-tuple-element.78.rest_1_), channel_id=1, source_target_pairs={{0,1},{1,0},{2,3},{3,2},{4,5},{5,4},{6,7},{7,6},{8,9},{9,8},{10,11... | collective-permute-start | bytes 1253384 | tf_op jit(solution)/shard_map/ppermute | solution.py:472
  109.5 27.8 %collective-permute-start.14 = (bf16[272,768]{1,0:T(8,128)(2,1)}, bf16[272,768]{1,0:T(8,128)(2,1)S(1)}, u32[]{:S(2)}, u32[]{:S(2)}) collective-permute-start(bf16[272,768]{1,0:T(8,128)(2,1)} %get-tuple-element.78.rest_1_), channel_id=1, source_target_pairs={{0,16},{16,0},{1,17},{17,1},{2,18},{18,2},{3,19},{19,3},{4,20},{20... | collective-permute-start | bytes 1253384 | tf_op jit(solution)/shard_map/ppermute | solution.py:472
  109.7 30.2 %collective-permute-start.13 = (bf16[272,768]{1,0:T(8,128)(2,1)S(1)}, bf16[272,768]{1,0:T(8,128)(2,1)S(1)}, u32[]{:S(2)}, u32[]{:S(2)}) collective-permute-start(bf16[272,768]{1,0:T(8,128)(2,1)S(1)} %copy-done.5), channel_id=1, source_target_pairs={{0,16},{16,0},{1,17},{17,1},{2,18},{18,2},{3,19},{19,3},{4,20},{20... | collective-permute-start | bytes 1253384 | tf_op jit(solution)/shard_map/ppermute | solution.py:472
  127.8 12.1 %collective-permute-start.16 = (bf16[272,768]{1,0:T(8,128)(2,1)}, bf16[272,768]{1,0:T(8,128)(2,1)}, u32[]{:S(2)}, u32[]{:S(2)}) collective-permute-start(bf16[272,768]{1,0:T(8,128)(2,1)} %collective-permute-done.12.rest_3_), channel_id=1, source_target_pairs={{0,16},{16,0},{1,17},{17,1},{2,18},{18,2},{3,19},{19,3},{4,20},{20... | collective-permute-start | bytes 1253384 | tf_op jit(solution)/shard_map/ppermute | solution.py:472
  127.9 12.1 %collective-permute-start.15 = (bf16[272,768]{1,0:T(8,128)(2,1)S(1)}, bf16[272,768]{1,0:T(8,128)(2,1)}, u32[]{:S(2)}, u32[]{:S(2)}) collective-permute-start(bf16[272,768]{1,0:T(8,128)(2,1)S(1)} %collective-permute-done.11.refs_1_.rest_2_), channel_id=1, source_target_pairs={{0,16},{16,0},{1,17},{17,1},{2,18},{18,2},{3,19},{19,3},{4,20},{20... | collective-permute-start | bytes 1253384 | tf_op jit(solution)/shard_map/ppermute | solution.py:472
  137.3 27.0 %collective-permute-start.22 = (bf16[4,192,768]{2,1,0:T(8,128)(2,1)}, bf16[4,192,768]{2,1,0:T(8,128)(2,1)S(1)}, u32[]{:S(2)}, u32[]{:S(2)}) collective-permute-start(bf16[4,192,768]{2,1,0:T(8,128)(2,1)} %after.18.rest_12_), channel_id=1, source_target_pairs={{0,2},{2,0},{1,3},{3,1},{4,6},{6,4},{5,7},{7,5},{8,10},{10,8},{9,1... | collective-permute-start | bytes 3538952 | tf_op jit(solution)/shard_map/ppermute | solution.py:472
  182.8 78.1 %all-to-all-start.4 = ((bf16[4,384,768]{2,1,0:T(8,128)(2,1)}), bf16[4,384,768]{2,1,0:T(8,128)(2,1)S(1)}, u32[]{:S(2)}, u32[]{:S(2)}) async-start(bf16[4,384,768]{2,1,0:T(8,128)(2,1)} %bitcast.145), calls=%async_computation.5 | async-start | bytes 4718592 | tf_op jit(solution)/shard_map/all_to_all | solution.py:618
  205.3 6.2 %collective-permute-start.27 = (bf16[272,768]{1,0:T(8,128)(2,1)}, bf16[272,768]{1,0:T(8,128)(2,1)S(1)}, u32[]{:S(2)}, u32[]{:S(2)}) collective-permute-start(bf16[272,768]{1,0:T(8,128)(2,1)} %get-tuple-element.113), channel_id=1, source_target_pairs={{0,16},{16,0},{1,17},{17,1},{2,18},{18,2},{3,19},{19,3},{4,20},{20... | collective-permute-start | bytes 1253384 | tf_op jit(solution)/shard_map/ppermute | solution.py:472
  205.9 15.2 %collective-permute-start.25 = (bf16[544,768]{1,0:T(8,128)(2,1)}, bf16[544,768]{1,0:T(8,128)(2,1)S(1)}, u32[]{:S(2)}, u32[]{:S(2)}) collective-permute-start(bf16[544,768]{1,0:T(8,128)(2,1)} %get-tuple-element.107), channel_id=1, source_target_pairs={{0,16},{16,0},{1,17},{17,1},{2,18},{18,2},{3,19},{19,3},{4,20},{20... | collective-permute-start | bytes 2506760 | tf_op jit(solution)/shard_map/ppermute | solution.py:472
  207.6 12.6 %collective-permute-start.29 = (bf16[272,768]{1,0:T(8,128)(2,1)S(1)}, bf16[272,768]{1,0:T(8,128)(2,1)S(1)}, u32[]{:S(2)}, u32[]{:S(2)}) collective-permute-start(bf16[272,768]{1,0:T(8,128)(2,1)S(1)} %add_convert_fusion.10), channel_id=1, source_target_pairs={{0,1},{1,0},{2,3},{3,2},{4,5},{5,4},{6,7},{7,6},{8,9},{9,8},{10,11... | collective-permute-start | bytes 1253384 | tf_op jit(solution)/shard_map/ppermute | solution.py:472
  209.2 13.7 %collective-permute-start.30 = (bf16[272,768]{1,0:T(8,128)(2,1)}, bf16[272,768]{1,0:T(8,128)(2,1)}, u32[]{:S(2)}, u32[]{:S(2)}) collective-permute-start(bf16[272,768]{1,0:T(8,128)(2,1)} %get-tuple-element.117), channel_id=1, source_target_pairs={{0,16},{16,0},{1,17},{17,1},{2,18},{18,2},{3,19},{19,3},{4,20},{20... | collective-permute-start | bytes 1253384 | tf_op jit(solution)/shard_map/ppermute | solution.py:472
  209.2 42.7 %collective-permute-start.42 = (bf16[4,192,768]{2,1,0:T(8,128)(2,1)}, bf16[4,192,768]{2,1,0:T(8,128)(2,1)}, u32[]{:S(2)}, u32[]{:S(2)}) collective-permute-start(bf16[4,192,768]{2,1,0:T(8,128)(2,1)} %get-tuple-element.138), channel_id=1, source_target_pairs={{0,2},{2,0},{1,3},{3,1},{4,6},{6,4},{5,7},{7,5},{8,10},{10,8},{9,1... | collective-permute-start | bytes 3538952 | tf_op jit(solution)/shard_map/ppermute | solution.py:472
  211.6 16.7 %collective-permute-start.32 = (bf16[272,768]{1,0:T(8,128)(2,1)}, bf16[272,768]{1,0:T(8,128)(2,1)S(1)}, u32[]{:S(2)}, u32[]{:S(2)}) collective-permute-start(bf16[272,768]{1,0:T(8,128)(2,1)} %add_convert_fusion.8), channel_id=1, source_target_pairs={{0,1},{1,0},{2,3},{3,2},{4,5},{5,4},{6,7},{7,6},{8,9},{9,8},{10,11... | collective-permute-start | bytes 1253384 | tf_op jit(solution)/shard_map/ppermute | solution.py:472
  250.8 7.6 %collective-permute-start.37 = (bf16[4,104,768]{2,1,0:T(8,128)(2,1)}, bf16[4,104,768]{2,1,0:T(8,128)(2,1)S(1)}, u32[]{:S(2)}, u32[]{:S(2)}) collective-permute-start(bf16[4,104,768]{2,1,0:T(8,128)(2,1)} %get-tuple-element.133), channel_id=1, source_target_pairs={{0,16},{16,0},{1,17},{17,1},{2,18},{18,2},{3,19},{19,3},{4,20},{20... | collective-permute-start | bytes 1916936 | tf_op jit(solution)/shard_map/ppermute | solution.py:472
  251.3 14.6 %collective-permute-start.33 = (bf16[4,104,768]{2,1,0:T(8,128)(2,1)}, bf16[4,104,768]{2,1,0:T(8,128)(2,1)}, u32[]{:S(2)}, u32[]{:S(2)}) collective-permute-start(bf16[4,104,768]{2,1,0:T(8,128)(2,1)} %get-tuple-element.128), channel_id=1, source_target_pairs={{0,16},{16,0},{1,17},{17,1},{2,18},{18,2},{3,19},{19,3},{4,20},{20... | collective-permute-start | bytes 1916936 | tf_op jit(solution)/shard_map/ppermute | solution.py:472
  251.4 17.5 %collective-permute-start.39 = (bf16[4,104,768]{2,1,0:T(8,128)(2,1)}, bf16[4,104,768]{2,1,0:T(8,128)(2,1)}, u32[]{:S(2)}, u32[]{:S(2)}) collective-permute-start(bf16[4,104,768]{2,1,0:T(8,128)(2,1)} %get-tuple-element.135), channel_id=1, source_target_pairs={{0,16},{16,0},{1,17},{17,1},{2,18},{18,2},{3,19},{19,3},{4,20},{20... | collective-permute-start | bytes 1916936 | tf_op jit(solution)/shard_map/ppermute | solution.py:472
  257.0 17.6 %collective-permute-start.36 = (bf16[4,104,768]{2,1,0:T(8,128)(2,1)}, bf16[4,104,768]{2,1,0:T(8,128)(2,1)}, u32[]{:S(2)}, u32[]{:S(2)}) collective-permute-start(bf16[4,104,768]{2,1,0:T(8,128)(2,1)} %add_convert_fusion.6), channel_id=1, source_target_pairs={{0,1},{1,0},{2,3},{3,2},{4,5},{5,4},{6,7},{7,6},{8,9},{9,8},{10,11... | collective-permute-start | bytes 1916936 | tf_op jit(solution)/shard_map/ppermute | solution.py:472
  259.4 30.1 %collective-permute-start.38 = (bf16[4,104,768]{2,1,0:T(8,128)(2,1)}, bf16[4,104,768]{2,1,0:T(8,128)(2,1)}, u32[]{:S(2)}, u32[]{:S(2)}) collective-permute-start(bf16[4,104,768]{2,1,0:T(8,128)(2,1)} %add_convert_fusion.5), channel_id=1, source_target_pairs={{0,2},{2,0},{1,3},{3,1},{4,6},{6,4},{5,7},{7,5},{8,10},{10,8},{9,1... | collective-permute-start | bytes 1916936 | tf_op jit(solution)/shard_map/ppermute | solution.py:472
  260.9 36.1 %all-to-all-start.5 = ((bf16[4,192,768]{2,1,0:T(8,128)(2,1)}), bf16[4,192,768]{2,1,0:T(8,128)(2,1)S(1)}, u32[]{:S(2)}, u32[]{:S(2)}) async-start(bf16[4,192,768]{2,1,0:T(8,128)(2,1)} %add_convert_fusion), calls=%async_computation.6 | async-start | bytes 2359296 | tf_op jit(solution)/shard_map/all_to_all | solution.py:618
  268.2 21.3 %collective-permute-start.34 = (bf16[4,104,768]{2,1,0:T(8,128)(2,1)}, bf16[4,104,768]{2,1,0:T(8,128)(2,1)}, u32[]{:S(2)}, u32[]{:S(2)}) collective-permute-start(bf16[4,104,768]{2,1,0:T(8,128)(2,1)} %after.21), channel_id=1, source_target_pairs={{0,3},{1,2},{2,1},{3,0},{4,7},{5,6},{6,5},{7,4},{8,11},{9,10},{10,... | collective-permute-start | bytes 1916936 | tf_op jit(solution)/shard_map/ppermute | solution.py:476
  268.9 35.7 %collective-permute-start.24 = (bf16[544,768]{1,0:T(8,128)(2,1)}, bf16[544,768]{1,0:T(8,128)(2,1)}, u32[]{:S(2)}, u32[]{:S(2)}) collective-permute-start(bf16[544,768]{1,0:T(8,128)(2,1)} %get-tuple-element.105), channel_id=1, source_target_pairs={{0,16},{16,0},{1,17},{17,1},{2,18},{18,2},{3,19},{19,3},{4,20},{20... | collective-permute-start | bytes 2506760 | tf_op jit(solution)/shard_map/ppermute | solution.py:472
  269.4 35.9 %collective-permute-start.26 = (bf16[544,768]{1,0:T(8,128)(2,1)S(1)}, bf16[544,768]{1,0:T(8,128)(2,1)}, u32[]{:S(2)}, u32[]{:S(2)}) collective-permute-start(bf16[544,768]{1,0:T(8,128)(2,1)S(1)} %copy-done.13), channel_id=1, source_target_pairs={{0,1},{1,0},{2,3},{3,2},{4,5},{5,4},{6,7},{7,6},{8,9},{9,8},{10,11... | collective-permute-start | bytes 2506760 | tf_op jit(solution)/shard_map/ppermute | solution.py:472
  295.5 7.9 %collective-permute-start.41 = (bf16[192,768]{1,0:T(8,128)(2,1)}, bf16[192,768]{1,0:T(8,128)(2,1)}, u32[]{:S(2)}, u32[]{:S(2)}) collective-permute-start(bf16[192,768]{1,0:T(8,128)(2,1)} %fusion.14), channel_id=1, source_target_pairs={{0,2},{2,0},{1,3},{3,1},{4,6},{6,4},{5,7},{7,5},{8,10},{10,8},{9,1... | collective-permute-start | bytes 884744 | tf_op jit(solution)/shard_map/ppermute | solution.py:472
  297.9 21.2 %all-to-all-start.3 = ((bf16[4,104,768]{2,1,0:T(8,128)(2,1)}), bf16[4,104,768]{2,1,0:T(8,128)(2,1)S(1)}, u32[]{:S(2)}, u32[]{:S(2)}) async-start(bf16[4,104,768]{2,1,0:T(8,128)(2,1)} %get-tuple-element.139), calls=%async_computation.4 | async-start | bytes 1277952 | tf_op jit(solution)/shard_map/all_to_all | solution.py:645
  304.6 4.9 %collective-permute-start.45 = (bf16[3,96,768]{2,1,0:T(8,128)(2,1)S(1)}, bf16[3,96,768]{2,1,0:T(8,128)(2,1)S(1)}, u32[]{:S(2)}, u32[]{:S(2)}) collective-permute-start(bf16[3,96,768]{2,1,0:T(8,128)(2,1)S(1)} %slice.237), channel_id=1, source_target_pairs={{0,16},{16,0},{1,17},{17,1},{2,18},{18,2},{3,19},{19,3},{4,20},{20... | collective-permute-start | bytes 1327112 | tf_op jit(solution)/shard_map/ppermute | solution.py:472
  309.6 11.5 %collective-permute-start.43 = (bf16[3,48,768]{2,1,0:T(8,128)(2,1)S(1)}, bf16[3,48,768]{2,1,0:T(8,128)(2,1)S(1)}, u32[]{:S(2)}, u32[]{:S(2)}) collective-permute-start(bf16[3,48,768]{2,1,0:T(8,128)(2,1)S(1)} %dynamic-slice_bitcast_fusion), channel_id=1, source_target_pairs={{0,1},{1,0},{2,3},{3,2},{4,5},{5,4},{6,7},{7,6},{8,9},{9,8},{10,11... | collective-permute-start | bytes 663560 | tf_op jit(solution)/shard_map/ppermute | solution.py:472
  (33 other events, 179.0 us)
Sparse Core Ops, SparseCore 0:
  67.7 73.6 all-gather.2
Sparse Core Ops, SparseCore 1:
  158.1 84.6 reduce-scatter.1

commit v4 on v3

--- a/solution.py
+++ b/solution.py
@@ -129,7 +129,7 @@
             mixed_ref[rows, cols] = merge_heads(dot(probs, v_ref[rows, cols])).astype(BF16)
             return carry
 
-        lax.fori_loop(0, PAIRS, step, 0, unroll=3)
+        lax.fori_loop(0, PAIRS, step, 0, unroll=True)
     middle = tok[...].astype(F32) + dot(mixed_ref[...], weight(3)) + vec_ref[2:3, :]
     mid_ref[...] = middle
     scaled_two, _ = norm_stats(middle)
@@ -420,7 +420,7 @@
             dk[rows, cols] = (dot_tn(score_grad, two_heads(q_ref[rows, cols])) * scale).astype(BF16)
             return carry
 
-        lax.fori_loop(0, PAIRS, step, 0, unroll=3)
+        lax.fori_loop(0, PAIRS, step, 0, unroll=True)
     scaled, inverse = norm_stats(tok[...].astype(F32))
     normed = (scaled * vec_ref[0:1, :] + vec_ref[1:2, :]).astype(BF16)
     put(0, dot_tn(normed, dq[...]))

time: 348 us -> 347 us (level)
  transfers between devices with their start and end apart: 54 -> 54, of which waited for: 17 -> 18; matrix products, arithmetic and copies ran while one was open for 14% -> 14% of each run, Pallas kernels for 26% -> 25%
where the time goes in v4:
time: 347 us; the launch traced here: 341 us
  waiting for transfers between devices  109 us (31%)
  Pallas kernels  86.1 us (25%)
  starting transfers between devices  59.2 us (17%)
  other arithmetic  32.9 us (9%)
  local copies, waits for them, and re-layouts  29.3 us (8%)
  between operations  19.2 us (6%)
  matrix products  5.65 us (2%)
    ppermute x43, waiting for transfers between devices, swap(): return lax.ppermute(value, axis, [(0, 1), (1, 0)])  80.6 us
    pallas_call x3, Pallas kernels, ffn(): pl.pallas_call(functools.partial(ffn_kernel, e, first, len(weights), whol...  52.3 us
    ppermute x43, starting transfers between devices, swap(): return lax.ppermute(value, axis, [(0, 1), (1, 0)])  26.2 us
    pallas_call x1, Pallas kernels, attn_bwd(): pl.pallas_call(functools.partial(attn_bwd_kernel, share), out_shape=(jax....  19.8 us
    pallas_call x1, Pallas kernels, attn_fwd(): pl.pallas_call(functools.partial(attn_fwd_kernel, share), out_shape=(jax....  13.9 us
    all_to_all x3, waiting for transfers between devices, spread(): lax.all_to_all(after(copies, *wait) if wait else copies, 'z', 0, 0, tiled...  13.4 us
    all_to_all x3, starting transfers between devices, spread(): lax.all_to_all(after(copies, *wait) if wait else copies, 'z', 0, 0, tiled...  13.4 us
    convert_element_type x7, other arithmetic, add_low(): return (a.astype(F32) + b.astype(F32)).astype(BF16)  11.6 us
  transfers between devices with their start and end apart: 54, of which 18 were waited for; matrix products, arithmetic and copies ran while one was open for 14% of the time, Pallas kernels for 25%

profile of v4, /device:TPU:0, one launch (start us, length us, event | category | flops | bytes accessed | tf_op | source)
XLA Modules:
  0.0 341.1 jit_solution(1853905493164036757)
XLA Ops:
  11.4 6.3 %all-to-all-start = ((bf16[4,104,768]{2,1,0:T(8,128)(2,1)}), bf16[4,104,768]{2,1,0:T(8,128)(2,1)S(1)}, u32[]{:S(2)}, u32[]{:S(2)}) async-start(bf16[4,104,768]{2,1,0:T(8,128)(2,1)} %broadcast_in_dim.37), calls=%async_computation | async-start | bytes 1277952 | tf_op jit(solution)/shard_map/all_to_all | solution.py:503
  21.0 2.4 collective-permute-start.21
  30.8 1.5 convolution_convert_fusion.refs_1_.refs_0_
  32.3 2.4 all-to-all-done.refs_0_
  35.7 2.5 collective-permute-start.4
  41.4 3.5 %all-to-all-start.1 = ((bf16[4,192,768]{2,1,0:T(8,128)(2,1)}), bf16[4,192,768]{2,1,0:T(8,128)(2,1)S(1)}, u32[]{:S(2)}, u32[]{:S(2)}) async-start(bf16[4,192,768]{2,1,0:T(8,128)(2,1)} %after.13), calls=%async_computation.1 | async-start | bytes 2359296 | tf_op jit(solution)/shard_map/all_to_all | solution.py:503
  46.0 8.2 %collective-permute-done.4.rest_3_.refs_1_.refs_3_ = bf16[4,104,768]{2,1,0:T(8,128)(2,1)} collective-permute-done((bf16[4,104,768]{2,1,0:T(8,128)(2,1)}, bf16[4,104,768]{2,1,0:T(8,128)(2,1)}, u32[]{:S(2)}, u32[]{:S(2)}) %collective-permute-start.4) | collective-permute-done | bytes 639008 | tf_op jit(solution)/shard_map/ppermute | solution.py:476
  54.2 13.3 %collective-permute-done.3.rest_2_.refs_2_ = bf16[4,104,768]{2,1,0:T(8,128)(2,1)} collective-permute-done((bf16[4,104,768]{2,1,0:T(8,128)(2,1)}, bf16[4,104,768]{2,1,0:T(8,128)(2,1)}, u32[]{:S(2)}, u32[]{:S(2)}) %collective-permute-start.3) | collective-permute-done | bytes 639008 | tf_op jit(solution)/shard_map/ppermute | solution.py:472
  67.6 1.6 collective-permute-start.17
  71.9 1.7 all-to-all-done.1.refs_1_.refs_0_
  73.6 3.5 %all-to-all-start.2 = ((bf16[4,192,768]{2,1,0:T(8,128)(2,1)}), bf16[4,192,768]{2,1,0:T(8,128)(2,1)S(1)}, u32[]{:S(2)}, u32[]{:S(2)}) async-start(bf16[4,192,768]{2,1,0:T(8,128)(2,1)} %after.17), calls=%async_computation.2 | async-start | bytes 2359296 | tf_op jit(solution)/shard_map/all_to_all | solution.py:503
  78.0 1.5 collective-permute-start.8
  79.5 8.9 %collective-permute-done.8 = f32[3]{0:T(128)S(1)} collective-permute-done((f32[3]{0:T(128)S(1)}, f32[3]{0:T(128)S(1)}, u32[]{:S(2)}, u32[]{:S(2)}) %collective-permute-start.8) | collective-permute-done | bytes 44 | tf_op jit(solution)/shard_map/ppermute | solution.py:472
  90.1 13.9 %attn_fwd.1 = (f32[512,768]{1,0:T(8,128)}, bf16[272,768]{1,0:T(8,128)(2,1)}, bf16[272,768]{1,0:T(8,128)(2,1)}, bf16[512,768]{1,0:T(8,128)(2,1)}, bf16[512,768]{1...) custom-call(s32[3]{0:T(128)} %pad_add_fusion.1.where_ref, ...), custom_call_target="tpu_custom_call" | custom-call | flops 6000000000 | bytes 1 | tf_op jit(solution)/shard_map/attn_fwd/pallas_call | solution.py:185
  104.1 1.6 collective-permute-start.23
  108.7 17.6 %collective-permute-done.12.rest_3_ = bf16[272,768]{1,0:T(8,128)(2,1)} collective-permute-done((bf16[272,768]{1,0:T(8,128)(2,1)}, bf16[272,768]{1,0:T(8,128)(2,1)}, u32[]{:S(2)}, u32[]{:S(2)}) %collective-permute-start.12) | collective-permute-done | bytes 417824 | tf_op jit(solution)/shard_map/ppermute | solution.py:472
  126.9 9.3 %all-to-all-done.2.refs_0_ = bf16[4,192,768]{2,1,0:T(8,128)(2,1)S(1)} async-done(((bf16[4,192,768]{2,1,0:T(8,128)(2,1)}), bf16[4,192,768]{2,1,0:T(8,128)(2,1)S(1)}, u32[]{:S(2)}, u32[]{:S(2)}) %all-to-all-start.2) | async-done | bytes 1179680 | tf_op jit(solution)/shard_map/all_to_all | solution.py:503
  137.3 1.5 collective-permute-start.22
  140.7 17.7 %ffn.3 = (bf16[544,768]{1,0:T(8,128)(2,1)}, bf16[544,768]{1,0:T(8,128)(2,1)}, bf16[544,768]{1,0:T(8,128)(2,1)}, bf16[544,768]{1,0:T(8,128)(2,1)}, bf16[272,768]{...) custom-call(s32[144]{0:T(256)} %bitcast.170, ...), custom_call_target="tpu_custom_call" | custom-call | flops 1 | bytes 1 | tf_op jit(solution)/shard_map/ffn/pallas_call | solution.py:336
  158.4 5.9 %collective-permute-done.22.rest_13_ = bf16[4,192,768]{2,1,0:T(8,128)(2,1)S(1)} collective-permute-done((bf16[4,192,768]{2,1,0:T(8,128)(2,1)}, bf16[4,192,768]{2,1,0:T(8,128)(2,1)S(1)}, u32[]{:S(2)}, u32[]{:S(2)}) %collective-permute-start.22) | collective-permute-done | bytes 1179680 | tf_op jit(solution)/shard_map/ppermute | solution.py:472
  165.3 17.3 %ffn.4 = (bf16[544,768]{1,0:T(8,128)(2,1)}, bf16[544,768]{1,0:T(8,128)(2,1)}, bf16[544,768]{1,0:T(8,128)(2,1)}, bf16[544,768]{1,0:T(8,128)(2,1)}, bf16[272,768]{...) custom-call(s32[144]{0:T(256)} %bitcast.169, ...), custom_call_target="tpu_custom_call", output_to_operand_aliasing={{0}: (18, {}), {1}: (19, {}), {2}: (20, {}), {3}: (21, {}),... | custom-call | flops 1 | bytes 1 | tf_op jit(solution)/shard_map/ffn/pallas_call | solution.py:336
  182.6 3.7 %all-to-all-start.4 = ((bf16[4,384,768]{2,1,0:T(8,128)(2,1)}), bf16[4,384,768]{2,1,0:T(8,128)(2,1)S(1)}, u32[]{:S(2)}, u32[]{:S(2)}) async-start(bf16[4,384,768]{2,1,0:T(8,128)(2,1)} %bitcast.145), calls=%async_computation.5 | async-start | bytes 4718592 | tf_op jit(solution)/shard_map/all_to_all | solution.py:618
  186.3 17.4 %ffn.5 = (bf16[544,768]{1,0:T(8,128)(2,1)}, bf16[544,768]{1,0:T(8,128)(2,1)}, bf16[544,768]{1,0:T(8,128)(2,1)}, bf16[544,768]{1,0:T(8,128)(2,1)}, bf16[272,768]{...) custom-call(s32[144]{0:T(256)} %bitcast.168, ...), custom_call_target="tpu_custom_call", output_to_operand_aliasing={{0}: (17, {}), {1}: (18, {}), {2}: (19, {}), {3}: (20, {}),... | custom-call | flops 1 | bytes 1 | tf_op jit(solution)/shard_map/ffn/pallas_call | solution.py:336
  206.4 1.2 add_convert_fusion.10
  207.7 1.5 collective-permute-start.29
  209.2 1.6 collective-permute-start.42
  212.2 8.0 %collective-permute-done.29 = bf16[272,768]{1,0:T(8,128)(2,1)S(1)} collective-permute-done((bf16[272,768]{1,0:T(8,128)(2,1)S(1)}, bf16[272,768]{1,0:T(8,128)(2,1)S(1)}, u32[]{:S(2)}, u32[]{:S(2)}) %collective-permute-start.29) | collective-permute-done | bytes 417824 | tf_op jit(solution)/shard_map/ppermute | solution.py:472
  222.9 5.4 %collective-permute-done.32 = bf16[272,768]{1,0:T(8,128)(2,1)S(1)} collective-permute-done((bf16[272,768]{1,0:T(8,128)(2,1)}, bf16[272,768]{1,0:T(8,128)(2,1)S(1)}, u32[]{:S(2)}, u32[]{:S(2)}) %collective-permute-start.32) | collective-permute-done | bytes 417824 | tf_op jit(solution)/shard_map/ppermute | solution.py:472
  228.3 2.0 select_convert_fusion.2.rest_1_
  230.3 19.8 %attn_bwd.1 = (bf16[512,768]{1,0:T(8,128)(2,1)}, bf16[4,104,768]{2,1,0:T(8,128)(2,1)}, bf16[4,104,768]{2,1,0:T(8,128)(2,1)}, bf16[4,104,768]{2,1,0:T(8,128)(2,1)...) custom-call(s32[3]{0:T(128)} %pad_add_fusion.1.where_ref, ...), custom_call_target="tpu_custom_call" | custom-call | flops 1 | bytes 1 | tf_op jit(solution)/shard_map/attn_bwd/pallas_call | solution.py:451
  251.1 3.0 add_convert_fusion
  254.1 2.1 add_convert_fusion.6
  256.3 1.4 collective-permute-start.36
  258.7 1.5 collective-permute-start.38
  260.2 5.0 %all-to-all-start.5 = ((bf16[4,192,768]{2,1,0:T(8,128)(2,1)}), bf16[4,192,768]{2,1,0:T(8,128)(2,1)S(1)}, u32[]{:S(2)}, u32[]{:S(2)}) async-start(bf16[4,192,768]{2,1,0:T(8,128)(2,1)} %add_convert_fusion), calls=%async_computation.6 | async-start | bytes 2359296 | tf_op jit(solution)/shard_map/all_to_all | solution.py:618
  265.2 2.3 add_convert_fusion.7.refs_0_
  269.6 4.2 %collective-permute-done.36 = bf16[4,104,768]{2,1,0:T(8,128)(2,1)} collective-permute-done((bf16[4,104,768]{2,1,0:T(8,128)(2,1)}, bf16[4,104,768]{2,1,0:T(8,128)(2,1)}, u32[]{:S(2)}, u32[]{:S(2)}) %collective-permute-start.36) | collective-permute-done | bytes 639008 | tf_op jit(solution)/shard_map/ppermute | solution.py:472
  273.8 14.9 %collective-permute-done.38 = bf16[4,104,768]{2,1,0:T(8,128)(2,1)} collective-permute-done((bf16[4,104,768]{2,1,0:T(8,128)(2,1)}, bf16[4,104,768]{2,1,0:T(8,128)(2,1)}, u32[]{:S(2)}, u32[]{:S(2)}) %collective-permute-start.38) | collective-permute-done | bytes 639008 | tf_op jit(solution)/shard_map/ppermute | solution.py:472
  288.8 3.1 add_convert_fusion.3
  291.9 2.1 convert_reduce_fusion
  294.7 1.5 collective-permute-start.41
  297.2 5.1 %all-to-all-start.3 = ((bf16[4,104,768]{2,1,0:T(8,128)(2,1)}), bf16[4,104,768]{2,1,0:T(8,128)(2,1)S(1)}, u32[]{:S(2)}, u32[]{:S(2)}) async-start(bf16[4,104,768]{2,1,0:T(8,128)(2,1)} %get-tuple-element.139), calls=%async_computation.4 | async-start | bytes 1277952 | tf_op jit(solution)/shard_map/all_to_all | solution.py:645
  304.9 2.6 fusion.1
  307.5 1.3 fusion
  310.2 1.3 copy.96
  311.5 6.6 %all-to-all-done.3 = bf16[4,104,768]{2,1,0:T(8,128)(2,1)S(1)} async-done(((bf16[4,104,768]{2,1,0:T(8,128)(2,1)}), bf16[4,104,768]{2,1,0:T(8,128)(2,1)S(1)}, u32[]{:S(2)}, u32[]{:S(2)}) %all-to-all-start.3) | async-done | bytes 639008 | tf_op jit(solution)/shard_map/all_to_all | solution.py:645
  325.9 3.0 convert_bitcast_fusion
  328.9 4.4 %reshape.440 = f32[3,48,3072]{2,1,0:T(8,128)} reshape(f32[3,48,8,2,2,96]{5,4,3,2,1,0:T(2,128)S(1)} %convert_bitcast_fusion) | data formatting | bytes 3538944 | tf_op jit(solution)/shard_map/convert_element_type | solution.py:672
  (230 shorter events, 53.8 us)
Async XLA Ops:
  11.4 23.3 %all-to-all-start = ((bf16[4,104,768]{2,1,0:T(8,128)(2,1)}), bf16[4,104,768]{2,1,0:T(8,128)(2,1)S(1)}, u32[]{:S(2)}, u32[]{:S(2)}) async-start(bf16[4,104,768]{2,1,0:T(8,128)(2,1)} %broadcast_in_dim.37), calls=%async_computation | async-start | bytes 1277952 | tf_op jit(solution)/shard_map/all_to_all | solution.py:503
  21.0 18.3 %collective-permute-start.21 = (bf16[48,768]{1,0:T(8,128)(2,1)}, bf16[48,768]{1,0:T(8,128)(2,1)}, u32[]{:S(2)}, u32[]{:S(2)}) collective-permute-start(bf16[48,768]{1,0:T(8,128)(2,1)} %squeeze.87), channel_id=1, source_target_pairs={{0,3},{1,2},{2,1},{3,0},{4,7},{5,6},{6,5},{7,4},{8,11},{9,10},{10,... | collective-permute-start | bytes 221192 | tf_op jit(solution)/shard_map/ppermute | solution.py:476
  23.6 8.7 %collective-permute-start = (bf16[3,48,768]{2,1,0:T(8,128)(2,1)S(1)}, bf16[3,48,768]{2,1,0:T(8,128)(2,1)S(1)}, u32[]{:S(2)}, u32[]{:S(2)}) collective-permute-start(bf16[3,48,768]{2,1,0:T(8,128)(2,1)S(1)} %reshape.435), channel_id=1, source_target_pairs={{0,1},{1,0},{2,3},{3,2},{4,5},{5,4},{6,7},{7,6},{8,9},{9,8},{10,11... | collective-permute-start | bytes 663560 | tf_op jit(solution)/shard_map/ppermute | solution.py:472
  25.6 10.0 %collective-permute-start.20 = (bf16[144,768]{1,0:T(8,128)(2,1)S(1)}, bf16[144,768]{1,0:T(8,128)(2,1)S(1)}, u32[]{:S(2)}, u32[]{:S(2)}) collective-permute-start(bf16[144,768]{1,0:T(8,128)(2,1)S(1)} %pad_maximum_fusion.7), channel_id=1, source_target_pairs={{0,2},{2,0},{1,3},{3,1},{4,6},{6,4},{5,7},{7,5},{8,10},{10,8},{9,1... | collective-permute-start | bytes 663560 | tf_op jit(solution)/shard_map/ppermute | solution.py:472
  35.6 4.6 %collective-permute-start.1 = (bf16[4,104,768]{2,1,0:T(8,128)(2,1)}, bf16[4,104,768]{2,1,0:T(8,128)(2,1)S(1)}, u32[]{:S(2)}, u32[]{:S(2)}) collective-permute-start(bf16[4,104,768]{2,1,0:T(8,128)(2,1)} %after.12.rest_0_), channel_id=1, source_target_pairs={{0,16},{16,0},{1,17},{17,1},{2,18},{18,2},{3,19},{19,3},{4,20},{20... | collective-permute-start | bytes 1916936 | tf_op jit(solution)/shard_map/ppermute | solution.py:472
  35.7 18.5 %collective-permute-start.4 = (bf16[4,104,768]{2,1,0:T(8,128)(2,1)}, bf16[4,104,768]{2,1,0:T(8,128)(2,1)}, u32[]{:S(2)}, u32[]{:S(2)}) collective-permute-start(bf16[4,104,768]{2,1,0:T(8,128)(2,1)} %after.12.rest_0_), channel_id=1, source_target_pairs={{0,3},{1,2},{2,1},{3,0},{4,7},{5,6},{6,5},{7,4},{8,11},{9,10},{10,... | collective-permute-start | bytes 1916936 | tf_op jit(solution)/shard_map/ppermute | solution.py:476
  38.2 29.3 %collective-permute-start.3 = (bf16[4,104,768]{2,1,0:T(8,128)(2,1)}, bf16[4,104,768]{2,1,0:T(8,128)(2,1)}, u32[]{:S(2)}, u32[]{:S(2)}) collective-permute-start(bf16[4,104,768]{2,1,0:T(8,128)(2,1)} %after.12.rest_0_), channel_id=1, source_target_pairs={{0,2},{2,0},{1,3},{3,1},{4,6},{6,4},{5,7},{7,5},{8,10},{10,8},{9,1... | collective-permute-start | bytes 1916936 | tf_op jit(solution)/shard_map/ppermute | solution.py:472
  38.7 28.8 %collective-permute-start.2 = (bf16[4,104,768]{2,1,0:T(8,128)(2,1)}, bf16[4,104,768]{2,1,0:T(8,128)(2,1)}, u32[]{:S(2)}, u32[]{:S(2)}) collective-permute-start(bf16[4,104,768]{2,1,0:T(8,128)(2,1)} %after.12.rest_0_), channel_id=1, source_target_pairs={{0,1},{1,0},{2,3},{3,2},{4,5},{5,4},{6,7},{7,6},{8,9},{9,8},{10,11... | collective-permute-start | bytes 1916936 | tf_op jit(solution)/shard_map/ppermute | solution.py:472
  41.4 32.1 %all-to-all-start.1 = ((bf16[4,192,768]{2,1,0:T(8,128)(2,1)}), bf16[4,192,768]{2,1,0:T(8,128)(2,1)S(1)}, u32[]{:S(2)}, u32[]{:S(2)}) async-start(bf16[4,192,768]{2,1,0:T(8,128)(2,1)} %after.13), calls=%async_computation.1 | async-start | bytes 2359296 | tf_op jit(solution)/shard_map/all_to_all | solution.py:503
  45.0 141.3 %all-gather.3.cloned.1.call-start = ((), (), s32[]{:S(2)}) async-start(), calls=%async_computation.8 | async-start | bytes 2949120 | tf_op jit(solution)/shard_map/all_gather | solution.py:588
  67.6 22.3 %collective-permute-start.17 = (bf16[544,768]{1,0:T(8,128)(2,1)}, bf16[544,768]{1,0:T(8,128)(2,1)}, u32[]{:S(2)}, u32[]{:S(2)}) collective-permute-start(bf16[544,768]{1,0:T(8,128)(2,1)} %after.15.rest_8_), channel_id=1, source_target_pairs={{0,1},{1,0},{2,3},{3,2},{4,5},{5,4},{6,7},{7,6},{8,9},{9,8},{10,11... | collective-permute-start | bytes 2506760 | tf_op jit(solution)/shard_map/ppermute | solution.py:472
  69.1 8.8 %collective-permute-start.9 = (f32[3]{0:T(128)S(1)}, f32[3]{0:T(128)S(1)}, u32[]{:S(2)}, u32[]{:S(2)}) collective-permute-start(f32[3]{0:T(128)S(1)} %get-tuple-element.192), channel_id=1, source_target_pairs={{0,16},{16,0},{1,17},{17,1},{2,18},{18,2},{3,19},{19,3},{4,20},{20... | collective-permute-start | bytes 44 | tf_op jit(solution)/shard_map/ppermute | solution.py:472
  69.7 20.4 %collective-permute-start.7 = (bf16[4,104,768]{2,1,0:T(8,128)(2,1)}, bf16[4,104,768]{2,1,0:T(8,128)(2,1)}, u32[]{:S(2)}, u32[]{:S(2)}) collective-permute-start(bf16[4,104,768]{2,1,0:T(8,128)(2,1)} %collective-permute-done.4.rest_3_.refs_1_.refs_3_), channel_id=1, source_target_pairs={{0,16},{16,0},{1,17},{17,1},{2,18},{18,2},{3,19},{19,3},{4,20},{20... | collective-permute-start | bytes 1916936 | tf_op jit(solution)/shard_map/ppermute | solution.py:472
  70.2 19.9 %collective-permute-start.6 = (bf16[4,104,768]{2,1,0:T(8,128)(2,1)}, bf16[4,104,768]{2,1,0:T(8,128)(2,1)}, u32[]{:S(2)}, u32[]{:S(2)}) collective-permute-start(bf16[4,104,768]{2,1,0:T(8,128)(2,1)} %collective-permute-done.3.rest_2_.refs_2_), channel_id=1, source_target_pairs={{0,16},{16,0},{1,17},{17,1},{2,18},{18,2},{3,19},{19,3},{4,20},{20... | collective-permute-start | bytes 1916936 | tf_op jit(solution)/shard_map/ppermute | solution.py:472
  70.2 19.9 %collective-permute-start.5 = (bf16[4,104,768]{2,1,0:T(8,128)(2,1)}, bf16[4,104,768]{2,1,0:T(8,128)(2,1)}, u32[]{:S(2)}, u32[]{:S(2)}) collective-permute-start(bf16[4,104,768]{2,1,0:T(8,128)(2,1)} %collective-permute-done.2.rest_1_.refs_1_), channel_id=1, source_target_pairs={{0,16},{16,0},{1,17},{17,1},{2,18},{18,2},{3,19},{19,3},{4,20},{20... | collective-permute-start | bytes 1916936 | tf_op jit(solution)/shard_map/ppermute | solution.py:472
  73.6 62.7 %all-to-all-start.2 = ((bf16[4,192,768]{2,1,0:T(8,128)(2,1)}), bf16[4,192,768]{2,1,0:T(8,128)(2,1)S(1)}, u32[]{:S(2)}, u32[]{:S(2)}) async-start(bf16[4,192,768]{2,1,0:T(8,128)(2,1)} %after.17), calls=%async_computation.2 | async-start | bytes 2359296 | tf_op jit(solution)/shard_map/all_to_all | solution.py:503
  77.1 190.4 %reduce-scatter.2.cloned.1.call-start = ((), (), s32[]{:S(2)}) async-start(), calls=%async_computation.7 | async-start | bytes 2654208 | tf_op jit(solution)/shard_map/reduce_scatter | solution.py:622
  78.0 10.4 %collective-permute-start.8 = (f32[3]{0:T(128)S(1)}, f32[3]{0:T(128)S(1)}, u32[]{:S(2)}, u32[]{:S(2)}) collective-permute-start(f32[3]{0:T(128)S(1)} %get-tuple-element.192), channel_id=1, source_target_pairs={{0,1},{1,0},{2,3},{3,2},{4,5},{5,4},{6,7},{7,6},{8,9},{9,8},{10,11... | collective-permute-start | bytes 44 | tf_op jit(solution)/shard_map/ppermute | solution.py:472
  89.5 18.4 %collective-permute-start.18 = (bf16[544,768]{1,0:T(8,128)(2,1)S(1)}, bf16[544,768]{1,0:T(8,128)(2,1)}, u32[]{:S(2)}, u32[]{:S(2)}) collective-permute-start(bf16[544,768]{1,0:T(8,128)(2,1)S(1)} %copy-done.1), channel_id=1, source_target_pairs={{0,16},{16,0},{1,17},{17,1},{2,18},{18,2},{3,19},{19,3},{4,20},{20... | collective-permute-start | bytes 2506760 | tf_op jit(solution)/shard_map/ppermute | solution.py:472
  89.8 18.4 %collective-permute-start.19 = (bf16[544,768]{1,0:T(8,128)(2,1)}, bf16[544,768]{1,0:T(8,128)(2,1)}, u32[]{:S(2)}, u32[]{:S(2)}) collective-permute-start(bf16[544,768]{1,0:T(8,128)(2,1)} %collective-permute-done.17.rest_9_), channel_id=1, source_target_pairs={{0,16},{16,0},{1,17},{17,1},{2,18},{18,2},{3,19},{19,3},{4,20},{20... | collective-permute-start | bytes 2506760 | tf_op jit(solution)/shard_map/ppermute | solution.py:472
  104.1 35.8 %collective-permute-start.23 = (bf16[4,192,768]{2,1,0:T(8,128)(2,1)}, bf16[4,192,768]{2,1,0:T(8,128)(2,1)}, u32[]{:S(2)}, u32[]{:S(2)}) collective-permute-start(bf16[4,192,768]{2,1,0:T(8,128)(2,1)} %after.19.rest_12_), channel_id=1, source_target_pairs={{0,2},{2,0},{1,3},{3,1},{4,6},{6,4},{5,7},{7,5},{8,10},{10,8},{9,1... | collective-permute-start | bytes 3538952 | tf_op jit(solution)/shard_map/ppermute | solution.py:472
  105.8 20.5 %collective-permute-start.11 = (bf16[272,768]{1,0:T(8,128)(2,1)S(1)}, bf16[272,768]{1,0:T(8,128)(2,1)S(1)}, u32[]{:S(2)}, u32[]{:S(2)}) collective-permute-start(bf16[272,768]{1,0:T(8,128)(2,1)S(1)} %copy-done.5), channel_id=1, source_target_pairs={{0,1},{1,0},{2,3},{3,2},{4,5},{5,4},{6,7},{7,6},{8,9},{9,8},{10,11... | collective-permute-start | bytes 1253384 | tf_op jit(solution)/shard_map/ppermute | solution.py:472
  106.6 19.7 %collective-permute-start.12 = (bf16[272,768]{1,0:T(8,128)(2,1)}, bf16[272,768]{1,0:T(8,128)(2,1)}, u32[]{:S(2)}, u32[]{:S(2)}) collective-permute-start(bf16[272,768]{1,0:T(8,128)(2,1)} %get-tuple-element.78.rest_1_), channel_id=1, source_target_pairs={{0,1},{1,0},{2,3},{3,2},{4,5},{5,4},{6,7},{7,6},{8,9},{9,8},{10,11... | collective-permute-start | bytes 1253384 | tf_op jit(solution)/shard_map/ppermute | solution.py:472
  107.9 29.3 %collective-permute-start.14 = (bf16[272,768]{1,0:T(8,128)(2,1)}, bf16[272,768]{1,0:T(8,128)(2,1)S(1)}, u32[]{:S(2)}, u32[]{:S(2)}) collective-permute-start(bf16[272,768]{1,0:T(8,128)(2,1)} %get-tuple-element.78.rest_1_), channel_id=1, source_target_pairs={{0,16},{16,0},{1,17},{17,1},{2,18},{18,2},{3,19},{19,3},{4,20},{20... | collective-permute-start | bytes 1253384 | tf_op jit(solution)/shard_map/ppermute | solution.py:472
  108.2 31.7 %collective-permute-start.13 = (bf16[272,768]{1,0:T(8,128)(2,1)S(1)}, bf16[272,768]{1,0:T(8,128)(2,1)S(1)}, u32[]{:S(2)}, u32[]{:S(2)}) collective-permute-start(bf16[272,768]{1,0:T(8,128)(2,1)S(1)} %copy-done.5), channel_id=1, source_target_pairs={{0,16},{16,0},{1,17},{17,1},{2,18},{18,2},{3,19},{19,3},{4,20},{20... | collective-permute-start | bytes 1253384 | tf_op jit(solution)/shard_map/ppermute | solution.py:472
  126.3 13.6 %collective-permute-start.16 = (bf16[272,768]{1,0:T(8,128)(2,1)}, bf16[272,768]{1,0:T(8,128)(2,1)}, u32[]{:S(2)}, u32[]{:S(2)}) collective-permute-start(bf16[272,768]{1,0:T(8,128)(2,1)} %collective-permute-done.12.rest_3_), channel_id=1, source_target_pairs={{0,16},{16,0},{1,17},{17,1},{2,18},{18,2},{3,19},{19,3},{4,20},{20... | collective-permute-start | bytes 1253384 | tf_op jit(solution)/shard_map/ppermute | solution.py:472
  126.3 13.6 %collective-permute-start.15 = (bf16[272,768]{1,0:T(8,128)(2,1)S(1)}, bf16[272,768]{1,0:T(8,128)(2,1)}, u32[]{:S(2)}, u32[]{:S(2)}) collective-permute-start(bf16[272,768]{1,0:T(8,128)(2,1)S(1)} %collective-permute-done.11.refs_1_.rest_2_), channel_id=1, source_target_pairs={{0,16},{16,0},{1,17},{17,1},{2,18},{18,2},{3,19},{19,3},{4,20},{20... | collective-permute-start | bytes 1253384 | tf_op jit(solution)/shard_map/ppermute | solution.py:472
  137.3 27.0 %collective-permute-start.22 = (bf16[4,192,768]{2,1,0:T(8,128)(2,1)}, bf16[4,192,768]{2,1,0:T(8,128)(2,1)S(1)}, u32[]{:S(2)}, u32[]{:S(2)}) collective-permute-start(bf16[4,192,768]{2,1,0:T(8,128)(2,1)} %after.18.rest_12_), channel_id=1, source_target_pairs={{0,2},{2,0},{1,3},{3,1},{4,6},{6,4},{5,7},{7,5},{8,10},{10,8},{9,1... | collective-permute-start | bytes 3538952 | tf_op jit(solution)/shard_map/ppermute | solution.py:472
  182.6 77.6 %all-to-all-start.4 = ((bf16[4,384,768]{2,1,0:T(8,128)(2,1)}), bf16[4,384,768]{2,1,0:T(8,128)(2,1)S(1)}, u32[]{:S(2)}, u32[]{:S(2)}) async-start(bf16[4,384,768]{2,1,0:T(8,128)(2,1)} %bitcast.145), calls=%async_computation.5 | async-start | bytes 4718592 | tf_op jit(solution)/shard_map/all_to_all | solution.py:618
  205.4 6.3 %collective-permute-start.27 = (bf16[272,768]{1,0:T(8,128)(2,1)}, bf16[272,768]{1,0:T(8,128)(2,1)S(1)}, u32[]{:S(2)}, u32[]{:S(2)}) collective-permute-start(bf16[272,768]{1,0:T(8,128)(2,1)} %get-tuple-element.113), channel_id=1, source_target_pairs={{0,16},{16,0},{1,17},{17,1},{2,18},{18,2},{3,19},{19,3},{4,20},{20... | collective-permute-start | bytes 1253384 | tf_op jit(solution)/shard_map/ppermute | solution.py:472
  206.0 15.2 %collective-permute-start.25 = (bf16[544,768]{1,0:T(8,128)(2,1)}, bf16[544,768]{1,0:T(8,128)(2,1)S(1)}, u32[]{:S(2)}, u32[]{:S(2)}) collective-permute-start(bf16[544,768]{1,0:T(8,128)(2,1)} %get-tuple-element.107), channel_id=1, source_target_pairs={{0,16},{16,0},{1,17},{17,1},{2,18},{18,2},{3,19},{19,3},{4,20},{20... | collective-permute-start | bytes 2506760 | tf_op jit(solution)/shard_map/ppermute | solution.py:472
  207.7 12.6 %collective-permute-start.29 = (bf16[272,768]{1,0:T(8,128)(2,1)S(1)}, bf16[272,768]{1,0:T(8,128)(2,1)S(1)}, u32[]{:S(2)}, u32[]{:S(2)}) collective-permute-start(bf16[272,768]{1,0:T(8,128)(2,1)S(1)} %add_convert_fusion.10), channel_id=1, source_target_pairs={{0,1},{1,0},{2,3},{3,2},{4,5},{5,4},{6,7},{7,6},{8,9},{9,8},{10,11... | collective-permute-start | bytes 1253384 | tf_op jit(solution)/shard_map/ppermute | solution.py:472
  209.1 13.7 %collective-permute-start.30 = (bf16[272,768]{1,0:T(8,128)(2,1)}, bf16[272,768]{1,0:T(8,128)(2,1)}, u32[]{:S(2)}, u32[]{:S(2)}) collective-permute-start(bf16[272,768]{1,0:T(8,128)(2,1)} %get-tuple-element.117), channel_id=1, source_target_pairs={{0,16},{16,0},{1,17},{17,1},{2,18},{18,2},{3,19},{19,3},{4,20},{20... | collective-permute-start | bytes 1253384 | tf_op jit(solution)/shard_map/ppermute | solution.py:472
  209.2 42.0 %collective-permute-start.42 = (bf16[4,192,768]{2,1,0:T(8,128)(2,1)}, bf16[4,192,768]{2,1,0:T(8,128)(2,1)}, u32[]{:S(2)}, u32[]{:S(2)}) collective-permute-start(bf16[4,192,768]{2,1,0:T(8,128)(2,1)} %get-tuple-element.138), channel_id=1, source_target_pairs={{0,2},{2,0},{1,3},{3,1},{4,6},{6,4},{5,7},{7,5},{8,10},{10,8},{9,1... | collective-permute-start | bytes 3538952 | tf_op jit(solution)/shard_map/ppermute | solution.py:472
  211.7 16.6 %collective-permute-start.32 = (bf16[272,768]{1,0:T(8,128)(2,1)}, bf16[272,768]{1,0:T(8,128)(2,1)S(1)}, u32[]{:S(2)}, u32[]{:S(2)}) collective-permute-start(bf16[272,768]{1,0:T(8,128)(2,1)} %add_convert_fusion.8), channel_id=1, source_target_pairs={{0,1},{1,0},{2,3},{3,2},{4,5},{5,4},{6,7},{7,6},{8,9},{9,8},{10,11... | collective-permute-start | bytes 1253384 | tf_op jit(solution)/shard_map/ppermute | solution.py:472
  250.1 7.6 %collective-permute-start.37 = (bf16[4,104,768]{2,1,0:T(8,128)(2,1)}, bf16[4,104,768]{2,1,0:T(8,128)(2,1)S(1)}, u32[]{:S(2)}, u32[]{:S(2)}) collective-permute-start(bf16[4,104,768]{2,1,0:T(8,128)(2,1)} %get-tuple-element.133), channel_id=1, source_target_pairs={{0,16},{16,0},{1,17},{17,1},{2,18},{18,2},{3,19},{19,3},{4,20},{20... | collective-permute-start | bytes 1916936 | tf_op jit(solution)/shard_map/ppermute | solution.py:472
  250.6 14.6 %collective-permute-start.33 = (bf16[4,104,768]{2,1,0:T(8,128)(2,1)}, bf16[4,104,768]{2,1,0:T(8,128)(2,1)}, u32[]{:S(2)}, u32[]{:S(2)}) collective-permute-start(bf16[4,104,768]{2,1,0:T(8,128)(2,1)} %get-tuple-element.128), channel_id=1, source_target_pairs={{0,16},{16,0},{1,17},{17,1},{2,18},{18,2},{3,19},{19,3},{4,20},{20... | collective-permute-start | bytes 1916936 | tf_op jit(solution)/shard_map/ppermute | solution.py:472
  250.7 17.4 %collective-permute-start.39 = (bf16[4,104,768]{2,1,0:T(8,128)(2,1)}, bf16[4,104,768]{2,1,0:T(8,128)(2,1)}, u32[]{:S(2)}, u32[]{:S(2)}) collective-permute-start(bf16[4,104,768]{2,1,0:T(8,128)(2,1)} %get-tuple-element.135), channel_id=1, source_target_pairs={{0,16},{16,0},{1,17},{17,1},{2,18},{18,2},{3,19},{19,3},{4,20},{20... | collective-permute-start | bytes 1916936 | tf_op jit(solution)/shard_map/ppermute | solution.py:472
  256.3 17.6 %collective-permute-start.36 = (bf16[4,104,768]{2,1,0:T(8,128)(2,1)}, bf16[4,104,768]{2,1,0:T(8,128)(2,1)}, u32[]{:S(2)}, u32[]{:S(2)}) collective-permute-start(bf16[4,104,768]{2,1,0:T(8,128)(2,1)} %add_convert_fusion.6), channel_id=1, source_target_pairs={{0,1},{1,0},{2,3},{3,2},{4,5},{5,4},{6,7},{7,6},{8,9},{9,8},{10,11... | collective-permute-start | bytes 1916936 | tf_op jit(solution)/shard_map/ppermute | solution.py:472
  258.7 30.1 %collective-permute-start.38 = (bf16[4,104,768]{2,1,0:T(8,128)(2,1)}, bf16[4,104,768]{2,1,0:T(8,128)(2,1)}, u32[]{:S(2)}, u32[]{:S(2)}) collective-permute-start(bf16[4,104,768]{2,1,0:T(8,128)(2,1)} %add_convert_fusion.5), channel_id=1, source_target_pairs={{0,2},{2,0},{1,3},{3,1},{4,6},{6,4},{5,7},{7,5},{8,10},{10,8},{9,1... | collective-permute-start | bytes 1916936 | tf_op jit(solution)/shard_map/ppermute | solution.py:472
  260.2 36.1 %all-to-all-start.5 = ((bf16[4,192,768]{2,1,0:T(8,128)(2,1)}), bf16[4,192,768]{2,1,0:T(8,128)(2,1)S(1)}, u32[]{:S(2)}, u32[]{:S(2)}) async-start(bf16[4,192,768]{2,1,0:T(8,128)(2,1)} %add_convert_fusion), calls=%async_computation.6 | async-start | bytes 2359296 | tf_op jit(solution)/shard_map/all_to_all | solution.py:618
  267.5 21.3 %collective-permute-start.34 = (bf16[4,104,768]{2,1,0:T(8,128)(2,1)}, bf16[4,104,768]{2,1,0:T(8,128)(2,1)}, u32[]{:S(2)}, u32[]{:S(2)}) collective-permute-start(bf16[4,104,768]{2,1,0:T(8,128)(2,1)} %after.21), channel_id=1, source_target_pairs={{0,3},{1,2},{2,1},{3,0},{4,7},{5,6},{6,5},{7,4},{8,11},{9,10},{10,... | collective-permute-start | bytes 1916936 | tf_op jit(solution)/shard_map/ppermute | solution.py:476
  268.1 35.9 %collective-permute-start.24 = (bf16[544,768]{1,0:T(8,128)(2,1)}, bf16[544,768]{1,0:T(8,128)(2,1)}, u32[]{:S(2)}, u32[]{:S(2)}) collective-permute-start(bf16[544,768]{1,0:T(8,128)(2,1)} %get-tuple-element.105), channel_id=1, source_target_pairs={{0,16},{16,0},{1,17},{17,1},{2,18},{18,2},{3,19},{19,3},{4,20},{20... | collective-permute-start | bytes 2506760 | tf_op jit(solution)/shard_map/ppermute | solution.py:472
  268.6 36.0 %collective-permute-start.26 = (bf16[544,768]{1,0:T(8,128)(2,1)S(1)}, bf16[544,768]{1,0:T(8,128)(2,1)}, u32[]{:S(2)}, u32[]{:S(2)}) collective-permute-start(bf16[544,768]{1,0:T(8,128)(2,1)S(1)} %copy-done.13), channel_id=1, source_target_pairs={{0,1},{1,0},{2,3},{3,2},{4,5},{5,4},{6,7},{7,6},{8,9},{9,8},{10,11... | collective-permute-start | bytes 2506760 | tf_op jit(solution)/shard_map/ppermute | solution.py:472
  294.7 7.9 %collective-permute-start.41 = (bf16[192,768]{1,0:T(8,128)(2,1)}, bf16[192,768]{1,0:T(8,128)(2,1)}, u32[]{:S(2)}, u32[]{:S(2)}) collective-permute-start(bf16[192,768]{1,0:T(8,128)(2,1)} %fusion.14), channel_id=1, source_target_pairs={{0,2},{2,0},{1,3},{3,1},{4,6},{6,4},{5,7},{7,5},{8,10},{10,8},{9,1... | collective-permute-start | bytes 884744 | tf_op jit(solution)/shard_map/ppermute | solution.py:472
  297.2 20.9 %all-to-all-start.3 = ((bf16[4,104,768]{2,1,0:T(8,128)(2,1)}), bf16[4,104,768]{2,1,0:T(8,128)(2,1)S(1)}, u32[]{:S(2)}, u32[]{:S(2)}) async-start(bf16[4,104,768]{2,1,0:T(8,128)(2,1)} %get-tuple-element.139), calls=%async_computation.4 | async-start | bytes 1277952 | tf_op jit(solution)/shard_map/all_to_all | solution.py:645
  303.9 4.9 %collective-permute-start.45 = (bf16[3,96,768]{2,1,0:T(8,128)(2,1)S(1)}, bf16[3,96,768]{2,1,0:T(8,128)(2,1)S(1)}, u32[]{:S(2)}, u32[]{:S(2)}) collective-permute-start(bf16[3,96,768]{2,1,0:T(8,128)(2,1)S(1)} %slice.237), channel_id=1, source_target_pairs={{0,16},{16,0},{1,17},{17,1},{2,18},{18,2},{3,19},{19,3},{4,20},{20... | collective-permute-start | bytes 1327112 | tf_op jit(solution)/shard_map/ppermute | solution.py:472
  308.9 11.2 %collective-permute-start.43 = (bf16[3,48,768]{2,1,0:T(8,128)(2,1)S(1)}, bf16[3,48,768]{2,1,0:T(8,128)(2,1)S(1)}, u32[]{:S(2)}, u32[]{:S(2)}) collective-permute-start(bf16[3,48,768]{2,1,0:T(8,128)(2,1)S(1)} %dynamic-slice_bitcast_fusion), channel_id=1, source_target_pairs={{0,1},{1,0},{2,3},{3,2},{4,5},{5,4},{6,7},{7,6},{8,9},{9,8},{10,11... | collective-permute-start | bytes 663560 | tf_op jit(solution)/shard_map/ppermute | solution.py:472
  (33 other events, 180.3 us)
Sparse Core Ops, SparseCore 0:
  67.7 73.6 all-gather.2
Sparse Core Ops, SparseCore 1:
  158.5 84.4 reduce-scatter.1
